TPU v7x, 512 devices: a whole 4x8x8 slice. The times are simulated.
512 devices in a mesh: ctx: 64 (over z, y_lo, core), head: 8 (over x, y_hi).
Axes of the slice: x: 4, y: 8 (y_hi: 2, y_lo: 4; y = y_hi * 4 + y_lo), z: 8, core: 2. Of those that a mesh axis runs over, the one named last changes fastest.
Arguments:
- queries: bfloat16 [65536, 4096], P('ctx', 'head'), may hold values from -5 to 5
- keys: bfloat16 [65536, 1024], P('ctx', 'head'), may hold values from -5 to 5
- values: bfloat16 [65536, 1024], P('ctx', 'head'), may hold values from -16 to 16
- d_attn: bfloat16 [65536, 4096], P('ctx', 'head'), may hold values from -16 to 16
- inputs: bfloat16 [65536, 4096], P('ctx', 'head'), may hold values from -6 to 6
- random_ids: int32 [1024, 3], replicated, may hold values from 0 to 1023, as said below
- global_ids: int32 [2], replicated, may hold values from 0 to 1023
- step_codes: int32 [2], replicated, may hold values from 0 to 999
- momentum: float32 [8, 256, 256], P('head', 'ctx'), may hold values from -6 to 6
Outputs:
- d_queries: bfloat16 [65536, 4096], P('ctx', 'head')
- new_momentum: float32 [8, 256, 256], P('head', 'ctx')
- weight_step: float32 [8, 256, 4096], P('head', 'ctx')
Inputs may be any that keep to these rules, and one draw needn't show every extreme that they name: `random_ids`: row b names the random key blocks of query block b. In the rows of one device of ctx (aligned runs of 16 rows), at most 2 entries name blocks of any one device (blocks c * 16 to (c + 1) * 16 - 1), a block named twice counting twice, and in the rows of every device some device is named exactly 2 times.
All inputs are finite; a program needn't handle non-finite values.
Results may differ from a plain program's by a relative error of at most 0.027.
Values may be sent and summed in bfloat16 or wider, within the bound.
No kernel may reach another device: no remote copies, remote signals or barrier semaphores. Data moves between devices by JAX's collectives and lax.ppermute only.
A program may use at most 128 MiB of HBM per device.

v0:
```python
import math

import jax
import jax.numpy as jnp
from jax import lax
from jax.sharding import PartitionSpec as P

D = 4096
HEAD_SIZE = 128
GROUP = 4
BLK = 64
RAND = 3
GLOB = 2
RANK = 256


def padded_2(shard, sides, width):
    for axis, dim in sides:
        size, length = (lax.axis_size(axis), shard.shape[dim])
        up = [(i, (i + 1) % size) for i in range(size - 1)]
        down = [(j, i) for i, j in up]
        last = lax.slice_in_dim(shard, length - width, length, axis=dim)
        first = lax.slice_in_dim(shard, 0, width, axis=dim)
        before = lax.ppermute(last, axis, up)
        after = lax.ppermute(first, axis, down)
        shard = jnp.concatenate([before, shard, after], axis=dim)
    return shard


def broadcast(block, axis, source):
    block = jnp.where(lax.axis_index(axis) == source, block, jnp.zeros_like(block))
    return lax.psum(block, axis)


def proj_table(code_value, rank_ids, feature_ids):
    row_ids = rank_ids[:, None]
    col_ids = feature_ids[None, :]
    section_one = (row_ids * 31337 + col_ids * 7919 + code_value * 10007) % 65521
    section_two = (section_one * 181 + section_one % 251 * 4093 + col_ids) % 65521
    section_three = (section_two * (section_two % 127 + 1) + row_ids * 17) % 65521
    unit_value = (section_three.astype(jnp.float32) + 0.5) / 65521.0 - 0.5
    return (unit_value * math.sqrt(12.0 / D)).astype(jnp.bfloat16)


def local(queries, keys, values, d_attn, inputs, random_ids, global_ids, step_codes, momentum):
    highest = lax.Precision.HIGHEST
    tok_rows = queries.shape[0]
    blocks = tok_rows // BLK
    ctx_count = lax.axis_size("ctx")
    my_ctx = lax.axis_index("ctx")
    requests = blocks * RAND
    capacity = max(2, (requests + ctx_count - 1) // ctx_count)
    scaling = 1.0 / math.sqrt(HEAD_SIZE)
    rank_ids = jnp.arange(RANK, dtype=jnp.int32)
    feature_ids = jnp.arange(D, dtype=jnp.int32)
    table_new = proj_table(step_codes[1], rank_ids, feature_ids)
    table_old = proj_table(step_codes[0], rank_ids, feature_ids)
    slice_width = inputs.shape[1]
    table_part = lax.dynamic_slice_in_dim(
        table_new, lax.axis_index("head") * slice_width, slice_width, 1
    )
    partial_value = lax.dot_general(
        inputs, table_part, (((1,), (1,)), ((), ())), preferred_element_type=jnp.float32
    )
    projected = lax.psum(partial_value, "head").astype(jnp.bfloat16)
    key_panel = jnp.concatenate([keys, projected, values], axis=1)
    columns = key_panel.shape[1]
    padded = padded_2(key_panel, (("ctx", 0),), BLK)
    padded_blocks = padded.reshape(blocks + 2, BLK, columns)
    window = jnp.stack(
        [padded_blocks[:blocks], padded_blocks[1 : blocks + 1], padded_blocks[2:]], axis=1
    )
    own_blocks = key_panel.reshape(blocks, BLK, columns)
    fetched = []
    for number in range(GLOB):
        block_id = global_ids[number]
        chosen_block = lax.dynamic_index_in_dim(own_blocks, block_id % blocks, 0, keepdims=False)
        fetched.append(broadcast(chosen_block, "ctx", block_id // blocks))
    global_keys = jnp.stack(fetched)
    id_table = random_ids.reshape(ctx_count, requests)
    owners = id_table // blocks
    local_ids = id_table % blocks
    owner_hot = (owners[:, :, None] == jnp.arange(ctx_count, dtype=jnp.int32)).astype(jnp.int32)
    slot_rank = jnp.sum((jnp.cumsum(owner_hot, axis=1) - owner_hot) * owner_hot, axis=2)
    slot_ids = jnp.arange(capacity, dtype=jnp.int32)
    serving = ((owners == my_ctx)[:, :, None] & (slot_rank[:, :, None] == slot_ids)).astype(
        jnp.int32
    )
    sources = jnp.sum(serving * local_ids[:, :, None], axis=1)
    served = jnp.sum(serving, axis=1)
    my_owners = lax.dynamic_index_in_dim(owners, my_ctx, 0, keepdims=False)
    my_ranks = lax.dynamic_index_in_dim(slot_rank, my_ctx, 0, keepdims=False)
    arrival = my_owners * capacity + my_ranks
    pair_blocks = jnp.concatenate([keys, values], axis=1).reshape(blocks, BLK, 2 * HEAD_SIZE)
    replies = jnp.take(pair_blocks, sources.reshape(-1), axis=0).reshape(
        ctx_count, capacity, BLK, 2 * HEAD_SIZE
    )
    received = lax.all_to_all(replies, "ctx", split_axis=0, concat_axis=0, tiled=True)
    picked = jnp.take(received.reshape(ctx_count * capacity, BLK, 2 * HEAD_SIZE), arrival, axis=0)
    blank_cols = jnp.zeros((requests, BLK, RANK), jnp.bfloat16)
    random_keys = jnp.concatenate(
        [picked[:, :, :HEAD_SIZE], blank_cols, picked[:, :, HEAD_SIZE:]], axis=2
    )
    slot_count = 3 + RAND + GLOB
    every_key_row = jnp.concatenate(
        [
            window,
            random_keys.reshape(blocks, RAND, BLK, columns),
            jnp.broadcast_to(global_keys[None], (blocks, GLOB, BLK, columns)),
        ],
        axis=1,
    )
    block_pos = jnp.arange(blocks, dtype=jnp.int32)
    left_ok = (my_ctx > 0) | (block_pos > 0)
    right_ok = (my_ctx < ctx_count - 1) | (block_pos < blocks - 1)
    slot_ok = jnp.concatenate(
        [
            left_ok[:, None],
            jnp.ones((blocks, 1), bool),
            right_ok[:, None],
            jnp.ones((blocks, RAND + GLOB), bool),
        ],
        axis=1,
    )
    key_ok = jnp.repeat(slot_ok, BLK, axis=1)
    pairs = blocks // 2
    query_groups = queries.reshape(pairs, 2, BLK, GROUP, HEAD_SIZE)
    grad_groups = d_attn.reshape(pairs, 2, BLK, GROUP, HEAD_SIZE)
    key_groups = every_key_row.reshape(pairs, 2, slot_count * BLK, columns)
    mask_groups = key_ok.reshape(pairs, 2, slot_count * BLK)

    def group_stride(totals, group_in):
        key_grad, value_grad = totals
        query_row_span, grad_rows, key_row_span, mask_rows = group_in
        scores = (
            jnp.einsum(
                "tiuz,toz->tuio",
                query_row_span,
                key_row_span[..., :HEAD_SIZE],
                preferred_element_type=jnp.float32,
            )
            * scaling
        )
        scores = jnp.where(mask_rows[:, None, None, :], scores, -1e30)
        row_max = jnp.max(scores, axis=-1, keepdims=True)
        exponent = jnp.exp(scores - row_max)
        weights = exponent / jnp.sum(exponent, axis=-1, keepdims=True)
        weights_bf = weights.astype(jnp.bfloat16)
        mixed_out = jnp.einsum(
            "bjqk,bkc->bqjc",
            weights_bf,
            key_row_span[..., HEAD_SIZE:],
            preferred_element_type=jnp.float32,
        )
        attention = mixed_out[..., RANK:].astype(jnp.bfloat16)
        carried = mixed_out[..., :RANK]
        row_delta = jnp.sum(grad_rows.astype(jnp.float32) * attention.astype(jnp.float32), axis=-1)
        d_weights = jnp.einsum(
            "tiuz,toz->tuio",
            grad_rows,
            key_row_span[..., HEAD_SIZE + RANK :],
            preferred_element_type=jnp.float32,
        )
        d_scores = (weights * (d_weights - jnp.transpose(row_delta, (0, 2, 1))[..., None])).astype(
            jnp.bfloat16
        )
        back_prod = jnp.einsum(
            "bjqk,bkc->bqjc",
            d_scores,
            key_row_span[..., : HEAD_SIZE + RANK],
            preferred_element_type=jnp.float32,
        )
        d_query = (back_prod[..., :HEAD_SIZE] * scaling).astype(jnp.bfloat16)
        key_grad = (
            key_grad
            + jnp.einsum(
                "bqjd,bqjr->dr",
                query_row_span.astype(jnp.float32),
                back_prod[..., HEAD_SIZE:],
                precision=highest,
            )
            * scaling
        )
        value_grad = value_grad + jnp.einsum(
            "bqjd,bqjr->dr", grad_rows.astype(jnp.float32), carried, precision=highest
        )
        lower = 3 * BLK
        upper = (3 + RAND) * BLK
        rand_key = (
            jnp.einsum(
                "vcfn,vfct->vnt",
                d_scores[..., lower:upper],
                query_row_span,
                preferred_element_type=jnp.float32,
            )
            * scaling
        )
        rand_value = jnp.einsum(
            "vcfn,vfct->vnt",
            weights_bf[..., lower:upper],
            grad_rows,
            preferred_element_type=jnp.float32,
        )
        extras = jnp.concatenate([rand_key, rand_value], axis=-1)
        return ((key_grad, value_grad), (d_query, extras))

    start = (jnp.zeros((HEAD_SIZE, RANK), jnp.float32), jnp.zeros((HEAD_SIZE, RANK), jnp.float32))
    (key_grad, value_grad), (query_grad_groups, extra_groups) = lax.scan(
        group_stride, start, (query_groups, grad_groups, key_groups, mask_groups)
    )
    contribution = extra_groups.reshape(requests, BLK, 2 * HEAD_SIZE)
    matching = (
        my_owners[None, None, :] == jnp.arange(ctx_count, dtype=jnp.int32)[:, None, None]
    ) & (my_ranks[None, None, :] == slot_ids[None, :, None])
    chosen = jnp.sum(matching.astype(jnp.int32) * jnp.arange(requests, dtype=jnp.int32), axis=2)
    outgoing = jnp.take(contribution, chosen.reshape(-1), axis=0).reshape(
        ctx_count, capacity, BLK, 2 * HEAD_SIZE
    )
    incoming = lax.all_to_all(
        outgoing.astype(jnp.bfloat16), "ctx", split_axis=0, concat_axis=0, tiled=True
    ).astype(outgoing.dtype)
    src_hot = (
        (sources.reshape(-1)[:, None] == block_pos[None, :]) & (served.reshape(-1)[:, None] > 0)
    ).astype(jnp.float32)
    per_block = jnp.einsum(
        "nb,nxc->bxc",
        src_hot,
        incoming.reshape(ctx_count * capacity, BLK, 2 * HEAD_SIZE),
        precision=highest,
    )
    projection_blocks = projected.reshape(blocks, BLK, RANK).astype(jnp.float32)
    key_grad = key_grad + jnp.einsum(
        "bxd,bxr->dr", per_block[..., :HEAD_SIZE], projection_blocks, precision=highest
    )
    value_grad = value_grad + jnp.einsum(
        "bxd,bxr->dr", per_block[..., HEAD_SIZE:], projection_blocks, precision=highest
    )
    gradient = jnp.concatenate([key_grad, value_grad], axis=0) / math.sqrt(tok_rows * ctx_count)
    share = lax.psum_scatter(gradient, "ctx", scatter_dimension=0, tiled=True)
    expanded = jnp.einsum("grk,kd->grd", momentum, table_old.astype(jnp.float32), precision=highest)
    carried_back = jnp.einsum(
        "grd,kd->grk", expanded, table_new.astype(jnp.float32), precision=highest
    )
    new_momentum = 0.9 * carried_back + share[None]
    weight_step = jnp.einsum(
        "grk,kd->grd", new_momentum, table_new.astype(jnp.float32), precision=highest
    )
    dq_out = query_grad_groups.reshape(tok_rows, GROUP * HEAD_SIZE)
    return (dq_out, new_momentum, weight_step)


def solution(mesh):
    in_specs = (
        P("ctx", "head"),
        P("ctx", "head"),
        P("ctx", "head"),
        P("ctx", "head"),
        P("ctx", "head"),
        P(),
        P(),
        P(),
        P("head", "ctx", None),
    )
    out_specs = (P("ctx", "head"), P("head", "ctx", None), P("head", "ctx", None))
    return jax.shard_map(local, mesh=mesh, in_specs=in_specs, out_specs=out_specs, check_vma=False)
```

profile of v0, /device:TPU:1, one launch (start us, length us, event | category | flops | bytes accessed | tf_op | source)
XLA Modules:
  0.0 1485.2 jit_solution(3948728334131455742)
XLA Ops:
  8.6 1.7 fusion.141
  12.5 2.7 gather_fusion
  15.2 4.6 broadcast_select_fusion
  19.8 15.7 %all-to-all-start = ((bf16[64,2,64,256]{3,2,1,0:T(8,128)(2,1)}), bf16[64,2,64,256]{3,2,1,0:T(8,128)(2,1)}, u32[]{:S(2)}, u32[]{:S(2)}) async-start(bf16[64,2,64,256]{3,2,1,0:T(8,128)(2,1)} %broadcast_select_fusion), calls=%async_computation | async-start | bytes 8388608 | tf_op jit(solution)/shard_map/all_to_all | solution.py:98
  37.3 13.3 fusion.53
  51.1 177.6 %all-reduce.9 = bf16[1024,256]{0,1:T(8,128)(2,1)S(1)} all-reduce(f32[1024,256]{0,1:T(8,128)S(1)} %convolution_bitcast_fusion.8), channel_id=1, replica_groups=mesh['ctx'=64,'head'=8] {'head'}, use_global_device_ids=true, to_apply=%region_0.1 | all-reduce | flops 262144 | bytes 1572864 | tf_op jit(solution)/shard_map/psum | solution.py:65
  229.6 4.6 collective-permute-start
  234.2 6.8 collective-permute-start.1
  248.6 2.1 reshape.356
  250.7 2.1 reshape.364
  253.1 3.0 pad_maximum_fusion.1
  256.1 2.3 copy.94
  258.9 2.3 constant_dynamic-update-slice_fusion.3
  263.3 472.0 %all-reduce.8.cloned.1.call-done = (bf16[1,64,512]{2,1,0:T(8,128)(2,1)}, bf16[1,64,512]{2,1,0:T(8,128)(2,1)}) async-done(((bf16[1,64,512]{2,1,0:T(8,128)(2,1)}, bf16[1,64,512]{2,1,0:T(8,128)(2,1)}), (bf16[1,64,512]{2,1,0:T(8,128)(2,1)}, bf16[1,64,512]{2,1,0:T(8,128)(2,1)})) %all-reduce.8.cloned.1.call-update) | async-done | bytes 131088 | tf_op jit(solution)/shard_map/psum | solution.py:32
  736.2 2.8 gather_fusion.1
  740.2 2.0 constant_dynamic-update-slice_fusion
  742.1 1.5 broadcast_dynamic-update-slice_fusion
  743.7 60.7 %while.17 = (s32[]{:T(128)}, f32[128,256]{1,0:T(8,128)S(1)}, f32[128,256]{1,0:T(8,128)S(1)}, bf16[8,2,64,4,128]{4,3,2,1,0:T(4,128)(2,1)}, bf16[8,2,192,256]{3,2,...) while((s32[]{:T(128)}, f32[128,256]{1,0:T(8,128)S(1)}, ...), condition=%wide.region_10.11_spmd.clone, body=%wide.region_6.10_spmd.clone.sunk | while | flops 993525760 | bytes 15944836 | solution.py:208
  744.7 1.3 dynamic-slice_bitcast_fusion.5
  804.4 4.2 gather_fusion.2
  808.5 3.0 select_convert_fusion
  811.5 6.4 copy.115
  817.9 7.9 all-to-all-start.1
  827.1 98.8 %all-to-all-done.1 = bf16[64,2,64,256]{3,1,2,0:T(2,128)(2,1)} async-done(((bf16[64,2,64,256]{3,1,2,0:T(2,128)(2,1)}), bf16[64,2,64,256]{3,1,2,0:T(2,128)(2,1)}, u32[]{:S(2)}, u32[]{:S(2)}) %all-to-all-start.1) | async-done | bytes 4194336 | tf_op jit(solution)/shard_map/all_to_all | solution.py:219
  925.8 8.8 copy.116
  934.6 7.3 reshape.370
  942.0 2.8 fusion.94
  947.0 13.6 fusion.71
  962.5 2.4 copy.155
  964.9 484.1 %all-reduce.6.cloned.1.call-done = f32[256,256]{1,0:T(8,128)} async-done(((f32[256,256]{1,0:T(8,128)}), f32[256,256]{1,0:T(8,128)}) %all-reduce.6.cloned.1.call-update) | async-done | bytes 262160
  1449.0 15.0 %fusion.78 = f32[4,256]{1,0:T(4,128)S(1)} fusion(f32[4096,4]{0,1:T(4,128)S(1)} %fusion.71, s32[256]{0:T(256)S(1)} %get-tuple-element.170, s32[]{:T(128)} %bitcast, s32[4096]{0:T(1024)S(1)} %iota_multiply_fusion, s32[256]{0:T(256)S(1)} %get-tuple-element.171, f32[256,256]{1,0:T(8,128)} %all-reduce.6.cloned.1.call-done, u32[]{:T(128)S(6)} %multiply.4), kind=kOutput, calls=%fused_computation.127 | convolution fusion | flops 97519616 | bytes 92168 | tf_op jit(solution)/shard_map/grd,kd->grk/dot_general | solution.py:241
  1464.0 14.1 convolution_bitcast_fusion.7
  (227 shorter events, 75.1 us)
Async XLA Ops:
  7.2 43.4 %copy-start = (bf16[1024,512]{1,0:T(8,128)(2,1)S(1)}, bf16[1024,512]{1,0:T(8,128)(2,1)}, u32[]{:S(2)}) copy-start(bf16[1024,512]{1,0:T(8,128)(2,1)} %param.15) | copy-start | bytes 3145732
  19.8 15.8 %copy-start.8 = (bf16[1024,128]{1,0:T(8,128)(2,1)S(1)}, bf16[1024,128]{1,0:T(8,128)(2,1)}, u32[]{:S(2)}) copy-start(bf16[1024,128]{1,0:T(8,128)(2,1)} %param.12) | copy-start | bytes 786436
  19.8 16.0 %copy-start.9 = (bf16[1024,128]{1,0:T(8,128)(2,1)S(1)}, bf16[1024,128]{1,0:T(8,128)(2,1)}, u32[]{:S(2)}) copy-start(bf16[1024,128]{1,0:T(8,128)(2,1)} %param.13) | copy-start | bytes 786436
  19.8 16.1 %copy-start.10 = (s32[2]{0:T(128)S(1)}, s32[2]{0:T(128)}, u32[]{:S(2)}) copy-start(s32[2]{0:T(128)} %param.18) | copy-start | bytes 28
  19.8 716.4 %all-to-all-start = ((bf16[64,2,64,256]{3,2,1,0:T(8,128)(2,1)}), bf16[64,2,64,256]{3,2,1,0:T(8,128)(2,1)}, u32[]{:S(2)}, u32[]{:S(2)}) async-start(bf16[64,2,64,256]{3,2,1,0:T(8,128)(2,1)} %broadcast_select_fusion), calls=%async_computation | async-start | bytes 8388608 | tf_op jit(solution)/shard_map/all_to_all | solution.py:98
  35.6 699.7 %all-reduce.8.cloned.1.call-start = ((), (), s32[]{:S(2)}) async-start(), calls=%async_computation.3 | async-start | bytes 262144 | tf_op jit(solution)/shard_map/psum | solution.py:32
  35.8 193.0 %copy-start.4 = (bf16[1024,128]{0,1:T(8,128)(2,1)}, bf16[1024,128]{0,1:T(8,128)(2,1)S(1)}, u32[]{:S(2)}) copy-start(bf16[1024,128]{0,1:T(8,128)(2,1)S(1)} %copy.92) | copy-start | bytes 786436
  36.0 193.7 %copy-start.6 = (bf16[1024,128]{0,1:T(8,128)(2,1)}, bf16[1024,128]{0,1:T(8,128)(2,1)S(1)}, u32[]{:S(2)}) copy-start(bf16[1024,128]{0,1:T(8,128)(2,1)S(1)} %copy.93) | copy-start | bytes 786436
  50.6 191.0 %copy-start.11 = (s32[2]{0:T(128)S(1)}, s32[2]{0:T(128)}, u32[]{:S(2)}) copy-start(s32[2]{0:T(128)} %param.17) | copy-start | bytes 28
  228.7 24.4 %copy-start.2 = (bf16[1024,256]{0,1:T(8,128)(2,1)}, bf16[1024,256]{0,1:T(8,128)(2,1)S(1)}, u32[]{:S(2)}) copy-start(bf16[1024,256]{0,1:T(8,128)(2,1)S(1)} %all-reduce.9) | copy-start | bytes 1572868
  229.6 23.5 %copy-start.5 = (bf16[1024,128]{0,1:T(8,128)(2,1)S(1)}, bf16[1024,128]{0,1:T(8,128)(2,1)}, u32[]{:S(2)}) copy-start(bf16[1024,128]{0,1:T(8,128)(2,1)} %copy-done.4) | copy-start | bytes 786436
  229.6 23.5 %copy-start.7 = (bf16[1024,128]{0,1:T(8,128)(2,1)S(1)}, bf16[1024,128]{0,1:T(8,128)(2,1)}, u32[]{:S(2)}) copy-start(bf16[1024,128]{0,1:T(8,128)(2,1)} %copy-done.6) | copy-start | bytes 786436
  229.6 23.5 %collective-permute-start = (bf16[64,512]{0,1:T(8,128)(2,1)}, bf16[64,512]{0,1:T(8,128)(2,1)}, u32[]{:S(2)}, u32[]{:S(2)}) collective-permute-start(bf16[64,512]{0,1:T(8,128)(2,1)} %get-tuple-element.161), channel_id=1, source_target_pairs={{0,8},{8,16},{16,24},{24,32},{32,40},{40,48},{48,56},{56,64},{64,7... | collective-permute-start | bytes 196616 | tf_op jit(solution)/shard_map/ppermute | solution.py:24
  234.2 18.9 %collective-permute-start.1 = (bf16[64,512]{0,1:T(8,128)(2,1)}, bf16[64,512]{0,1:T(8,128)(2,1)}, u32[]{:S(2)}, u32[]{:S(2)}) collective-permute-start(bf16[64,512]{0,1:T(8,128)(2,1)} %get-tuple-element.160), channel_id=1, source_target_pairs={{8,0},{16,8},{24,16},{32,24},{40,32},{48,40},{56,48},{64,56},{72,6... | collective-permute-start | bytes 196616 | tf_op jit(solution)/shard_map/ppermute | solution.py:25
  817.9 8.1 copy-start.3
  817.9 108.0 %all-to-all-start.1 = ((bf16[64,2,64,256]{3,1,2,0:T(2,128)(2,1)}), bf16[64,2,64,256]{3,1,2,0:T(2,128)(2,1)}, u32[]{:S(2)}, u32[]{:S(2)}) async-start(bf16[64,2,64,256]{3,1,2,0:T(2,128)(2,1)} %copy.115), calls=%async_computation.1 | async-start | bytes 8388608 | tf_op jit(solution)/shard_map/all_to_all | solution.py:219
  825.8 623.2 %all-reduce.6.cloned.1.call-start = ((), (), s32[]{:S(2)}) async-start(), calls=%async_computation.2 | async-start | bytes 524288
  941.9 5.1 copy-start.12
  1464.0 14.2 copy-start.13
  1464.0 14.2 copy-start.1
Sparse Core Ops, SparseCore 0:
  248.2 487.0 all-reduce.7
  947.1 501.8 all-reduce.5
where the time goes:
time: 1490 us
  waiting for transfers between devices  1050 us (70%)
  blocking collectives  178 us (12%)
  local copies, waits for them, and re-layouts  82.1 us (6%)
  matrix products  73.5 us (5%)
  other arithmetic  38.7 us (3%)
  starting transfers between devices  35.1 us (2%)
  between operations  22 us (1%)
    unnamed x3, waiting for transfers between devices  484 us
    psum x1, waiting for transfers between devices, broadcast(): return lax.psum(block, axis)  472 us
    psum x1, blocking collectives, local(): projected = lax.psum(partial_value, 'head').astype(jnp.bfloat16)  178 us
    all_to_all x1, waiting for transfers between devices, local(): lax.all_to_all(outgoing.astype(jnp.bfloat16), 'ctx', split_axis=0, concat...  98.8 us
  transfers between devices with their start and end apart: 6, of which 3 were waited for; matrix products, arithmetic and copies ran while one was open for 3% of the time, Pallas kernels for 0%

commit v1 on v0

v1 whole, which is shorter than its diff:
```python
import functools
import math

import jax
import jax.numpy as jnp
from jax import lax
from jax.experimental import pallas as pl
from jax.experimental.pallas import tpu as pltpu
from jax.sharding import PartitionSpec as P

D = 4096
HEAD_SIZE = 128
GROUP = 4
BLK = 64
RAND = 3
GLOB = 2
RANK = 256
CAP = 2
ROWS = 16
PARTS = BLK // ROWS
LIMIT = 48 * 1024 * 1024
F32 = jnp.float32
BF16 = jnp.bfloat16
VMEM = pl.BlockSpec(memory_space=pltpu.VMEM)
SMEM = pl.BlockSpec(memory_space=pltpu.SMEM)
PARAMS = pltpu.CompilerParams(vmem_limit_bytes=LIMIT)


def proj_table(code_value, rank_ids, feature_ids):
    row_ids = rank_ids[:, None]
    col_ids = feature_ids[None, :]
    section_one = (row_ids * 31337 + col_ids * 7919 + code_value * 10007) % 65521
    section_two = (section_one * 181 + section_one % 251 * 4093 + col_ids) % 65521
    section_three = (section_two * (section_two % 127 + 1) + row_ids * 17) % 65521
    unit_value = (section_three.astype(jnp.float32) + 0.5) / 65521.0 - 0.5
    return (unit_value * math.sqrt(12.0 / D)).astype(jnp.bfloat16)


def dot(a, b, da, db):
    return lax.dot_general(a, b, (((da,), (db,)), ((), ())), preferred_element_type=F32)


def split3(x):
    high = x.astype(BF16)
    rest = x - high.astype(F32)
    mid = rest.astype(BF16)
    return high, mid, (rest - mid.astype(F32)).astype(BF16)


def pack_kv(src_ref, k_ref, v_ref, out_ref):
    here = out_ref.shape[0]
    first = pl.program_id(0) * here
    for i in range(here):
        rows = pl.ds(pl.multiple_of(src_ref[first + i] * BLK, BLK), BLK)
        out_ref[i, :, :HEAD_SIZE] = k_ref[rows, :]
        out_ref[i, :, HEAD_SIZE:] = v_ref[rows, :]


def project(x_ref, t_ref, out_ref):
    blocks = out_ref.shape[1]
    y = dot(x_ref[...], t_ref[...], 1, 1).astype(out_ref.dtype)
    for b in range(blocks):
        for part in range(PARTS):
            row = b * BLK + part * ROWS
            for half in range(2):
                out_ref[half * PARTS + part, b] = y[row : row + ROWS, half * 128 : half * 128 + 128]


def sum_pack(src_ref, gid_ref, x_ref, own_ref, out_ref, acc):
    own = x_ref[0].astype(F32)
    for i in range(1, x_ref.shape[0]):
        own = own + x_ref[i].astype(F32)
    acc[...] = own.astype(BF16)
    own_ref[...] = acc[...]
    for i in range(out_ref.shape[0]):
        for c in range(CAP):
            out_ref[i, c] = acc[src_ref[i * CAP + c]]
        for g in range(GLOB):
            out_ref[i, CAP + g] = acc[gid_ref[g]]


def collect(arrival_ref, owner_ref, own_ref, before_ref, after_ref, recv_ref, out_ref):
    blocks = own_ref.shape[0]
    tiles = [before_ref[...]] + [own_ref[b] for b in range(blocks)] + [after_ref[...]]
    tiles += [recv_ref[owner_ref[g] * (CAP + GLOB) + CAP + g] for g in range(GLOB)]
    tiles += [recv_ref[arrival_ref[n] // CAP * (CAP + GLOB) + arrival_ref[n] % CAP] for n in range(blocks * RAND)]
    for n, tile in enumerate(tiles):
        for h in range(out_ref.shape[0]):
            out_ref[h, n] = tile


def attend(
    arrival_ref, edge_ref, q_ref, g_ref, k_ref, v_ref, before_ref, after_ref, glob_ref, recv_ref,
    dq_ref, kg_ref, kwin, vwin, wacc, gacc,
):
    step, steps = pl.program_id(0), pl.num_programs(0)
    tokens = k_ref.shape[0]
    blocks = tokens // BLK
    unroll = q_ref.shape[0] // BLK
    scaling = 1.0 / math.sqrt(HEAD_SIZE)
    h = HEAD_SIZE

    @pl.when(step == 0)
    def _():
        for win, ref, low in ((kwin, k_ref, 0), (vwin, v_ref, h)):
            win[:BLK] = before_ref[:, low : low + h]
            win[BLK : BLK + tokens] = ref[...]
            win[BLK + tokens :] = after_ref[:, low : low + h]
        wacc[...] = jnp.zeros_like(wacc)
        gacc[...] = jnp.zeros_like(gacc)

    for u in range(unroll):
        b = step * unroll + u
        rows = pl.ds(pl.multiple_of(b * BLK, BLK), 3 * BLK)
        picks = [arrival_ref[b * RAND + r] for r in range(RAND)]
        k_all = jnp.concatenate([kwin[rows, :]] + [recv_ref[p, :, :h] for p in picks] + [glob_ref[:, :h]], axis=0)
        v_all = jnp.concatenate([vwin[rows, :]] + [recv_ref[p, :, h:] for p in picks] + [glob_ref[:, h:]], axis=0)
        here = slice(u * BLK, (u + 1) * BLK)
        q = jnp.concatenate([q_ref[here, j * h : (j + 1) * h] for j in range(GROUP)], axis=0)
        g = jnp.concatenate([g_ref[here, j * h : (j + 1) * h] for j in range(GROUP)], axis=0)
        s = dot(k_all, q, 1, 1) * (scaling * math.log2(math.e))
        left = jnp.where(b == 0, edge_ref[0], 0).astype(F32) * -1e30
        right = jnp.where(b == blocks - 1, edge_ref[1], 0).astype(F32) * -1e30
        s = jnp.concatenate(
            [s[:BLK] + left, s[BLK : 2 * BLK], s[2 * BLK : 3 * BLK] + right, s[3 * BLK :]], axis=0
        )
        e = jnp.exp2(s - jnp.max(s, axis=0, keepdims=True))
        w = e * (1.0 / jnp.sum(e, axis=0, keepdims=True))
        w_bf = w.astype(BF16)
        dw = dot(v_all, g, 1, 1)
        delta = jnp.sum(w_bf.astype(F32) * dw, axis=0, keepdims=True)
        ds = (w * (dw - delta)).astype(BF16)
        dq = jnp.transpose(dot(k_all, ds, 0, 0) * scaling).astype(BF16)
        for j in range(GROUP):
            dq_ref[here, j * h : (j + 1) * h] = dq[j * BLK : (j + 1) * BLK]
        kg = dot(ds, q, 1, 0) * scaling
        vg = dot(w_bf, g, 1, 0)
        wacc[rows, :h] += kg[: 3 * BLK]
        wacc[rows, h:] += vg[: 3 * BLK]
        gacc[:, :h] += kg[(3 + RAND) * BLK :]
        gacc[:, h:] += vg[(3 + RAND) * BLK :]
        for r in range(RAND):
            for part in range(PARTS):
                low = (3 + r) * BLK + part * ROWS
                place = blocks + 2 + GLOB + b * RAND + r
                kg_ref[part, place, :, :h] = kg[low : low + ROWS].astype(BF16)
                kg_ref[part, place, :, h:] = vg[low : low + ROWS].astype(BF16)

    @pl.when(step == steps - 1)
    def _():
        for acc, first, count in ((wacc, 0, blocks + 2), (gacc, blocks + 2, GLOB)):
            for n in range(count):
                for part in range(PARTS):
                    low = n * BLK + part * ROWS
                    kg_ref[part, first + n] = acc[low : low + ROWS, :].astype(BF16)


def gradient(kg_ref, p_ref, out_ref, acc):
    step = pl.program_id(0)
    terms = jnp.concatenate([dot(kg_ref[0], p_ref[i, 0], 0, 0) for i in range(2)], axis=1)

    @pl.when(step == 0)
    def _():
        acc[...] = terms

    @pl.when(step > 0)
    def _():
        acc[...] += terms

    @pl.when(step == pl.num_programs(0) - 1)
    def _():
        out_ref[...] = acc[...]


def carry(m_ref, old_ref, new_ref, out_ref):
    rows = m_ref.shape[0]
    x = dot(jnp.concatenate(split3(m_ref[...]), axis=0), old_ref[...], 1, 0)
    x = x[:rows] + x[rows : 2 * rows] + x[2 * rows :]
    y = dot(jnp.concatenate(split3(x), axis=0), new_ref[...], 1, 1)
    out_ref[...] = 0.9 * (y[:rows] + y[rows : 2 * rows] + y[2 * rows :])


def finish(scale, recv_ref, carried_ref, new_ref, mom_ref, step_ref):
    rows = mom_ref.shape[0]
    total = carried_ref[:rows] + jnp.sum(recv_ref[...], axis=0) * scale
    mom_ref[...] = total
    padded = jnp.concatenate([total, jnp.zeros((8 - rows, RANK), F32)], axis=0)
    y = dot(jnp.concatenate(split3(padded), axis=0), new_ref[...], 1, 0)
    step_ref[...] = (y[:8] + y[8:16] + y[16:])[:rows]


def local(queries, keys, values, d_attn, inputs, random_ids, global_ids, step_codes, momentum):
    tokens = queries.shape[0]
    blocks = tokens // BLK
    ctx, heads = lax.axis_size("ctx"), lax.axis_size("head")
    my_ctx, my_head = lax.axis_index("ctx"), lax.axis_index("head")
    requests = blocks * RAND
    places = blocks + 2 + GLOB + requests
    h = HEAD_SIZE
    up = [(i, i + 1) for i in range(ctx - 1)]
    down = [(i + 1, i) for i in range(ctx - 1)]

    ids = random_ids.reshape(ctx, requests)
    owners, inner = ids // blocks, ids % blocks
    order = jnp.arange(requests, dtype=jnp.int32)
    tagged = order[None, :] * blocks + inner
    mine = owners == my_ctx
    first = jnp.min(jnp.where(mine, tagged, requests * blocks), axis=1) % blocks
    last = jnp.max(jnp.where(mine, tagged, 0), axis=1) % blocks
    sources = jnp.stack([first, last], axis=1).reshape(-1)
    my_owners = lax.dynamic_index_in_dim(owners, my_ctx, 0, keepdims=False)
    earlier = (my_owners[:, None] == my_owners[None, :]) & (order[None, :] < order[:, None])
    arrival = my_owners * CAP + jnp.any(earlier, axis=1).astype(jnp.int32)
    global_owner, global_inner = global_ids // blocks, global_ids % blocks

    chunk = 16
    kv_out = pl.pallas_call(
        pack_kv,
        grid_spec=pltpu.PrefetchScalarGridSpec(
            num_scalar_prefetch=1,
            grid=(ctx * CAP // chunk,),
            in_specs=[VMEM, VMEM],
            out_specs=pl.BlockSpec((chunk, BLK, 2 * h), lambda i, s: (i, 0, 0)),
        ),
        out_shape=jax.ShapeDtypeStruct((ctx * CAP, BLK, 2 * h), BF16),
        compiler_params=PARAMS,
    )(sources, keys, values)
    kv_in = lax.all_to_all(kv_out.reshape(ctx, CAP, BLK, 2 * h), "ctx", 0, 0, tiled=True)
    kv_in = kv_in.reshape(ctx * CAP, BLK, 2 * h)

    feature_ids = my_head * inputs.shape[1] + jnp.arange(inputs.shape[1], dtype=jnp.int32)
    rank_ids = jnp.arange(RANK, dtype=jnp.int32)
    table_part = proj_table(step_codes[1], rank_ids, feature_ids)
    terms = pl.pallas_call(
        project,
        in_specs=[VMEM] * 2,
        out_specs=VMEM,
        out_shape=jax.ShapeDtypeStruct((heads, blocks, ROWS, 128), BF16),
        compiler_params=PARAMS,
    )(inputs, table_part)
    terms = lax.all_to_all(terms, "head", 0, 0, tiled=True)
    own, p_out = pl.pallas_call(
        sum_pack,
        in_specs=[SMEM, SMEM, VMEM],
        out_specs=[VMEM] * 2,
        out_shape=[
            jax.ShapeDtypeStruct((blocks, ROWS, 128), BF16),
            jax.ShapeDtypeStruct((ctx, CAP + GLOB, ROWS, 128), BF16),
        ],
        scratch_shapes=[pltpu.VMEM((blocks, ROWS, 128), BF16)],
        compiler_params=PARAMS,
    )(sources, global_inner, terms)

    kv_before = lax.ppermute(jnp.concatenate([keys[-BLK:], values[-BLK:]], axis=1), "ctx", up)
    kv_after = lax.ppermute(jnp.concatenate([keys[:BLK], values[:BLK]], axis=1), "ctx", down)
    p_before = lax.ppermute(own[-1], "ctx", up)
    p_after = lax.ppermute(own[0], "ctx", down)
    kv_glob = []
    for g in range(GLOB):
        row = global_inner[g] * BLK
        kv_glob.append(jnp.concatenate([lax.dynamic_slice_in_dim(x, row, BLK, 0) for x in (keys, values)], axis=1))
    kv_glob = jnp.stack(kv_glob)
    apart = my_ctx ^ global_owner
    bit = 1
    while bit < ctx:
        other = lax.ppermute(kv_glob, "ctx", [(i, i ^ bit) for i in range(ctx)])
        kv_glob = jnp.where(((apart & bit) != 0)[:, None, None], other, kv_glob)
        bit *= 2
    kv_glob = kv_glob.reshape(GLOB * BLK, 2 * h)

    p_in = lax.all_to_all(p_out, "ctx", 0, 0, tiled=True)
    tiles = pl.pallas_call(
        collect,
        in_specs=[SMEM, SMEM] + [VMEM] * 4,
        out_specs=VMEM,
        out_shape=jax.ShapeDtypeStruct((heads, places, ROWS, 128), BF16),
        compiler_params=PARAMS,
    )(arrival, global_owner, own, p_before, p_after, p_in.reshape(ctx * (CAP + GLOB), ROWS, 128))
    tiles = lax.all_to_all(tiles, "head", 0, 0, tiled=True)

    every = jnp.arange(D, dtype=jnp.int32)
    table_new = proj_table(step_codes[1], rank_ids, every)
    table_old = proj_table(step_codes[0], rank_ids, every)
    share = momentum.shape[1]
    carried = pl.pallas_call(
        carry,
        in_specs=[VMEM] * 3,
        out_specs=VMEM,
        out_shape=jax.ShapeDtypeStruct((8, RANK), F32),
        compiler_params=PARAMS,
    )(jnp.pad(momentum[0], ((0, 8 - share), (0, 0))), table_old, table_new)

    edges = jnp.stack([my_ctx == 0, my_ctx == ctx - 1]).astype(jnp.int32)
    unroll = 2
    wide = pl.BlockSpec((unroll * BLK, GROUP * h), lambda i: (i, 0))
    dq, grads = pl.pallas_call(
        attend,
        grid=(blocks // unroll,),
        in_specs=[SMEM, SMEM, wide, wide] + [VMEM] * 6,
        out_specs=[wide, VMEM],
        out_shape=[
            jax.ShapeDtypeStruct((tokens, GROUP * h), BF16),
            jax.ShapeDtypeStruct((PARTS, places, ROWS, 2 * h), BF16),
        ],
        scratch_shapes=[
            pltpu.VMEM((tokens + 2 * BLK, h), BF16),
            pltpu.VMEM((tokens + 2 * BLK, h), BF16),
            pltpu.VMEM((tokens + 2 * BLK, 2 * h), F32),
            pltpu.VMEM((GLOB * BLK, 2 * h), F32),
        ],
        compiler_params=PARAMS,
    )(arrival, edges, queries, d_attn, keys, values, kv_before, kv_after, kv_glob, kv_in)

    grad = pl.pallas_call(
        gradient,
        grid=(PARTS,),
        in_specs=[
            pl.BlockSpec((1, places * ROWS, 2 * h), lambda i: (i, 0, 0)),
            pl.BlockSpec((2, 1, places * ROWS, 128), lambda i: (0, i, 0, 0)),
        ],
        out_specs=pl.BlockSpec((2 * h, RANK), lambda i: (0, 0)),
        out_shape=jax.ShapeDtypeStruct((2 * h, RANK), F32),
        scratch_shapes=[pltpu.VMEM((2 * h, RANK), F32)],
        compiler_params=PARAMS,
    )(grads.reshape(PARTS, places * ROWS, 2 * h), tiles.reshape(2, PARTS, places * ROWS, 128))
    grad = lax.all_to_all(grad.reshape(ctx, share, RANK), "ctx", 0, 0, tiled=True)
    new_momentum, weight_step = pl.pallas_call(
        functools.partial(finish, 1.0 / math.sqrt(tokens * ctx)),
        in_specs=[VMEM] * 3,
        out_specs=[VMEM] * 2,
        out_shape=[
            jax.ShapeDtypeStruct((share, RANK), F32),
            jax.ShapeDtypeStruct((share, D), F32),
        ],
        compiler_params=PARAMS,
    )(grad, carried, table_new)
    return dq, new_momentum[None], weight_step[None]


def solution(mesh):
    in_specs = (
        P("ctx", "head"),
        P("ctx", "head"),
        P("ctx", "head"),
        P("ctx", "head"),
        P("ctx", "head"),
        P(),
        P(),
        P(),
        P("head", "ctx", None),
    )
    out_specs = (P("ctx", "head"), P("head", "ctx", None), P("head", "ctx", None))
    return jax.shard_map(local, mesh=mesh, in_specs=in_specs, out_specs=out_specs, check_vma=False)
```

time: 1490 us -> 359 us (0.24)
  waiting for transfers between devices: 1050 us -> 165 us
  blocking collectives: 178 us -> 0 us
  starting transfers between devices: 35.1 us -> 119 us
  matrix products: 73.5 us -> 0 us
  local copies, waits for them, and re-layouts: 82.1 us -> 12.4 us
  Pallas kernels: 0 us -> 27.1 us
  between operations: 22 us -> 3.65 us
    unnamed x3 -> x0, waiting for transfers between devices: 484 us -> none
    psum x1 -> x0, waiting for transfers between devices: 472 us -> none  [broadcast(): return lax.psum(block, axis)]
    psum x1 -> x0, blocking collectives: 178 us -> none  [local(): projected = lax.psum(partial_value, 'head').astype(jnp.bfloat16)]
    ppermute x2 -> x10, waiting for transfers between devices: 0.01 us -> 103 us  [the longest x1 71 us: local(): p_before = lax.ppermute(own[-1], 'ctx', up)]
    dot_general x63 -> x0, matrix products: 69.4 us -> none  [the longest x1 15 us: local(): jnp.einsum('grd,kd->grk', expanded, table_new.astype(jnp.float32), precis...]
    ppermute x2 -> x10, starting transfers between devices: 11.4 us -> 68 us  [the longest x6 58.2 us: local(): other = lax.ppermute(kv_glob, 'ctx', [(i, i ^ bit) for i in range(ctx)])]
    all_to_all x2 -> x5, waiting for transfers between devices: 98.8 us -> 62.2 us  [the longest x1 24.9 us: local(): p_in = lax.all_to_all(p_out, 'ctx', 0, 0, tiled=True)]
    all_to_all x2 -> x5, starting transfers between devices: 23.6 us -> 51.3 us  [the longest x1 16.7 us: local(): p_in = lax.all_to_all(p_out, 'ctx', 0, 0, tiled=True)]
  transfers between devices with their start and end apart: 6 -> 15, of which waited for: 3 -> 8; matrix products, arithmetic and copies ran while one was open for 3% -> 8% of each run, Pallas kernels for 0% -> 6%
where the time goes in v1:
time: 359 us; the launch traced here: 357 us
  waiting for transfers between devices  165 us (46%)
  starting transfers between devices  119 us (33%)
  other arithmetic  30 us (8%)
  Pallas kernels  27.1 us (8%)
  local copies, waits for them, and re-layouts  12.4 us (3%)
  between operations  3.65 us (1%)
    ppermute x1, waiting for transfers between devices, local(): p_before = lax.ppermute(own[-1], 'ctx', up)  71 us
    ppermute x6, starting transfers between devices, local(): other = lax.ppermute(kv_glob, 'ctx', [(i, i ^ bit) for i in range(ctx)])  58.2 us
    ppermute x6, waiting for transfers between devices, local(): other = lax.ppermute(kv_glob, 'ctx', [(i, i ^ bit) for i in range(ctx)])  31.8 us
    convert_element_type x2, other arithmetic, proj_table(): return (unit_value * math.sqrt(12.0 / D)).astype(jnp.bfloat16)  27.4 us
    all_to_all x1, waiting for transfers between devices, local(): p_in = lax.all_to_all(p_out, 'ctx', 0, 0, tiled=True)  24.9 us
    all_to_all x1, waiting for transfers between devices, local(): lax.all_to_all(kv_out.reshape(ctx, CAP, BLK, 2 * h), 'ctx', 0, 0, tiled=T...  24.6 us
    all_to_all x1, starting transfers between devices, local(): p_in = lax.all_to_all(p_out, 'ctx', 0, 0, tiled=True)  16.7 us
    pallas_call x1, Pallas kernels, local(): pl.pallas_call(attend, grid=(blocks // unroll,), in_specs=[SMEM, SMEM, wi...  15.6 us
  transfers between devices with their start and end apart: 15, of which 8 were waited for; matrix products, arithmetic and copies ran while one was open for 8% of the time, Pallas kernels for 6%

profile of v1, /device:TPU:1, one launch (start us, length us, event | category | flops | bytes accessed | tf_op | source)
XLA Modules:
  0.0 357.4 jit_solution(18194894509505661091)
XLA Ops:
  2.6 1.8 fusion.59.t_ref
  7.0 10.1 %all-to-all-start.1 = ((bf16[8,16,16,128]{3,2,1,0:T(8,128)(2,1)}), bf16[8,16,16,128]{3,2,1,0:T(8,128)(2,1)S(1)}, u32[]{:S(2)}, u32[]{:S(2)}) async-start(bf16[8,16,16,128]{3,2,1,0:T(8,128)(2,1)} %shard_map.114), calls=%async_computation.1 | async-start | bytes 1048576 | tf_op jit(solution)/shard_map/all_to_all | solution.py:241
  19.3 12.8 %all-to-all-done.1.x_ref = bf16[8,16,16,128]{3,2,1,0:T(8,128)(2,1)S(1)} async-done(((bf16[8,16,16,128]{3,2,1,0:T(8,128)(2,1)}), bf16[8,16,16,128]{3,2,1,0:T(8,128)(2,1)S(1)}, u32[]{:S(2)}, u32[]{:S(2)}) %all-to-all-start.1) | async-done | bytes 524320 | tf_op jit(solution)/shard_map/all_to_all | solution.py:241
  32.1 1.7 shard_map.115
  33.8 16.7 %all-to-all-start.2 = ((bf16[64,4,16,128]{3,2,1,0:T(8,128)(2,1)}), bf16[64,4,16,128]{3,2,1,0:T(8,128)(2,1)S(1)}, u32[]{:S(2)}, u32[]{:S(2)}) async-start(bf16[64,4,16,128]{3,2,1,0:T(8,128)(2,1)} %get-tuple-element.12), calls=%async_computation.2 | async-start | bytes 2097152 | tf_op jit(solution)/shard_map/all_to_all | solution.py:271
  50.5 1.5 shard_map.112
  52.1 2.0 copy-done
  54.1 24.9 %all-to-all-done.2 = bf16[64,4,16,128]{3,2,1,0:T(8,128)(2,1)S(1)} async-done(((bf16[64,4,16,128]{3,2,1,0:T(8,128)(2,1)}), bf16[64,4,16,128]{3,2,1,0:T(8,128)(2,1)S(1)}, u32[]{:S(2)}, u32[]{:S(2)}) %all-to-all-start.2) | async-done | bytes 1048608 | tf_op jit(solution)/shard_map/all_to_all | solution.py:271
  79.0 6.5 %all-to-all-start = ((bf16[64,2,64,256]{3,2,1,0:T(8,128)(2,1)}), bf16[64,2,64,256]{3,2,1,0:T(8,128)(2,1)}, u32[]{:S(2)}, u32[]{:S(2)}) async-start(bf16[64,2,64,256]{3,2,1,0:T(8,128)(2,1)} %bitcast.31), calls=%async_computation | async-start | bytes 8388608 | tf_op jit(solution)/shard_map/all_to_all | solution.py:228
  86.3 3.5 collective-permute-start.8
  89.8 1.9 collective-permute-start.9
  91.8 71.0 %collective-permute-done.8.before_ref = bf16[16,128]{1,0:T(8,128)(2,1)S(1)} collective-permute-done((bf16[16,128]{1,0:T(8,128)(2,1)S(1)}, bf16[16,128]{1,0:T(8,128)(2,1)S(1)}, u32[]{:S(2)}, u32[]{:S(2)}) %collective-permute-start.8) | collective-permute-done | bytes 4128 | tf_op jit(solution)/shard_map/ppermute | solution.py:256
  162.7 2.3 shard_map.116
  165.1 24.6 %all-to-all-done = bf16[64,2,64,256]{3,2,1,0:T(8,128)(2,1)} async-done(((bf16[64,2,64,256]{3,2,1,0:T(8,128)(2,1)}), bf16[64,2,64,256]{3,2,1,0:T(8,128)(2,1)}, u32[]{:S(2)}, u32[]{:S(2)}) %all-to-all-start) | async-done | bytes 4194336 | tf_op jit(solution)/shard_map/all_to_all | solution.py:228
  189.6 3.6 %all-to-all-start.3 = ((bf16[8,68,16,128]{3,2,1,0:T(8,128)(2,1)}), bf16[8,68,16,128]{3,2,1,0:T(8,128)(2,1)S(1)}, u32[]{:S(2)}, u32[]{:S(2)}) async-start(bf16[8,68,16,128]{3,2,1,0:T(8,128)(2,1)} %shard_map.116), calls=%async_computation.3 | async-start | bytes 4456448 | tf_op jit(solution)/shard_map/all_to_all | solution.py:279
  195.2 4.5 %collective-permute-start.2 = (bf16[2,64,256]{2,1,0:T(8,128)(2,1)S(1)}, bf16[2,64,256]{2,1,0:T(8,128)(2,1)S(1)}, u32[]{:S(2)}, u32[]{:S(2)}) collective-permute-start(bf16[2,64,256]{2,1,0:T(8,128)(2,1)S(1)} %pad_maximum_fusion), channel_id=1, source_target_pairs={{0,8},{8,0},{16,24},{24,16},{32,40},{40,32},{48,56},{56,48},{64,72... | collective-permute-start | bytes 196616 | tf_op jit(solution)/shard_map/ppermute | solution.py:266
  200.7 3.6 %collective-permute-start.3 = (bf16[2,64,256]{2,1,0:T(8,128)(2,1)S(1)}, bf16[2,64,256]{2,1,0:T(8,128)(2,1)S(1)}, u32[]{:S(2)}, u32[]{:S(2)}) collective-permute-start(bf16[2,64,256]{2,1,0:T(8,128)(2,1)S(1)} %broadcast_select_fusion), channel_id=1, source_target_pairs={{0,16},{8,24},{16,0},{24,8},{32,48},{40,56},{48,32},{56,40},{64,80... | collective-permute-start | bytes 196616 | tf_op jit(solution)/shard_map/ppermute | solution.py:266
  204.3 27.2 %collective-permute-done.3 = bf16[2,64,256]{2,1,0:T(8,128)(2,1)S(1)} collective-permute-done((bf16[2,64,256]{2,1,0:T(8,128)(2,1)S(1)}, bf16[2,64,256]{2,1,0:T(8,128)(2,1)S(1)}, u32[]{:S(2)}, u32[]{:S(2)}) %collective-permute-start.3) | collective-permute-done | bytes 65568 | tf_op jit(solution)/shard_map/ppermute | solution.py:266
  231.5 25.3 %collective-permute-start.4 = (bf16[2,64,256]{2,1,0:T(8,128)(2,1)S(1)}, bf16[2,64,256]{2,1,0:T(8,128)(2,1)S(1)}, u32[]{:S(2)}, u32[]{:S(2)}) collective-permute-start(bf16[2,64,256]{2,1,0:T(8,128)(2,1)S(1)} %broadcast_select_fusion.1), channel_id=1, source_target_pairs={{0,32},{8,40},{16,48},{24,56},{32,0},{40,8},{48,16},{56,24},{64,96... | collective-permute-start | bytes 196616 | tf_op jit(solution)/shard_map/ppermute | solution.py:266
  256.9 1.9 collective-permute-start
  258.9 1.9 collective-permute-start.5
  260.8 2.4 collective-permute-start.1
  264.0 4.5 %collective-permute-start.6 = (bf16[2,64,256]{2,1,0:T(8,128)(2,1)S(1)}, bf16[2,64,256]{2,1,0:T(8,128)(2,1)S(1)}, u32[]{:S(2)}, u32[]{:S(2)}) collective-permute-start(bf16[2,64,256]{2,1,0:T(8,128)(2,1)S(1)} %broadcast_select_fusion.3), channel_id=1, source_target_pairs={{0,128},{8,136},{16,144},{24,152},{32,160},{40,168},{48,176},{56,1... | collective-permute-start | bytes 196616 | tf_op jit(solution)/shard_map/ppermute | solution.py:266
  268.5 1.6 collective-permute-done.6
  270.2 18.3 %collective-permute-start.7 = (bf16[2,64,256]{2,1,0:T(8,128)(2,1)S(1)}, bf16[2,64,256]{2,1,0:T(8,128)(2,1)S(1)}, u32[]{:S(2)}, u32[]{:S(2)}) collective-permute-start(bf16[2,64,256]{2,1,0:T(8,128)(2,1)S(1)} %broadcast_select_fusion.4), channel_id=1, source_target_pairs={{0,256},{8,264},{16,272},{24,280},{32,288},{40,296},{48,304},{56,3... | collective-permute-start | bytes 196616 | tf_op jit(solution)/shard_map/ppermute | solution.py:266
  288.6 2.1 collective-permute-done.7
  293.2 15.6 %shard_map.113 = (bf16[1024,512]{1,0:T(8,128)(2,1)}, bf16[4,68,16,256]{3,2,1,0:T(8,128)(2,1)S(1)}) custom-call(s32[48]{0:T(128)S(1)} %convert_add_fusion.arrival_ref, s32[2]{0:T(128)S(1)} %add_convert_fusion.edge_ref, bf16[1024,512]{1,0:T(8,128)(2,1)S(1)} %copy-done.6, bf16[1024,512]{1,0:T(8,128)(2,1)S(1)} %copy-done.7, bf16[1024,128]{1,0:T(8,128)(2,1)S(1)} %copy-done.3, ...), custom_call_target="tpu_custom_call" | custom-call | tf_op jit(solution)/shard_map/pallas_call | solution.py:296
  308.8 1.4 copy-done.1
  310.2 1.6 copy-done.2
  311.8 2.4 shard_map.117
  315.0 14.4 %all-to-all-start.4 = ((f32[64,4,256]{2,1,0:T(4,128)}), f32[64,4,256]{2,1,0:T(4,128)S(1)}, u32[]{:S(2)}, u32[]{:S(2)}) async-start(f32[64,4,256]{2,1,0:T(4,128)} %reshape.167), calls=%async_computation.4 | async-start | bytes 524288 | tf_op jit(solution)/shard_map/all_to_all | solution.py:326
  329.4 25.6 %fusion.41 = (bf16[256,4096]{1,0:T(8,128)(2,1)S(1)}, bf16[256,4096]{1,0:T(8,128)(2,1)S(1)}) fusion(s32[]{:T(128)} %bitcast.13, s32[256]{0:T(256)S(1)} %get-tuple-element.49, s32[4096]{0:T(1024)S(1)} %iota_multiply_fusion, s32[256]{0:T(256)S(1)} %get-tuple-element.50, s32[]{:T(128)} %bitcast.19), kind=kLoop, calls=%fused_computation.53 | loop fusion | flops 93323264 | bytes 4212744 | tf_op jit(solution)/shard_map/convert_element_type | solution.py:36
  (73 shorter events, 14.4 us)
Async XLA Ops:
  0.6 49.9 %copy-start.3 = (bf16[1024,128]{1,0:T(8,128)(2,1)S(1)}, bf16[1024,128]{1,0:T(8,128)(2,1)}, u32[]{:S(2)}) copy-start(bf16[1024,128]{1,0:T(8,128)(2,1)} %k_ref.3) | copy-start | bytes 786436
  0.6 49.9 %copy-start.4 = (bf16[1024,128]{1,0:T(8,128)(2,1)S(1)}, bf16[1024,128]{1,0:T(8,128)(2,1)}, u32[]{:S(2)}) copy-start(bf16[1024,128]{1,0:T(8,128)(2,1)} %v_ref.3) | copy-start | bytes 786436
  4.5 1.2 copy-start.5
  7.0 25.1 %all-to-all-start.1 = ((bf16[8,16,16,128]{3,2,1,0:T(8,128)(2,1)}), bf16[8,16,16,128]{3,2,1,0:T(8,128)(2,1)S(1)}, u32[]{:S(2)}, u32[]{:S(2)}) async-start(bf16[8,16,16,128]{3,2,1,0:T(8,128)(2,1)} %shard_map.114), calls=%async_computation.1 | async-start | bytes 1048576 | tf_op jit(solution)/shard_map/all_to_all | solution.py:241
  33.8 45.2 %all-to-all-start.2 = ((bf16[64,4,16,128]{3,2,1,0:T(8,128)(2,1)}), bf16[64,4,16,128]{3,2,1,0:T(8,128)(2,1)S(1)}, u32[]{:S(2)}, u32[]{:S(2)}) async-start(bf16[64,4,16,128]{3,2,1,0:T(8,128)(2,1)} %get-tuple-element.12), calls=%async_computation.2 | async-start | bytes 2097152 | tf_op jit(solution)/shard_map/all_to_all | solution.py:271
  52.1 2.0 copy-start
  79.0 6.5 %copy-start.8 = (s32[1024,3]{0,1:T(4,128)S(1)}, s32[1024,3]{0,1:T(4,128)}, u32[]{:S(2)}) copy-start(s32[1024,3]{0,1:T(4,128)} %param.14) | copy-start | bytes 36868
  79.0 7.2 %copy-start.10 = (s32[2]{0:T(128)S(1)}, s32[2]{0:T(128)}, u32[]{:S(2)}) copy-start(s32[2]{0:T(128)} %param.15) | copy-start | bytes 28
  79.0 110.7 %all-to-all-start = ((bf16[64,2,64,256]{3,2,1,0:T(8,128)(2,1)}), bf16[64,2,64,256]{3,2,1,0:T(8,128)(2,1)}, u32[]{:S(2)}, u32[]{:S(2)}) async-start(bf16[64,2,64,256]{3,2,1,0:T(8,128)(2,1)} %bitcast.31), calls=%async_computation | async-start | bytes 8388608 | tf_op jit(solution)/shard_map/all_to_all | solution.py:228
  86.3 76.5 %collective-permute-start.8 = (bf16[16,128]{1,0:T(8,128)(2,1)S(1)}, bf16[16,128]{1,0:T(8,128)(2,1)S(1)}, u32[]{:S(2)}, u32[]{:S(2)}) collective-permute-start(bf16[16,128]{1,0:T(8,128)(2,1)S(1)} %get-tuple-element.29), channel_id=1, source_target_pairs={{0,8},{8,16},{16,24},{24,32},{32,40},{40,48},{48,56},{56,64},{64,7... | collective-permute-start | bytes 12296 | tf_op jit(solution)/shard_map/ppermute | solution.py:256
  89.8 72.9 %collective-permute-start.9 = (bf16[16,128]{1,0:T(8,128)(2,1)S(1)}, bf16[16,128]{1,0:T(8,128)(2,1)S(1)}, u32[]{:S(2)}, u32[]{:S(2)}) collective-permute-start(bf16[16,128]{1,0:T(8,128)(2,1)S(1)} %get-tuple-element.28), channel_id=1, source_target_pairs={{8,0},{16,8},{24,16},{32,24},{40,32},{48,40},{56,48},{64,56},{72,6... | collective-permute-start | bytes 12296 | tf_op jit(solution)/shard_map/ppermute | solution.py:257
  189.6 120.6 %all-to-all-start.3 = ((bf16[8,68,16,128]{3,2,1,0:T(8,128)(2,1)}), bf16[8,68,16,128]{3,2,1,0:T(8,128)(2,1)S(1)}, u32[]{:S(2)}, u32[]{:S(2)}) async-start(bf16[8,68,16,128]{3,2,1,0:T(8,128)(2,1)} %shard_map.116), calls=%async_computation.3 | async-start | bytes 4456448 | tf_op jit(solution)/shard_map/all_to_all | solution.py:279
  195.2 5.4 %collective-permute-start.2 = (bf16[2,64,256]{2,1,0:T(8,128)(2,1)S(1)}, bf16[2,64,256]{2,1,0:T(8,128)(2,1)S(1)}, u32[]{:S(2)}, u32[]{:S(2)}) collective-permute-start(bf16[2,64,256]{2,1,0:T(8,128)(2,1)S(1)} %pad_maximum_fusion), channel_id=1, source_target_pairs={{0,8},{8,0},{16,24},{24,16},{32,40},{40,32},{48,56},{56,48},{64,72... | collective-permute-start | bytes 196616 | tf_op jit(solution)/shard_map/ppermute | solution.py:266
  200.7 30.8 %collective-permute-start.3 = (bf16[2,64,256]{2,1,0:T(8,128)(2,1)S(1)}, bf16[2,64,256]{2,1,0:T(8,128)(2,1)S(1)}, u32[]{:S(2)}, u32[]{:S(2)}) collective-permute-start(bf16[2,64,256]{2,1,0:T(8,128)(2,1)S(1)} %broadcast_select_fusion), channel_id=1, source_target_pairs={{0,16},{8,24},{16,0},{24,8},{32,48},{40,56},{48,32},{56,40},{64,80... | collective-permute-start | bytes 196616 | tf_op jit(solution)/shard_map/ppermute | solution.py:266
  231.5 27.3 %collective-permute-start.4 = (bf16[2,64,256]{2,1,0:T(8,128)(2,1)S(1)}, bf16[2,64,256]{2,1,0:T(8,128)(2,1)S(1)}, u32[]{:S(2)}, u32[]{:S(2)}) collective-permute-start(bf16[2,64,256]{2,1,0:T(8,128)(2,1)S(1)} %broadcast_select_fusion.1), channel_id=1, source_target_pairs={{0,32},{8,40},{16,48},{24,56},{32,0},{40,8},{48,16},{56,24},{64,96... | collective-permute-start | bytes 196616 | tf_op jit(solution)/shard_map/ppermute | solution.py:266
  256.9 33.9 %collective-permute-start = (bf16[64,256]{1,0:T(8,128)(2,1)S(1)}, bf16[64,256]{1,0:T(8,128)(2,1)S(1)}, u32[]{:S(2)}, u32[]{:S(2)}) collective-permute-start(bf16[64,256]{1,0:T(8,128)(2,1)S(1)} %pad_maximum_fusion.1), channel_id=1, source_target_pairs={{0,8},{8,16},{16,24},{24,32},{32,40},{40,48},{48,56},{56,64},{64,7... | collective-permute-start | bytes 98312 | tf_op jit(solution)/shard_map/ppermute | solution.py:254
  258.9 5.0 %collective-permute-start.5 = (bf16[2,64,256]{2,1,0:T(8,128)(2,1)S(1)}, bf16[2,64,256]{2,1,0:T(8,128)(2,1)S(1)}, u32[]{:S(2)}, u32[]{:S(2)}) collective-permute-start(bf16[2,64,256]{2,1,0:T(8,128)(2,1)S(1)} %broadcast_select_fusion.2), channel_id=1, source_target_pairs={{0,64},{8,72},{16,80},{24,88},{32,96},{40,104},{48,112},{56,120},{... | collective-permute-start | bytes 196616 | tf_op jit(solution)/shard_map/ppermute | solution.py:266
  260.8 29.9 %collective-permute-start.1 = (bf16[64,256]{1,0:T(8,128)(2,1)S(1)}, bf16[64,256]{1,0:T(8,128)(2,1)S(1)}, u32[]{:S(2)}, u32[]{:S(2)}) collective-permute-start(bf16[64,256]{1,0:T(8,128)(2,1)S(1)} %pad_maximum_fusion.2), channel_id=1, source_target_pairs={{8,0},{16,8},{24,16},{32,24},{40,32},{48,40},{56,48},{64,56},{72,6... | collective-permute-start | bytes 98312 | tf_op jit(solution)/shard_map/ppermute | solution.py:255
  264.0 6.1 %collective-permute-start.6 = (bf16[2,64,256]{2,1,0:T(8,128)(2,1)S(1)}, bf16[2,64,256]{2,1,0:T(8,128)(2,1)S(1)}, u32[]{:S(2)}, u32[]{:S(2)}) collective-permute-start(bf16[2,64,256]{2,1,0:T(8,128)(2,1)S(1)} %broadcast_select_fusion.3), channel_id=1, source_target_pairs={{0,128},{8,136},{16,144},{24,152},{32,160},{40,168},{48,176},{56,1... | collective-permute-start | bytes 196616 | tf_op jit(solution)/shard_map/ppermute | solution.py:266
  270.2 20.5 %collective-permute-start.7 = (bf16[2,64,256]{2,1,0:T(8,128)(2,1)S(1)}, bf16[2,64,256]{2,1,0:T(8,128)(2,1)S(1)}, u32[]{:S(2)}, u32[]{:S(2)}) collective-permute-start(bf16[2,64,256]{2,1,0:T(8,128)(2,1)S(1)} %broadcast_select_fusion.4), channel_id=1, source_target_pairs={{0,256},{8,264},{16,272},{24,280},{32,288},{40,296},{48,304},{56,3... | collective-permute-start | bytes 196616 | tf_op jit(solution)/shard_map/ppermute | solution.py:266
  290.8 1.2 copy-start.6
  292.0 1.2 copy-start.7
  308.8 1.4 copy-start.1
  310.2 1.6 copy-start.2
  311.8 43.2 %copy-start.9 = (f32[1,4,256]{2,1,0:T(4,128)S(1)}, f32[1,4,256]{2,1,0:T(4,128)}, u32[]{:S(2)}) copy-start(f32[1,4,256]{2,1,0:T(4,128)} %param.17) | copy-start | bytes 12292
  315.0 41.2 %all-to-all-start.4 = ((f32[64,4,256]{2,1,0:T(4,128)}), f32[64,4,256]{2,1,0:T(4,128)S(1)}, u32[]{:S(2)}, u32[]{:S(2)}) async-start(f32[64,4,256]{2,1,0:T(4,128)} %reshape.167), calls=%async_computation.4 | async-start | bytes 524288 | tf_op jit(solution)/shard_map/all_to_all | solution.py:326

commit v2 on v1

--- a/solution.py
+++ b/solution.py
@@ -18,12 +18,13 @@
 CAP = 2
 ROWS = 16
 PARTS = BLK // ROWS
-LIMIT = 48 * 1024 * 1024
 F32 = jnp.float32
 BF16 = jnp.bfloat16
 VMEM = pl.BlockSpec(memory_space=pltpu.VMEM)
+ANY = pl.BlockSpec(memory_space=pl.ANY)
 SMEM = pl.BlockSpec(memory_space=pltpu.SMEM)
-PARAMS = pltpu.CompilerParams(vmem_limit_bytes=LIMIT)
+PARAMS = pltpu.CompilerParams(vmem_limit_bytes=16 * 1024 * 1024)
+LARGE = pltpu.CompilerParams(vmem_limit_bytes=30 * 1024 * 1024)
 
 
 def proj_table(code_value, rank_ids, feature_ids):
@@ -85,14 +86,14 @@
     tiles += [recv_ref[owner_ref[g] * (CAP + GLOB) + CAP + g] for g in range(GLOB)]
     tiles += [recv_ref[arrival_ref[n] // CAP * (CAP + GLOB) + arrival_ref[n] % CAP] for n in range(blocks * RAND)]
     for n, tile in enumerate(tiles):
-        for h in range(out_ref.shape[0]):
-            out_ref[h, n] = tile
+        out_ref[n] = tile
 
 
 def attend(
-    arrival_ref, edge_ref, q_ref, g_ref, k_ref, v_ref, before_ref, after_ref, glob_ref, recv_ref,
-    dq_ref, kg_ref, kwin, vwin, wacc, gacc,
+    arrival_ref, edge_ref, from_ref, q_ref, g_ref, k_ref, v_ref, before_ref, after_ref, glob_ref, recv_ref, *refs
 ):
+    dq_ref, out_ref, kwin, vwin, wacc, gacc, kg_ref, total = refs[-8:]
+    tile_refs = refs[:-10]
     step, steps = pl.program_id(0), pl.num_programs(0)
     tokens = k_ref.shape[0]
     blocks = tokens // BLK
@@ -153,23 +154,16 @@
                 for part in range(PARTS):
                     low = n * BLK + part * ROWS
                     kg_ref[part, first + n] = acc[low : low + ROWS, :].astype(BF16)
-
-
-def gradient(kg_ref, p_ref, out_ref, acc):
-    step = pl.program_id(0)
-    terms = jnp.concatenate([dot(kg_ref[0], p_ref[i, 0], 0, 0) for i in range(2)], axis=1)
-
-    @pl.when(step == 0)
-    def _():
-        acc[...] = terms
-
-    @pl.when(step > 0)
-    def _():
-        acc[...] += terms
-
-    @pl.when(step == pl.num_programs(0) - 1)
-    def _():
-        out_ref[...] = acc[...]
+        total[...] = jnp.zeros_like(total)
+        many = kg_ref.shape[1] * ROWS
+        for i, ref in enumerate(tile_refs):
+            head = from_ref[i]
+            kg = kg_ref[head % PARTS].reshape(many, 2 * h)
+            total[head // PARTS] += dot(kg, ref[...].reshape(many, 128), 0, 0)
+        rows = total.shape[1] // out_ref.shape[0]
+        for d in range(out_ref.shape[0]):
+            for half in range(2):
+                out_ref[d, half * rows : (half + 1) * rows] = total[half, d * rows : (d + 1) * rows]
 
 
 def carry(m_ref, old_ref, new_ref, out_ref):
@@ -182,7 +176,8 @@
 
 def finish(scale, recv_ref, carried_ref, new_ref, mom_ref, step_ref):
     rows = mom_ref.shape[0]
-    total = carried_ref[:rows] + jnp.sum(recv_ref[...], axis=0) * scale
+    grad = jnp.sum(recv_ref[...], axis=0) * scale
+    total = carried_ref[:rows] + jnp.concatenate([grad[:rows], grad[rows:]], axis=1)
     mom_ref[...] = total
     padded = jnp.concatenate([total, jnp.zeros((8 - rows, RANK), F32)], axis=0)
     y = dot(jnp.concatenate(split3(padded), axis=0), new_ref[...], 1, 0)
@@ -212,21 +207,6 @@
     earlier = (my_owners[:, None] == my_owners[None, :]) & (order[None, :] < order[:, None])
     arrival = my_owners * CAP + jnp.any(earlier, axis=1).astype(jnp.int32)
     global_owner, global_inner = global_ids // blocks, global_ids % blocks
-
-    chunk = 16
-    kv_out = pl.pallas_call(
-        pack_kv,
-        grid_spec=pltpu.PrefetchScalarGridSpec(
-            num_scalar_prefetch=1,
-            grid=(ctx * CAP // chunk,),
-            in_specs=[VMEM, VMEM],
-            out_specs=pl.BlockSpec((chunk, BLK, 2 * h), lambda i, s: (i, 0, 0)),
-        ),
-        out_shape=jax.ShapeDtypeStruct((ctx * CAP, BLK, 2 * h), BF16),
-        compiler_params=PARAMS,
-    )(sources, keys, values)
-    kv_in = lax.all_to_all(kv_out.reshape(ctx, CAP, BLK, 2 * h), "ctx", 0, 0, tiled=True)
-    kv_in = kv_in.reshape(ctx * CAP, BLK, 2 * h)
 
     feature_ids = my_head * inputs.shape[1] + jnp.arange(inputs.shape[1], dtype=jnp.int32)
     rank_ids = jnp.arange(RANK, dtype=jnp.int32)
@@ -273,10 +253,32 @@
         collect,
         in_specs=[SMEM, SMEM] + [VMEM] * 4,
         out_specs=VMEM,
-        out_shape=jax.ShapeDtypeStruct((heads, places, ROWS, 128), BF16),
+        out_shape=jax.ShapeDtypeStruct((places, ROWS, 128), BF16),
         compiler_params=PARAMS,
     )(arrival, global_owner, own, p_before, p_after, p_in.reshape(ctx * (CAP + GLOB), ROWS, 128))
-    tiles = lax.all_to_all(tiles, "head", 0, 0, tiled=True)
+    pair = [tiles, lax.ppermute(tiles, "head", [(i, i ^ 1) for i in range(heads)])]
+    chunk = 16
+    kv_out = pl.pallas_call(
+        pack_kv,
+        grid_spec=pltpu.PrefetchScalarGridSpec(
+            num_scalar_prefetch=1,
+            grid=(ctx * CAP // chunk,),
+            in_specs=[VMEM, VMEM],
+            out_specs=pl.BlockSpec((chunk, BLK, 2 * h), lambda i, s: (i, 0, 0)),
+        ),
+        out_shape=jax.ShapeDtypeStruct((ctx * CAP, BLK, 2 * h), BF16),
+        compiler_params=PARAMS,
+    )(sources, keys, values)
+    kv_out, pair[1], kv_before, kv_after, kv_glob = lax.optimization_barrier((kv_out, pair[1], kv_before, kv_after, kv_glob))
+    kv_in = lax.all_to_all(kv_out.reshape(ctx, CAP, BLK, 2 * h), "ctx", 0, 0, tiled=True)
+    kv_in = kv_in.reshape(ctx * CAP, BLK, 2 * h)
+
+    all_tiles, all_heads = list(pair), [my_head, my_head ^ 1]
+    for far in range(2, heads, 2):
+        there = [(i, (i + far) % heads) for i in range(heads)]
+        all_tiles += [lax.ppermute(t, "head", there) for t in pair]
+        source = (my_head - far) % heads
+        all_heads += [source, source ^ 1]
 
     every = jnp.arange(D, dtype=jnp.int32)
     table_new = proj_table(step_codes[1], rank_ids, every)
@@ -293,37 +295,29 @@
     edges = jnp.stack([my_ctx == 0, my_ctx == ctx - 1]).astype(jnp.int32)
     unroll = 2
     wide = pl.BlockSpec((unroll * BLK, GROUP * h), lambda i: (i, 0))
-    dq, grads = pl.pallas_call(
+    dq, grad = pl.pallas_call(
         attend,
         grid=(blocks // unroll,),
-        in_specs=[SMEM, SMEM, wide, wide] + [VMEM] * 6,
+        in_specs=[SMEM] * 3 + [wide] * 2 + [VMEM] * (6 + heads) + [ANY] * 2,
         out_specs=[wide, VMEM],
         out_shape=[
             jax.ShapeDtypeStruct((tokens, GROUP * h), BF16),
-            jax.ShapeDtypeStruct((PARTS, places, ROWS, 2 * h), BF16),
+            jax.ShapeDtypeStruct((ctx, 2 * share, 128), F32),
         ],
         scratch_shapes=[
             pltpu.VMEM((tokens + 2 * BLK, h), BF16),
             pltpu.VMEM((tokens + 2 * BLK, h), BF16),
             pltpu.VMEM((tokens + 2 * BLK, 2 * h), F32),
             pltpu.VMEM((GLOB * BLK, 2 * h), F32),
+            pltpu.VMEM((PARTS, places, ROWS, 2 * h), BF16),
+            pltpu.VMEM((2, 2 * h, 128), F32),
         ],
-        compiler_params=PARAMS,
-    )(arrival, edges, queries, d_attn, keys, values, kv_before, kv_after, kv_glob, kv_in)
-
-    grad = pl.pallas_call(
-        gradient,
-        grid=(PARTS,),
-        in_specs=[
-            pl.BlockSpec((1, places * ROWS, 2 * h), lambda i: (i, 0, 0)),
-            pl.BlockSpec((2, 1, places * ROWS, 128), lambda i: (0, i, 0, 0)),
-        ],
-        out_specs=pl.BlockSpec((2 * h, RANK), lambda i: (0, 0)),
-        out_shape=jax.ShapeDtypeStruct((2 * h, RANK), F32),
-        scratch_shapes=[pltpu.VMEM((2 * h, RANK), F32)],
-        compiler_params=PARAMS,
-    )(grads.reshape(PARTS, places * ROWS, 2 * h), tiles.reshape(2, PARTS, places * ROWS, 128))
-    grad = lax.all_to_all(grad.reshape(ctx, share, RANK), "ctx", 0, 0, tiled=True)
+        compiler_params=LARGE,
+    )(
+        arrival, edges, jnp.stack(all_heads), queries, d_attn, keys, values, kv_before, kv_after, kv_glob, kv_in,
+        *all_tiles, table_new, carried,
+    )
+    grad = lax.all_to_all(grad, "ctx", 0, 0, tiled=True)
     new_momentum, weight_step = pl.pallas_call(
         functools.partial(finish, 1.0 / math.sqrt(tokens * ctx)),
         in_specs=[VMEM] * 3,

time: 359 us -> 288 us (0.80)
  waiting for transfers between devices: 165 us -> 86.7 us
  blocking collectives: 0 us -> 30 us
  starting transfers between devices: 119 us -> 96.6 us
    ppermute x1, waiting for transfers between devices: 71 us -> 0.01 us  [local(): p_before = lax.ppermute(own[-1], 'ctx', up)]
    all_to_all x0 -> x1, blocking collectives: none -> 30 us  [local(): grad = lax.all_to_all(grad, 'ctx', 0, 0, tiled=True)]
    ppermute x6, starting transfers between devices: 58.2 us -> 31.2 us  [local(): other = lax.ppermute(kv_glob, 'ctx', [(i, i ^ bit) for i in range(ctx)])]
    all_to_all x1, waiting for transfers between devices: 24.6 us -> 51.4 us  [local(): lax.all_to_all(kv_out.reshape(ctx, CAP, BLK, 2 * h), 'ctx', 0, 0, tiled=T...]
    all_to_all x1, waiting for transfers between devices: 24.9 us -> 0.01 us  [local(): p_in = lax.all_to_all(p_out, 'ctx', 0, 0, tiled=True)]
    ppermute x0 -> x7, starting transfers between devices: none -> 20.7 us  [the longest x6 18.7 us: local(): all_tiles += [lax.ppermute(t, 'head', there) for t in pair]]
    all_to_all x2 -> x0, starting transfers between devices: 18 us -> none  [the longest x1 14.4 us: local(): lax.all_to_all(grad.reshape(ctx, share, RANK), 'ctx', 0, 0, tiled=True)]
    ppermute x6, waiting for transfers between devices: 31.8 us -> 20.5 us  [local(): other = lax.ppermute(kv_glob, 'ctx', [(i, i ^ bit) for i in range(ctx)])]
  transfers between devices with their start and end apart: 15 -> 20, of which waited for: 8 -> 6; matrix products, arithmetic and copies ran while one was open for 8% -> 11% of each run, Pallas kernels for 6% -> 2%
where the time goes in v2:
time: 288 us; the launch traced here: 286 us
  starting transfers between devices  96.6 us (34%)
  waiting for transfers between devices  86.7 us (30%)
  other arithmetic  30 us (10%)
  blocking collectives  30 us (10%)
  Pallas kernels  25.3 us (9%)
  local copies, waits for them, and re-layouts  14 us (5%)
  between operations  3.78 us (1%)
    all_to_all x1, waiting for transfers between devices, local(): lax.all_to_all(kv_out.reshape(ctx, CAP, BLK, 2 * h), 'ctx', 0, 0, tiled=T...  51.4 us
    ppermute x6, starting transfers between devices, local(): other = lax.ppermute(kv_glob, 'ctx', [(i, i ^ bit) for i in range(ctx)])  31.2 us
    all_to_all x1, blocking collectives, local(): grad = lax.all_to_all(grad, 'ctx', 0, 0, tiled=True)  30 us
    convert_element_type x2, other arithmetic, proj_table(): return (unit_value * math.sqrt(12.0 / D)).astype(jnp.bfloat16)  28.1 us
    ppermute x6, waiting for transfers between devices, local(): other = lax.ppermute(kv_glob, 'ctx', [(i, i ^ bit) for i in range(ctx)])  20.5 us
    ppermute x6, starting transfers between devices, local(): all_tiles += [lax.ppermute(t, 'head', there) for t in pair]  18.7 us
    pallas_call x1, Pallas kernels, local(): pl.pallas_call(attend, grid=(blocks // unroll,), in_specs=[SMEM] * 3 + [w...  17.6 us
    all_to_all x1, starting transfers between devices, local(): p_in = lax.all_to_all(p_out, 'ctx', 0, 0, tiled=True)  16.1 us
  transfers between devices with their start and end apart: 20, of which 6 were waited for; matrix products, arithmetic and copies ran while one was open for 11% of the time, Pallas kernels for 2%

profile of v2, /device:TPU:1, one launch (start us, length us, event | category | flops | bytes accessed | tf_op | source)
XLA Modules:
  0.0 286.2 jit_solution(3106553205388075223)
XLA Ops:
  4.2 8.8 %collective-permute-start.5 = (bf16[2,64,256]{2,1,0:T(8,128)(2,1)S(1)}, bf16[2,64,256]{2,1,0:T(8,128)(2,1)S(1)}, u32[]{:S(2)}, u32[]{:S(2)}) collective-permute-start(bf16[2,64,256]{2,1,0:T(8,128)(2,1)S(1)} %pad_maximum_fusion), channel_id=1, source_target_pairs={{0,8},{8,0},{16,24},{24,16},{32,40},{40,32},{48,56},{56,48},{64,72... | collective-permute-start | bytes 196616 | tf_op jit(solution)/shard_map/ppermute | solution.py:246
  15.0 1.8 fusion.59.t_ref
  19.3 4.0 %all-to-all-start = ((bf16[8,16,16,128]{3,2,1,0:T(8,128)(2,1)}), bf16[8,16,16,128]{3,2,1,0:T(8,128)(2,1)S(1)}, u32[]{:S(2)}, u32[]{:S(2)}) async-start(bf16[8,16,16,128]{3,2,1,0:T(8,128)(2,1)} %shard_map.113), calls=%async_computation | async-start | bytes 1048576 | tf_op jit(solution)/shard_map/all_to_all | solution.py:221
  23.3 2.5 collective-permute-start.3
  27.9 11.3 %all-to-all-done.x_ref = bf16[8,16,16,128]{3,2,1,0:T(8,128)(2,1)S(1)} async-done(((bf16[8,16,16,128]{3,2,1,0:T(8,128)(2,1)}), bf16[8,16,16,128]{3,2,1,0:T(8,128)(2,1)S(1)}, u32[]{:S(2)}, u32[]{:S(2)}) %all-to-all-start) | async-done | bytes 524320 | tf_op jit(solution)/shard_map/all_to_all | solution.py:221
  39.2 1.7 shard_map.114
  41.0 16.1 %all-to-all-start.1 = ((bf16[64,4,16,128]{3,2,1,0:T(8,128)(2,1)}), bf16[64,4,16,128]{3,2,1,0:T(8,128)(2,1)S(1)}, u32[]{:S(2)}, u32[]{:S(2)}) async-start(bf16[64,4,16,128]{3,2,1,0:T(8,128)(2,1)} %get-tuple-element.15), calls=%async_computation.1 | async-start | bytes 2097152 | tf_op jit(solution)/shard_map/all_to_all | solution.py:251
  57.2 3.3 %collective-permute-start.6 = (bf16[2,64,256]{2,1,0:T(8,128)(2,1)S(1)}, bf16[2,64,256]{2,1,0:T(8,128)(2,1)S(1)}, u32[]{:S(2)}, u32[]{:S(2)}) collective-permute-start(bf16[2,64,256]{2,1,0:T(8,128)(2,1)S(1)} %broadcast_select_fusion), channel_id=1, source_target_pairs={{0,16},{8,24},{16,0},{24,8},{32,48},{40,56},{48,32},{56,40},{64,80... | collective-permute-start | bytes 196616 | tf_op jit(solution)/shard_map/ppermute | solution.py:246
  60.5 14.7 %collective-permute-done.6 = bf16[2,64,256]{2,1,0:T(8,128)(2,1)S(1)} collective-permute-done((bf16[2,64,256]{2,1,0:T(8,128)(2,1)S(1)}, bf16[2,64,256]{2,1,0:T(8,128)(2,1)S(1)}, u32[]{:S(2)}, u32[]{:S(2)}) %collective-permute-start.6) | collective-permute-done | bytes 65568 | tf_op jit(solution)/shard_map/ppermute | solution.py:246
  75.3 6.1 %collective-permute-start.7 = (bf16[2,64,256]{2,1,0:T(8,128)(2,1)S(1)}, bf16[2,64,256]{2,1,0:T(8,128)(2,1)S(1)}, u32[]{:S(2)}, u32[]{:S(2)}) collective-permute-start(bf16[2,64,256]{2,1,0:T(8,128)(2,1)S(1)} %broadcast_select_fusion.1), channel_id=1, source_target_pairs={{0,32},{8,40},{16,48},{24,56},{32,0},{40,8},{48,16},{56,24},{64,96... | collective-permute-start | bytes 196616 | tf_op jit(solution)/shard_map/ppermute | solution.py:246
  81.6 3.9 %collective-permute-done.7 = bf16[2,64,256]{2,1,0:T(8,128)(2,1)S(1)} collective-permute-done((bf16[2,64,256]{2,1,0:T(8,128)(2,1)S(1)}, bf16[2,64,256]{2,1,0:T(8,128)(2,1)S(1)}, u32[]{:S(2)}, u32[]{:S(2)}) %collective-permute-start.7) | collective-permute-done | bytes 65568 | tf_op jit(solution)/shard_map/ppermute | solution.py:246
  85.6 3.1 %collective-permute-start.8 = (bf16[2,64,256]{2,1,0:T(8,128)(2,1)S(1)}, bf16[2,64,256]{2,1,0:T(8,128)(2,1)S(1)}, u32[]{:S(2)}, u32[]{:S(2)}) collective-permute-start(bf16[2,64,256]{2,1,0:T(8,128)(2,1)S(1)} %broadcast_select_fusion.2), channel_id=1, source_target_pairs={{0,64},{8,72},{16,80},{24,88},{32,96},{40,104},{48,112},{56,120},{... | collective-permute-start | bytes 196616 | tf_op jit(solution)/shard_map/ppermute | solution.py:246
  88.7 1.9 collective-permute-done.8
  90.6 4.0 %collective-permute-start.9 = (bf16[2,64,256]{2,1,0:T(8,128)(2,1)S(1)}, bf16[2,64,256]{2,1,0:T(8,128)(2,1)S(1)}, u32[]{:S(2)}, u32[]{:S(2)}) collective-permute-start(bf16[2,64,256]{2,1,0:T(8,128)(2,1)S(1)} %broadcast_select_fusion.3), channel_id=1, source_target_pairs={{0,128},{8,136},{16,144},{24,152},{32,160},{40,168},{48,176},{56,1... | collective-permute-start | bytes 196616 | tf_op jit(solution)/shard_map/ppermute | solution.py:246
  94.7 3.4 %collective-permute-start = (bf16[16,128]{1,0:T(8,128)(2,1)S(1)}, bf16[16,128]{1,0:T(8,128)(2,1)S(1)}, u32[]{:S(2)}, u32[]{:S(2)}) collective-permute-start(bf16[16,128]{1,0:T(8,128)(2,1)S(1)} %get-tuple-element.39), channel_id=1, source_target_pairs={{0,8},{8,16},{16,24},{24,32},{32,40},{40,48},{48,56},{56,64},{64,7... | collective-permute-start | bytes 12296 | tf_op jit(solution)/shard_map/ppermute | solution.py:236
  98.1 1.9 collective-permute-start.1
  100.1 5.9 %collective-permute-start.10 = (bf16[2,64,256]{2,1,0:T(8,128)(2,1)S(1)}, bf16[2,64,256]{2,1,0:T(8,128)(2,1)S(1)}, u32[]{:S(2)}, u32[]{:S(2)}) collective-permute-start(bf16[2,64,256]{2,1,0:T(8,128)(2,1)S(1)} %broadcast_select_fusion.4), channel_id=1, source_target_pairs={{0,256},{8,264},{16,272},{24,280},{32,288},{40,296},{48,304},{56,3... | collective-permute-start | bytes 196616 | tf_op jit(solution)/shard_map/ppermute | solution.py:246
  106.9 1.9 collective-permute-start.2
  108.9 7.8 %collective-permute-start.4 = (bf16[64,256]{1,0:T(8,128)(2,1)S(1)}, bf16[64,256]{1,0:T(8,128)(2,1)S(1)}, u32[]{:S(2)}, u32[]{:S(2)}) collective-permute-start(bf16[64,256]{1,0:T(8,128)(2,1)S(1)} %pad_maximum_fusion.2), channel_id=1, source_target_pairs={{8,0},{16,8},{24,16},{32,24},{40,32},{48,40},{56,48},{64,56},{72,6... | collective-permute-start | bytes 98312 | tf_op jit(solution)/shard_map/ppermute | solution.py:235
  118.3 2.0 copy-done
  120.4 3.4 %collective-permute-done.4.after_ref = bf16[64,256]{1,0:T(8,128)(2,1)S(1)} collective-permute-done((bf16[64,256]{1,0:T(8,128)(2,1)S(1)}, bf16[64,256]{1,0:T(8,128)(2,1)S(1)}, u32[]{:S(2)}, u32[]{:S(2)}) %collective-permute-start.4) | collective-permute-done | bytes 32800 | tf_op jit(solution)/shard_map/ppermute | solution.py:235
  124.5 9.0 %all-to-all-start.2 = ((bf16[64,2,64,256]{3,2,1,0:T(8,128)(2,1)}), bf16[64,2,64,256]{3,2,1,0:T(8,128)(2,1)}, u32[]{:S(2)}, u32[]{:S(2)}) async-start(bf16[64,2,64,256]{3,2,1,0:T(8,128)(2,1)} %bitcast.37), calls=%async_computation.2 | async-start | bytes 8388608 | tf_op jit(solution)/shard_map/all_to_all | solution.py:273
  133.5 1.9 collective-permute-start.11
  136.1 3.6 %collective-permute-start.13 = (bf16[68,16,128]{2,1,0:T(8,128)(2,1)S(1)}, bf16[68,16,128]{2,1,0:T(8,128)(2,1)}, u32[]{:S(2)}, u32[]{:S(2)}) collective-permute-start(bf16[68,16,128]{2,1,0:T(8,128)(2,1)S(1)} %shard_map.115.refs_0_), channel_id=1, source_target_pairs={{0,4},{1,5},{2,6},{3,7},{4,0},{5,1},{6,2},{7,3},{8,12},{9,13},{10,... | collective-permute-start | bytes 835592 | tf_op jit(solution)/shard_map/ppermute | solution.py:279
  139.7 2.9 %collective-permute-start.15 = (bf16[68,16,128]{2,1,0:T(8,128)(2,1)S(1)}, bf16[68,16,128]{2,1,0:T(8,128)(2,1)}, u32[]{:S(2)}, u32[]{:S(2)}) collective-permute-start(bf16[68,16,128]{2,1,0:T(8,128)(2,1)S(1)} %shard_map.115.refs_0_), channel_id=1, source_target_pairs={{0,6},{1,7},{2,0},{3,1},{4,2},{5,3},{6,4},{7,5},{8,14},{9,15},{10,... | collective-permute-start | bytes 835592 | tf_op jit(solution)/shard_map/ppermute | solution.py:279
  142.6 2.5 collective-permute-start.12
  145.1 3.7 %collective-permute-start.14 = (bf16[68,16,128]{2,1,0:T(8,128)(2,1)S(1)}, bf16[68,16,128]{2,1,0:T(8,128)(2,1)}, u32[]{:S(2)}, u32[]{:S(2)}) collective-permute-start(bf16[68,16,128]{2,1,0:T(8,128)(2,1)S(1)} %collective-permute-done.2.refs_1_), channel_id=1, source_target_pairs={{0,4},{1,5},{2,6},{3,7},{4,0},{5,1},{6,2},{7,3},{8,12},{9,13},{10,... | collective-permute-start | bytes 835592 | tf_op jit(solution)/shard_map/ppermute | solution.py:279
  148.8 4.1 %collective-permute-start.16 = (bf16[68,16,128]{2,1,0:T(8,128)(2,1)S(1)}, bf16[68,16,128]{2,1,0:T(8,128)(2,1)}, u32[]{:S(2)}, u32[]{:S(2)}) collective-permute-start(bf16[68,16,128]{2,1,0:T(8,128)(2,1)S(1)} %collective-permute-done.2.refs_1_), channel_id=1, source_target_pairs={{0,6},{1,7},{2,0},{3,1},{4,2},{5,3},{6,4},{7,5},{8,14},{9,15},{10,... | collective-permute-start | bytes 835592 | tf_op jit(solution)/shard_map/ppermute | solution.py:279
  152.9 26.3 %fusion.41 = (bf16[256,4096]{1,0:T(8,128)(2,1)}, bf16[256,4096]{1,0:T(8,128)(2,1)S(1)}) fusion(s32[]{:T(128)} %bitcast.25, s32[256]{0:T(256)S(1)} %get-tuple-element.55, s32[4096]{0:T(1024)S(1)} %iota_multiply_fusion, s32[256]{0:T(256)S(1)} %get-tuple-element.56, s32[]{:T(128)} %bitcast.13), kind=kLoop, calls=%fused_computation.53 | loop fusion | flops 93323264 | bytes 4212744 | tf_op jit(solution)/shard_map/convert_element_type | solution.py:37
  182.2 51.4 %all-to-all-done.2 = bf16[64,2,64,256]{3,2,1,0:T(8,128)(2,1)} async-done(((bf16[64,2,64,256]{3,2,1,0:T(8,128)(2,1)}), bf16[64,2,64,256]{3,2,1,0:T(8,128)(2,1)}, u32[]{:S(2)}, u32[]{:S(2)}) %all-to-all-start.2) | async-done | bytes 4194336 | tf_op jit(solution)/shard_map/all_to_all | solution.py:273
  237.5 17.6 %shard_map.117 = (bf16[1024,512]{1,0:T(8,128)(2,1)}, f32[64,8,128]{2,1,0:T(8,128)S(1)}) custom-call(s32[48]{0:T(128)S(1)} %convert_add_fusion.arrival_ref, s32[2]{0:T(128)S(1)} %add_convert_fusion.edge_ref, s32[8]{0:T(128)S(1)} %stack.61.from_ref, bf16[1024,512]{1,0:T(8,128)(2,1)S(1)} %copy-done.5, bf16[1024,512]{1,0:T(8,128)(2,1)S(1)} %copy-done.6, ...), custom_call_target="tpu_custom_call" | custom-call | tf_op jit(solution)/shard_map/pallas_call | solution.py:298
  255.1 30.0 %all_to_all.20.recv_ref = f32[64,8,128]{2,1,0:T(8,128)S(1)} all-to-all(f32[64,8,128]{2,1,0:T(8,128)S(1)} %get-tuple-element.22), channel_id=1, replica_groups=mesh['ctx'=64,'head'=8] {'ctx'}, dimensions={0} | all-to-all | bytes 524288 | tf_op jit(solution)/shard_map/all_to_all | solution.py:320
  (89 shorter events, 19.8 us)
Async XLA Ops:
  0.6 56.4 %copy-start.13 = (s32[2]{0:T(128)S(1)}, s32[2]{0:T(128)}, u32[]{:S(2)}) copy-start(s32[2]{0:T(128)} %param.15) | copy-start | bytes 28
  0.6 26.3 %copy-start.11 = (s32[1024,3]{0,1:T(4,128)S(1)}, s32[1024,3]{0,1:T(4,128)}, u32[]{:S(2)}) copy-start(s32[1024,3]{0,1:T(4,128)} %param.14) | copy-start | bytes 36868
  4.2 52.9 %collective-permute-start.5 = (bf16[2,64,256]{2,1,0:T(8,128)(2,1)S(1)}, bf16[2,64,256]{2,1,0:T(8,128)(2,1)S(1)}, u32[]{:S(2)}, u32[]{:S(2)}) collective-permute-start(bf16[2,64,256]{2,1,0:T(8,128)(2,1)S(1)} %pad_maximum_fusion), channel_id=1, source_target_pairs={{0,8},{8,0},{16,24},{24,16},{32,40},{40,32},{48,56},{56,48},{64,72... | collective-permute-start | bytes 196616 | tf_op jit(solution)/shard_map/ppermute | solution.py:246
  16.8 1.2 copy-start.4
  19.3 97.4 %copy-start.2 = (bf16[1024,128]{1,0:T(8,128)(2,1)S(1)}, bf16[1024,128]{1,0:T(8,128)(2,1)}, u32[]{:S(2)}) copy-start(bf16[1024,128]{1,0:T(8,128)(2,1)} %k_ref.3) | copy-start | bytes 786436
  19.3 97.4 %copy-start.3 = (bf16[1024,128]{1,0:T(8,128)(2,1)S(1)}, bf16[1024,128]{1,0:T(8,128)(2,1)}, u32[]{:S(2)}) copy-start(bf16[1024,128]{1,0:T(8,128)(2,1)} %v_ref.3) | copy-start | bytes 786436
  19.3 19.9 %all-to-all-start = ((bf16[8,16,16,128]{3,2,1,0:T(8,128)(2,1)}), bf16[8,16,16,128]{3,2,1,0:T(8,128)(2,1)S(1)}, u32[]{:S(2)}, u32[]{:S(2)}) async-start(bf16[8,16,16,128]{3,2,1,0:T(8,128)(2,1)} %shard_map.113), calls=%async_computation | async-start | bytes 1048576 | tf_op jit(solution)/shard_map/all_to_all | solution.py:221
  23.3 97.1 %collective-permute-start.3 = (bf16[64,256]{1,0:T(8,128)(2,1)S(1)}, bf16[64,256]{1,0:T(8,128)(2,1)S(1)}, u32[]{:S(2)}, u32[]{:S(2)}) collective-permute-start(bf16[64,256]{1,0:T(8,128)(2,1)S(1)} %pad_maximum_fusion.1), channel_id=1, source_target_pairs={{0,8},{8,16},{16,24},{24,32},{32,40},{40,48},{48,56},{56,64},{64,7... | collective-permute-start | bytes 98312 | tf_op jit(solution)/shard_map/ppermute | solution.py:234
  41.0 65.1 %all-to-all-start.1 = ((bf16[64,4,16,128]{3,2,1,0:T(8,128)(2,1)}), bf16[64,4,16,128]{3,2,1,0:T(8,128)(2,1)S(1)}, u32[]{:S(2)}, u32[]{:S(2)}) async-start(bf16[64,4,16,128]{3,2,1,0:T(8,128)(2,1)} %get-tuple-element.15), calls=%async_computation.1 | async-start | bytes 2097152 | tf_op jit(solution)/shard_map/all_to_all | solution.py:251
  57.2 18.0 %collective-permute-start.6 = (bf16[2,64,256]{2,1,0:T(8,128)(2,1)S(1)}, bf16[2,64,256]{2,1,0:T(8,128)(2,1)S(1)}, u32[]{:S(2)}, u32[]{:S(2)}) collective-permute-start(bf16[2,64,256]{2,1,0:T(8,128)(2,1)S(1)} %broadcast_select_fusion), channel_id=1, source_target_pairs={{0,16},{8,24},{16,0},{24,8},{32,48},{40,56},{48,32},{56,40},{64,80... | collective-permute-start | bytes 196616 | tf_op jit(solution)/shard_map/ppermute | solution.py:246
  75.3 10.2 %collective-permute-start.7 = (bf16[2,64,256]{2,1,0:T(8,128)(2,1)S(1)}, bf16[2,64,256]{2,1,0:T(8,128)(2,1)S(1)}, u32[]{:S(2)}, u32[]{:S(2)}) collective-permute-start(bf16[2,64,256]{2,1,0:T(8,128)(2,1)S(1)} %broadcast_select_fusion.1), channel_id=1, source_target_pairs={{0,32},{8,40},{16,48},{24,56},{32,0},{40,8},{48,16},{56,24},{64,96... | collective-permute-start | bytes 196616 | tf_op jit(solution)/shard_map/ppermute | solution.py:246
  85.6 5.0 %collective-permute-start.8 = (bf16[2,64,256]{2,1,0:T(8,128)(2,1)S(1)}, bf16[2,64,256]{2,1,0:T(8,128)(2,1)S(1)}, u32[]{:S(2)}, u32[]{:S(2)}) collective-permute-start(bf16[2,64,256]{2,1,0:T(8,128)(2,1)S(1)} %broadcast_select_fusion.2), channel_id=1, source_target_pairs={{0,64},{8,72},{16,80},{24,88},{32,96},{40,104},{48,112},{56,120},{... | collective-permute-start | bytes 196616 | tf_op jit(solution)/shard_map/ppermute | solution.py:246
  90.6 9.4 %collective-permute-start.9 = (bf16[2,64,256]{2,1,0:T(8,128)(2,1)S(1)}, bf16[2,64,256]{2,1,0:T(8,128)(2,1)S(1)}, u32[]{:S(2)}, u32[]{:S(2)}) collective-permute-start(bf16[2,64,256]{2,1,0:T(8,128)(2,1)S(1)} %broadcast_select_fusion.3), channel_id=1, source_target_pairs={{0,128},{8,136},{16,144},{24,152},{32,160},{40,168},{48,176},{56,1... | collective-permute-start | bytes 196616 | tf_op jit(solution)/shard_map/ppermute | solution.py:246
  94.7 11.4 %collective-permute-start = (bf16[16,128]{1,0:T(8,128)(2,1)S(1)}, bf16[16,128]{1,0:T(8,128)(2,1)S(1)}, u32[]{:S(2)}, u32[]{:S(2)}) collective-permute-start(bf16[16,128]{1,0:T(8,128)(2,1)S(1)} %get-tuple-element.39), channel_id=1, source_target_pairs={{0,8},{8,16},{16,24},{24,32},{32,40},{40,48},{48,56},{56,64},{64,7... | collective-permute-start | bytes 12296 | tf_op jit(solution)/shard_map/ppermute | solution.py:236
  98.1 8.0 %collective-permute-start.1 = (bf16[16,128]{1,0:T(8,128)(2,1)S(1)}, bf16[16,128]{1,0:T(8,128)(2,1)S(1)}, u32[]{:S(2)}, u32[]{:S(2)}) collective-permute-start(bf16[16,128]{1,0:T(8,128)(2,1)S(1)} %get-tuple-element.38), channel_id=1, source_target_pairs={{8,0},{16,8},{24,16},{32,24},{40,32},{48,40},{56,48},{64,56},{72,6... | collective-permute-start | bytes 12296 | tf_op jit(solution)/shard_map/ppermute | solution.py:237
  100.1 20.2 %collective-permute-start.10 = (bf16[2,64,256]{2,1,0:T(8,128)(2,1)S(1)}, bf16[2,64,256]{2,1,0:T(8,128)(2,1)S(1)}, u32[]{:S(2)}, u32[]{:S(2)}) collective-permute-start(bf16[2,64,256]{2,1,0:T(8,128)(2,1)S(1)} %broadcast_select_fusion.4), channel_id=1, source_target_pairs={{0,256},{8,264},{16,272},{24,280},{32,288},{40,296},{48,304},{56,3... | collective-permute-start | bytes 196616 | tf_op jit(solution)/shard_map/ppermute | solution.py:246
  106.9 16.9 %collective-permute-start.2 = (bf16[68,16,128]{2,1,0:T(8,128)(2,1)S(1)}, bf16[68,16,128]{2,1,0:T(8,128)(2,1)S(1)}, u32[]{:S(2)}, u32[]{:S(2)}) collective-permute-start(bf16[68,16,128]{2,1,0:T(8,128)(2,1)S(1)} %shard_map.115.refs_0_), channel_id=1, source_target_pairs={{0,1},{1,0},{2,3},{3,2},{4,5},{5,4},{6,7},{7,6},{8,9},{9,8},{10,11... | collective-permute-start | bytes 835592 | tf_op jit(solution)/shard_map/ppermute | solution.py:259
  108.9 15.0 %collective-permute-start.4 = (bf16[64,256]{1,0:T(8,128)(2,1)S(1)}, bf16[64,256]{1,0:T(8,128)(2,1)S(1)}, u32[]{:S(2)}, u32[]{:S(2)}) collective-permute-start(bf16[64,256]{1,0:T(8,128)(2,1)S(1)} %pad_maximum_fusion.2), channel_id=1, source_target_pairs={{8,0},{16,8},{24,16},{32,24},{40,32},{48,40},{56,48},{64,56},{72,6... | collective-permute-start | bytes 98312 | tf_op jit(solution)/shard_map/ppermute | solution.py:235
  118.3 2.0 copy-start
  120.4 3.5 %copy-start.7 = (bf16[64,256]{1,0:T(8,128)(2,1)}, bf16[64,256]{1,0:T(8,128)(2,1)S(1)}, u32[]{:S(2)}) copy-start(bf16[64,256]{1,0:T(8,128)(2,1)S(1)} %collective-permute-done.3.before_ref) | copy-start | bytes 98308
  124.5 109.1 %all-to-all-start.2 = ((bf16[64,2,64,256]{3,2,1,0:T(8,128)(2,1)}), bf16[64,2,64,256]{3,2,1,0:T(8,128)(2,1)}, u32[]{:S(2)}, u32[]{:S(2)}) async-start(bf16[64,2,64,256]{3,2,1,0:T(8,128)(2,1)} %bitcast.37), calls=%async_computation.2 | async-start | bytes 8388608 | tf_op jit(solution)/shard_map/all_to_all | solution.py:273
  133.5 45.8 %copy-start.12 = (f32[1,4,256]{2,1,0:T(4,128)S(1)}, f32[1,4,256]{2,1,0:T(4,128)}, u32[]{:S(2)}) copy-start(f32[1,4,256]{2,1,0:T(4,128)} %param.17) | copy-start | bytes 12292
  133.5 15.3 %collective-permute-start.11 = (bf16[68,16,128]{2,1,0:T(8,128)(2,1)S(1)}, bf16[68,16,128]{2,1,0:T(8,128)(2,1)S(1)}, u32[]{:S(2)}, u32[]{:S(2)}) collective-permute-start(bf16[68,16,128]{2,1,0:T(8,128)(2,1)S(1)} %shard_map.115.refs_0_), channel_id=1, source_target_pairs={{0,2},{1,3},{2,4},{3,5},{4,6},{5,7},{6,0},{7,1},{8,10},{9,11},{10,... | collective-permute-start | bytes 835592 | tf_op jit(solution)/shard_map/ppermute | solution.py:279
  136.1 46.1 %collective-permute-start.13 = (bf16[68,16,128]{2,1,0:T(8,128)(2,1)S(1)}, bf16[68,16,128]{2,1,0:T(8,128)(2,1)}, u32[]{:S(2)}, u32[]{:S(2)}) collective-permute-start(bf16[68,16,128]{2,1,0:T(8,128)(2,1)S(1)} %shard_map.115.refs_0_), channel_id=1, source_target_pairs={{0,4},{1,5},{2,6},{3,7},{4,0},{5,1},{6,2},{7,3},{8,12},{9,13},{10,... | collective-permute-start | bytes 835592 | tf_op jit(solution)/shard_map/ppermute | solution.py:279
  139.7 42.4 %collective-permute-start.15 = (bf16[68,16,128]{2,1,0:T(8,128)(2,1)S(1)}, bf16[68,16,128]{2,1,0:T(8,128)(2,1)}, u32[]{:S(2)}, u32[]{:S(2)}) collective-permute-start(bf16[68,16,128]{2,1,0:T(8,128)(2,1)S(1)} %shard_map.115.refs_0_), channel_id=1, source_target_pairs={{0,6},{1,7},{2,0},{3,1},{4,2},{5,3},{6,4},{7,5},{8,14},{9,15},{10,... | collective-permute-start | bytes 835592 | tf_op jit(solution)/shard_map/ppermute | solution.py:279
  142.6 39.6 %collective-permute-start.12 = (bf16[68,16,128]{2,1,0:T(8,128)(2,1)S(1)}, bf16[68,16,128]{2,1,0:T(8,128)(2,1)}, u32[]{:S(2)}, u32[]{:S(2)}) collective-permute-start(bf16[68,16,128]{2,1,0:T(8,128)(2,1)S(1)} %collective-permute-done.2.refs_1_), channel_id=1, source_target_pairs={{0,2},{1,3},{2,4},{3,5},{4,6},{5,7},{6,0},{7,1},{8,10},{9,11},{10,... | collective-permute-start | bytes 835592 | tf_op jit(solution)/shard_map/ppermute | solution.py:279
  145.1 37.1 %collective-permute-start.14 = (bf16[68,16,128]{2,1,0:T(8,128)(2,1)S(1)}, bf16[68,16,128]{2,1,0:T(8,128)(2,1)}, u32[]{:S(2)}, u32[]{:S(2)}) collective-permute-start(bf16[68,16,128]{2,1,0:T(8,128)(2,1)S(1)} %collective-permute-done.2.refs_1_), channel_id=1, source_target_pairs={{0,4},{1,5},{2,6},{3,7},{4,0},{5,1},{6,2},{7,3},{8,12},{9,13},{10,... | collective-permute-start | bytes 835592 | tf_op jit(solution)/shard_map/ppermute | solution.py:279
  148.8 33.4 %collective-permute-start.16 = (bf16[68,16,128]{2,1,0:T(8,128)(2,1)S(1)}, bf16[68,16,128]{2,1,0:T(8,128)(2,1)}, u32[]{:S(2)}, u32[]{:S(2)}) collective-permute-start(bf16[68,16,128]{2,1,0:T(8,128)(2,1)S(1)} %collective-permute-done.2.refs_1_), channel_id=1, source_target_pairs={{0,6},{1,7},{2,0},{3,1},{4,2},{5,3},{6,4},{7,5},{8,14},{9,15},{10,... | collective-permute-start | bytes 835592 | tf_op jit(solution)/shard_map/ppermute | solution.py:279
  179.3 1.6 copy-start.1
  233.5 1.2 copy-start.5
  234.8 1.2 copy-start.6
  236.0 0.8 copy-start.8
  (2 other events, 1.4 us)

commit v3 on v2

--- a/solution.py
+++ b/solution.py
@@ -233,8 +233,6 @@
 
     kv_before = lax.ppermute(jnp.concatenate([keys[-BLK:], values[-BLK:]], axis=1), "ctx", up)
     kv_after = lax.ppermute(jnp.concatenate([keys[:BLK], values[:BLK]], axis=1), "ctx", down)
-    p_before = lax.ppermute(own[-1], "ctx", up)
-    p_after = lax.ppermute(own[0], "ctx", down)
     kv_glob = []
     for g in range(GLOB):
         row = global_inner[g] * BLK
@@ -248,7 +246,10 @@
         bit *= 2
     kv_glob = kv_glob.reshape(GLOB * BLK, 2 * h)
 
+    p_out, kv_glob, kv_before, kv_after = lax.optimization_barrier((p_out, kv_glob, kv_before, kv_after))
     p_in = lax.all_to_all(p_out, "ctx", 0, 0, tiled=True)
+    p_before = lax.ppermute(own[-1], "ctx", up)
+    p_after = lax.ppermute(own[0], "ctx", down)
     tiles = pl.pallas_call(
         collect,
         in_specs=[SMEM, SMEM] + [VMEM] * 4,
@@ -266,7 +267,7 @@
             in_specs=[VMEM, VMEM],
             out_specs=pl.BlockSpec((chunk, BLK, 2 * h), lambda i, s: (i, 0, 0)),
         ),
-        out_shape=jax.ShapeDtypeStruct((ctx * CAP, BLK, 2 * h), BF16),
+        out_shape=pltpu.HBM((ctx * CAP, BLK, 2 * h), BF16),
         compiler_params=PARAMS,
     )(sources, keys, values)
     kv_out, pair[1], kv_before, kv_after, kv_glob = lax.optimization_barrier((kv_out, pair[1], kv_before, kv_after, kv_glob))
@@ -302,7 +303,7 @@
         out_specs=[wide, VMEM],
         out_shape=[
             jax.ShapeDtypeStruct((tokens, GROUP * h), BF16),
-            jax.ShapeDtypeStruct((ctx, 2 * share, 128), F32),
+            pltpu.HBM((ctx, 2 * share, 128), F32),
         ],
         scratch_shapes=[
             pltpu.VMEM((tokens + 2 * BLK, h), BF16),

time: 288 us -> 296 us (1.028)
  waiting for transfers between devices: 86.7 us -> 93.6 us
  local copies, waits for them, and re-layouts: 14 us -> 10.6 us
  Pallas kernels: 25.3 us -> 28.4 us
    all_to_all x1, waiting for transfers between devices: 0.01 us -> 11.7 us  [local(): p_in = lax.all_to_all(p_out, 'ctx', 0, 0, tiled=True)]
    all_to_all x1, waiting for transfers between devices: 11.3 us -> 0.01 us  [local(): terms = lax.all_to_all(terms, 'head', 0, 0, tiled=True)]
    ppermute x1, waiting for transfers between devices: 0.01 us -> 10.6 us  [local(): p_before = lax.ppermute(own[-1], 'ctx', up)]
    ppermute x1, starting transfers between devices: 7.83 us -> 2.4 us  [local(): lax.ppermute(jnp.concatenate([keys[:BLK], values[:BLK]], axis=1), 'ctx',...]
    ppermute x1, starting transfers between devices: 1.92 us -> 6.89 us  [local(): lax.ppermute(tiles, 'head', [(i, i ^ 1) for i in range(heads)])]
    ppermute x1, waiting for transfers between devices: 3.44 us -> 0.01 us  [local(): lax.ppermute(jnp.concatenate([keys[:BLK], values[:BLK]], axis=1), 'ctx',...]
    unnamed x29 -> x25, local copies, waits for them, and re-layouts: 10.4 us -> 7.02 us
    all_to_all x1, starting transfers between devices: 16.1 us -> 13 us  [local(): p_in = lax.all_to_all(p_out, 'ctx', 0, 0, tiled=True)]
  transfers between devices with their start and end apart: 20 -> 20, of which waited for: 6 -> 8; matrix products, arithmetic and copies ran while one was open for 11% -> 11% of each run, Pallas kernels for 2% -> 3%
where the time goes in v3:
time: 296 us; the launch traced here: 295 us
  starting transfers between devices  98.2 us (33%)
  waiting for transfers between devices  93.6 us (32%)
  other arithmetic  30.7 us (10%)
  blocking collectives  29.9 us (10%)
  Pallas kernels  28.4 us (10%)
  local copies, waits for them, and re-layouts  10.6 us (4%)
  between operations  3.72 us (1%)
    all_to_all x1, waiting for transfers between devices, local(): lax.all_to_all(kv_out.reshape(ctx, CAP, BLK, 2 * h), 'ctx', 0, 0, tiled=T...  50.8 us
    ppermute x6, starting transfers between devices, local(): other = lax.ppermute(kv_glob, 'ctx', [(i, i ^ bit) for i in range(ctx)])  33.3 us
    all_to_all x1, blocking collectives, local(): grad = lax.all_to_all(grad, 'ctx', 0, 0, tiled=True)  29.9 us
    convert_element_type x2, other arithmetic, proj_table(): return (unit_value * math.sqrt(12.0 / D)).astype(jnp.bfloat16)  28.2 us
    ppermute x6, starting transfers between devices, local(): all_tiles += [lax.ppermute(t, 'head', there) for t in pair]  19.4 us
    pallas_call x1, Pallas kernels, local(): pl.pallas_call(attend, grid=(blocks // unroll,), in_specs=[SMEM] * 3 + [w...  17.8 us
    ppermute x6, waiting for transfers between devices, local(): other = lax.ppermute(kv_glob, 'ctx', [(i, i ^ bit) for i in range(ctx)])  17.5 us
    all_to_all x1, starting transfers between devices, local(): p_in = lax.all_to_all(p_out, 'ctx', 0, 0, tiled=True)  13 us
  transfers between devices with their start and end apart: 20, of which 8 were waited for; matrix products, arithmetic and copies ran while one was open for 11% of the time, Pallas kernels for 3%

profile of v3, /device:TPU:1, one launch (start us, length us, event | category | flops | bytes accessed | tf_op | source)
XLA Modules:
  0.0 295.0 jit_solution(9912441294699430784)
XLA Ops:
  4.1 8.8 %collective-permute-start.2 = (bf16[2,64,256]{2,1,0:T(8,128)(2,1)S(1)}, bf16[2,64,256]{2,1,0:T(8,128)(2,1)S(1)}, u32[]{:S(2)}, u32[]{:S(2)}) collective-permute-start(bf16[2,64,256]{2,1,0:T(8,128)(2,1)S(1)} %pad_maximum_fusion), channel_id=1, source_target_pairs={{0,8},{8,0},{16,24},{24,16},{32,40},{40,32},{48,56},{56,48},{64,72... | collective-permute-start | bytes 196616 | tf_op jit(solution)/shard_map/ppermute | solution.py:244
  12.9 1.9 collective-permute-start.8
  14.9 2.4 collective-permute-start.9
  20.0 1.9 collective-permute-start.3
  22.0 1.8 fusion.59.t_ref
  26.3 4.4 %all-to-all-start = ((bf16[8,16,16,128]{3,2,1,0:T(8,128)(2,1)}), bf16[8,16,16,128]{3,2,1,0:T(8,128)(2,1)S(1)}, u32[]{:S(2)}, u32[]{:S(2)}) async-start(bf16[8,16,16,128]{3,2,1,0:T(8,128)(2,1)} %shard_map.113), calls=%async_computation | async-start | bytes 1048576 | tf_op jit(solution)/shard_map/all_to_all | solution.py:221
  30.8 6.3 %collective-permute-start.4 = (bf16[2,64,256]{2,1,0:T(8,128)(2,1)S(1)}, bf16[2,64,256]{2,1,0:T(8,128)(2,1)S(1)}, u32[]{:S(2)}, u32[]{:S(2)}) collective-permute-start(bf16[2,64,256]{2,1,0:T(8,128)(2,1)S(1)} %broadcast_select_fusion.1), channel_id=1, source_target_pairs={{0,32},{8,40},{16,48},{24,56},{32,0},{40,8},{48,16},{56,24},{64,96... | collective-permute-start | bytes 196616 | tf_op jit(solution)/shard_map/ppermute | solution.py:244
  37.2 12.3 %collective-permute-done.4 = bf16[2,64,256]{2,1,0:T(8,128)(2,1)S(1)} collective-permute-done((bf16[2,64,256]{2,1,0:T(8,128)(2,1)S(1)}, bf16[2,64,256]{2,1,0:T(8,128)(2,1)S(1)}, u32[]{:S(2)}, u32[]{:S(2)}) %collective-permute-start.4) | collective-permute-done | bytes 65568 | tf_op jit(solution)/shard_map/ppermute | solution.py:244
  49.6 3.9 %collective-permute-start.5 = (bf16[2,64,256]{2,1,0:T(8,128)(2,1)S(1)}, bf16[2,64,256]{2,1,0:T(8,128)(2,1)S(1)}, u32[]{:S(2)}, u32[]{:S(2)}) collective-permute-start(bf16[2,64,256]{2,1,0:T(8,128)(2,1)S(1)} %broadcast_select_fusion.2), channel_id=1, source_target_pairs={{0,64},{8,72},{16,80},{24,88},{32,96},{40,104},{48,112},{56,120},{... | collective-permute-start | bytes 196616 | tf_op jit(solution)/shard_map/ppermute | solution.py:244
  55.6 5.8 %collective-permute-start.6 = (bf16[2,64,256]{2,1,0:T(8,128)(2,1)S(1)}, bf16[2,64,256]{2,1,0:T(8,128)(2,1)S(1)}, u32[]{:S(2)}, u32[]{:S(2)}) collective-permute-start(bf16[2,64,256]{2,1,0:T(8,128)(2,1)S(1)} %broadcast_select_fusion.3), channel_id=1, source_target_pairs={{0,128},{8,136},{16,144},{24,152},{32,160},{40,168},{48,176},{56,1... | collective-permute-start | bytes 196616 | tf_op jit(solution)/shard_map/ppermute | solution.py:244
  63.2 6.6 %collective-permute-start.7 = (bf16[2,64,256]{2,1,0:T(8,128)(2,1)S(1)}, bf16[2,64,256]{2,1,0:T(8,128)(2,1)S(1)}, u32[]{:S(2)}, u32[]{:S(2)}) collective-permute-start(bf16[2,64,256]{2,1,0:T(8,128)(2,1)S(1)} %broadcast_select_fusion.4), channel_id=1, source_target_pairs={{0,256},{8,264},{16,272},{24,280},{32,288},{40,296},{48,304},{56,3... | collective-permute-start | bytes 196616 | tf_op jit(solution)/shard_map/ppermute | solution.py:244
  70.1 2.1 collective-permute-done.7
  72.2 1.7 shard_map.114
  74.0 13.0 %all-to-all-start.1 = ((bf16[64,4,16,128]{3,2,1,0:T(8,128)(2,1)}), bf16[64,4,16,128]{3,2,1,0:T(8,128)(2,1)S(1)}, u32[]{:S(2)}, u32[]{:S(2)}) async-start(bf16[64,4,16,128]{3,2,1,0:T(8,128)(2,1)} %get-tuple-element.20), calls=%async_computation.1 | async-start | bytes 2097152 | tf_op jit(solution)/shard_map/all_to_all | solution.py:250
  87.7 3.5 %collective-permute-start = (bf16[16,128]{1,0:T(8,128)(2,1)S(1)}, bf16[16,128]{1,0:T(8,128)(2,1)S(1)}, u32[]{:S(2)}, u32[]{:S(2)}) collective-permute-start(bf16[16,128]{1,0:T(8,128)(2,1)S(1)} %get-tuple-element.47), channel_id=1, source_target_pairs={{0,8},{8,16},{16,24},{24,32},{32,40},{40,48},{48,56},{56,64},{64,7... | collective-permute-start | bytes 12296 | tf_op jit(solution)/shard_map/ppermute | solution.py:251
  91.2 1.9 collective-permute-start.1
  93.2 10.6 %collective-permute-done.before_ref = bf16[16,128]{1,0:T(8,128)(2,1)S(1)} collective-permute-done((bf16[16,128]{1,0:T(8,128)(2,1)S(1)}, bf16[16,128]{1,0:T(8,128)(2,1)S(1)}, u32[]{:S(2)}, u32[]{:S(2)}) %collective-permute-start) | collective-permute-done | bytes 4128 | tf_op jit(solution)/shard_map/ppermute | solution.py:251
  103.8 11.7 %all-to-all-done.1 = bf16[64,4,16,128]{3,2,1,0:T(8,128)(2,1)S(1)} async-done(((bf16[64,4,16,128]{3,2,1,0:T(8,128)(2,1)}), bf16[64,4,16,128]{3,2,1,0:T(8,128)(2,1)S(1)}, u32[]{:S(2)}, u32[]{:S(2)}) %all-to-all-start.1) | async-done | bytes 1048608 | tf_op jit(solution)/shard_map/all_to_all | solution.py:250
  116.4 6.9 %collective-permute-start.10 = (bf16[68,16,128]{2,1,0:T(8,128)(2,1)S(1)}, bf16[68,16,128]{2,1,0:T(8,128)(2,1)S(1)}, u32[]{:S(2)}, u32[]{:S(2)}) collective-permute-start(bf16[68,16,128]{2,1,0:T(8,128)(2,1)S(1)} %shard_map.115.refs_0_), channel_id=1, source_target_pairs={{0,1},{1,0},{2,3},{3,2},{4,5},{5,4},{6,7},{7,6},{8,9},{9,8},{10,11... | collective-permute-start | bytes 835592 | tf_op jit(solution)/shard_map/ppermute | solution.py:260
  123.3 4.5 %shard_map.112 = bf16[128,64,256]{2,1,0:T(8,128)(2,1)} custom-call(s32[128]{0:T(128)S(1)} %reshape.151.src_ref, bf16[1024,128]{1,0:T(8,128)(2,1)S(1)} %copy-done.1, bf16[1024,128]{1,0:T(8,128)(2,1)S(1)} %copy-done.2), custom_call_target="tpu_custom_call" | custom-call | tf_op jit(solution)/shard_map/pallas_call | solution.py:262
  127.8 2.9 collective-permute-done.10.refs_1_
  130.7 11.3 %all-to-all-start.2 = ((bf16[64,2,64,256]{3,2,1,0:T(8,128)(2,1)}), bf16[64,2,64,256]{3,2,1,0:T(8,128)(2,1)}, u32[]{:S(2)}, u32[]{:S(2)}) async-start(bf16[64,2,64,256]{3,2,1,0:T(8,128)(2,1)} %bitcast.39), calls=%async_computation.2 | async-start | bytes 8388608 | tf_op jit(solution)/shard_map/all_to_all | solution.py:274
  142.0 3.4 %collective-permute-start.11 = (bf16[68,16,128]{2,1,0:T(8,128)(2,1)S(1)}, bf16[68,16,128]{2,1,0:T(8,128)(2,1)S(1)}, u32[]{:S(2)}, u32[]{:S(2)}) collective-permute-start(bf16[68,16,128]{2,1,0:T(8,128)(2,1)S(1)} %shard_map.115.refs_0_), channel_id=1, source_target_pairs={{0,2},{1,3},{2,4},{3,5},{4,6},{5,7},{6,0},{7,1},{8,10},{9,11},{10,... | collective-permute-start | bytes 835592 | tf_op jit(solution)/shard_map/ppermute | solution.py:280
  146.1 4.3 %collective-permute-start.13 = (bf16[68,16,128]{2,1,0:T(8,128)(2,1)S(1)}, bf16[68,16,128]{2,1,0:T(8,128)(2,1)}, u32[]{:S(2)}, u32[]{:S(2)}) collective-permute-start(bf16[68,16,128]{2,1,0:T(8,128)(2,1)S(1)} %shard_map.115.refs_0_), channel_id=1, source_target_pairs={{0,4},{1,5},{2,6},{3,7},{4,0},{5,1},{6,2},{7,3},{8,12},{9,13},{10,... | collective-permute-start | bytes 835592 | tf_op jit(solution)/shard_map/ppermute | solution.py:280
  150.4 3.0 %collective-permute-start.15 = (bf16[68,16,128]{2,1,0:T(8,128)(2,1)S(1)}, bf16[68,16,128]{2,1,0:T(8,128)(2,1)}, u32[]{:S(2)}, u32[]{:S(2)}) collective-permute-start(bf16[68,16,128]{2,1,0:T(8,128)(2,1)S(1)} %shard_map.115.refs_0_), channel_id=1, source_target_pairs={{0,6},{1,7},{2,0},{3,1},{4,2},{5,3},{6,4},{7,5},{8,14},{9,15},{10,... | collective-permute-start | bytes 835592 | tf_op jit(solution)/shard_map/ppermute | solution.py:280
  153.5 2.3 collective-permute-start.12
  155.7 2.8 collective-permute-start.14
  158.5 3.6 %collective-permute-start.16 = (bf16[68,16,128]{2,1,0:T(8,128)(2,1)S(1)}, bf16[68,16,128]{2,1,0:T(8,128)(2,1)}, u32[]{:S(2)}, u32[]{:S(2)}) collective-permute-start(bf16[68,16,128]{2,1,0:T(8,128)(2,1)S(1)} %collective-permute-done.10.refs_1_), channel_id=1, source_target_pairs={{0,6},{1,7},{2,0},{3,1},{4,2},{5,3},{6,4},{7,5},{8,14},{9,15},{10,... | collective-permute-start | bytes 835592 | tf_op jit(solution)/shard_map/ppermute | solution.py:280
  162.2 26.3 %fusion.41 = (bf16[256,4096]{1,0:T(8,128)(2,1)}, bf16[256,4096]{1,0:T(8,128)(2,1)S(1)}) fusion(s32[]{:T(128)} %bitcast.25, s32[256]{0:T(256)S(1)} %get-tuple-element.63, s32[4096]{0:T(1024)S(1)} %iota_multiply_fusion, s32[256]{0:T(256)S(1)} %get-tuple-element.64, s32[]{:T(128)} %bitcast.13), kind=kLoop, calls=%fused_computation.53 | loop fusion | flops 93323264 | bytes 4212744 | tf_op jit(solution)/shard_map/convert_element_type | solution.py:37
  191.4 50.8 %all-to-all-done.2 = bf16[64,2,64,256]{3,2,1,0:T(8,128)(2,1)} async-done(((bf16[64,2,64,256]{3,2,1,0:T(8,128)(2,1)}), bf16[64,2,64,256]{3,2,1,0:T(8,128)(2,1)}, u32[]{:S(2)}, u32[]{:S(2)}) %all-to-all-start.2) | async-done | bytes 4194336 | tf_op jit(solution)/shard_map/all_to_all | solution.py:274
  246.2 17.8 %shard_map.117 = (bf16[1024,512]{1,0:T(8,128)(2,1)}, f32[64,8,128]{2,1,0:T(8,128)}) custom-call(s32[48]{0:T(128)S(1)} %convert_add_fusion.arrival_ref, s32[2]{0:T(128)S(1)} %add_convert_fusion.edge_ref, s32[8]{0:T(128)S(1)} %stack.61.from_ref, bf16[1024,512]{1,0:T(8,128)(2,1)S(1)} %copy-done.4, bf16[1024,512]{1,0:T(8,128)(2,1)S(1)} %copy-done.5, ...), custom_call_target="tpu_custom_call" | custom-call | tf_op jit(solution)/shard_map/pallas_call | solution.py:299
  264.0 29.9 %all_to_all.20.recv_ref = f32[64,8,128]{2,1,0:T(8,128)S(1)} all-to-all(f32[64,8,128]{2,1,0:T(8,128)} %get-tuple-element.30), channel_id=1, replica_groups=mesh['ctx'=64,'head'=8] {'ctx'}, dimensions={0} | all-to-all | bytes 524288 | tf_op jit(solution)/shard_map/all_to_all | solution.py:321
  (85 shorter events, 20.7 us)
Async XLA Ops:
  0.6 52.9 %copy-start.10 = (s32[1024,3]{0,1:T(4,128)S(1)}, s32[1024,3]{0,1:T(4,128)}, u32[]{:S(2)}) copy-start(s32[1024,3]{0,1:T(4,128)} %param.14) | copy-start | bytes 36868
  4.1 15.9 %collective-permute-start.2 = (bf16[2,64,256]{2,1,0:T(8,128)(2,1)S(1)}, bf16[2,64,256]{2,1,0:T(8,128)(2,1)S(1)}, u32[]{:S(2)}, u32[]{:S(2)}) collective-permute-start(bf16[2,64,256]{2,1,0:T(8,128)(2,1)S(1)} %pad_maximum_fusion), channel_id=1, source_target_pairs={{0,8},{8,0},{16,24},{24,16},{32,40},{40,32},{48,56},{56,48},{64,72... | collective-permute-start | bytes 196616 | tf_op jit(solution)/shard_map/ppermute | solution.py:244
  12.9 61.0 %collective-permute-start.8 = (bf16[64,256]{1,0:T(8,128)(2,1)S(1)}, bf16[64,256]{1,0:T(8,128)(2,1)S(1)}, u32[]{:S(2)}, u32[]{:S(2)}) collective-permute-start(bf16[64,256]{1,0:T(8,128)(2,1)S(1)} %pad_maximum_fusion.1), channel_id=1, source_target_pairs={{0,8},{8,16},{16,24},{24,32},{32,40},{40,48},{48,56},{56,64},{64,7... | collective-permute-start | bytes 98312 | tf_op jit(solution)/shard_map/ppermute | solution.py:234
  14.9 59.1 %collective-permute-start.9 = (bf16[64,256]{1,0:T(8,128)(2,1)S(1)}, bf16[64,256]{1,0:T(8,128)(2,1)S(1)}, u32[]{:S(2)}, u32[]{:S(2)}) collective-permute-start(bf16[64,256]{1,0:T(8,128)(2,1)S(1)} %pad_maximum_fusion.2), channel_id=1, source_target_pairs={{8,0},{16,8},{24,16},{32,24},{40,32},{48,40},{56,48},{64,56},{72,6... | collective-permute-start | bytes 98312 | tf_op jit(solution)/shard_map/ppermute | solution.py:235
  20.0 10.7 %collective-permute-start.3 = (bf16[2,64,256]{2,1,0:T(8,128)(2,1)S(1)}, bf16[2,64,256]{2,1,0:T(8,128)(2,1)S(1)}, u32[]{:S(2)}, u32[]{:S(2)}) collective-permute-start(bf16[2,64,256]{2,1,0:T(8,128)(2,1)S(1)} %broadcast_select_fusion), channel_id=1, source_target_pairs={{0,16},{8,24},{16,0},{24,8},{32,48},{40,56},{48,32},{56,40},{64,80... | collective-permute-start | bytes 196616 | tf_op jit(solution)/shard_map/ppermute | solution.py:244
  23.8 1.2 copy-start.3
  26.3 97.0 %copy-start.1 = (bf16[1024,128]{1,0:T(8,128)(2,1)S(1)}, bf16[1024,128]{1,0:T(8,128)(2,1)}, u32[]{:S(2)}) copy-start(bf16[1024,128]{1,0:T(8,128)(2,1)} %k_ref.3) | copy-start | bytes 786436
  26.3 97.0 %copy-start.2 = (bf16[1024,128]{1,0:T(8,128)(2,1)S(1)}, bf16[1024,128]{1,0:T(8,128)(2,1)}, u32[]{:S(2)}) copy-start(bf16[1024,128]{1,0:T(8,128)(2,1)} %v_ref.3) | copy-start | bytes 786436
  26.3 45.9 %all-to-all-start = ((bf16[8,16,16,128]{3,2,1,0:T(8,128)(2,1)}), bf16[8,16,16,128]{3,2,1,0:T(8,128)(2,1)S(1)}, u32[]{:S(2)}, u32[]{:S(2)}) async-start(bf16[8,16,16,128]{3,2,1,0:T(8,128)(2,1)} %shard_map.113), calls=%async_computation | async-start | bytes 1048576 | tf_op jit(solution)/shard_map/all_to_all | solution.py:221
  30.8 18.7 %collective-permute-start.4 = (bf16[2,64,256]{2,1,0:T(8,128)(2,1)S(1)}, bf16[2,64,256]{2,1,0:T(8,128)(2,1)S(1)}, u32[]{:S(2)}, u32[]{:S(2)}) collective-permute-start(bf16[2,64,256]{2,1,0:T(8,128)(2,1)S(1)} %broadcast_select_fusion.1), channel_id=1, source_target_pairs={{0,32},{8,40},{16,48},{24,56},{32,0},{40,8},{48,16},{56,24},{64,96... | collective-permute-start | bytes 196616 | tf_op jit(solution)/shard_map/ppermute | solution.py:244
  49.6 5.9 %collective-permute-start.5 = (bf16[2,64,256]{2,1,0:T(8,128)(2,1)S(1)}, bf16[2,64,256]{2,1,0:T(8,128)(2,1)S(1)}, u32[]{:S(2)}, u32[]{:S(2)}) collective-permute-start(bf16[2,64,256]{2,1,0:T(8,128)(2,1)S(1)} %broadcast_select_fusion.2), channel_id=1, source_target_pairs={{0,64},{8,72},{16,80},{24,88},{32,96},{40,104},{48,112},{56,120},{... | collective-permute-start | bytes 196616 | tf_op jit(solution)/shard_map/ppermute | solution.py:244
  55.6 7.5 %collective-permute-start.6 = (bf16[2,64,256]{2,1,0:T(8,128)(2,1)S(1)}, bf16[2,64,256]{2,1,0:T(8,128)(2,1)S(1)}, u32[]{:S(2)}, u32[]{:S(2)}) collective-permute-start(bf16[2,64,256]{2,1,0:T(8,128)(2,1)S(1)} %broadcast_select_fusion.3), channel_id=1, source_target_pairs={{0,128},{8,136},{16,144},{24,152},{32,160},{40,168},{48,176},{56,1... | collective-permute-start | bytes 196616 | tf_op jit(solution)/shard_map/ppermute | solution.py:244
  63.2 8.9 %collective-permute-start.7 = (bf16[2,64,256]{2,1,0:T(8,128)(2,1)S(1)}, bf16[2,64,256]{2,1,0:T(8,128)(2,1)S(1)}, u32[]{:S(2)}, u32[]{:S(2)}) collective-permute-start(bf16[2,64,256]{2,1,0:T(8,128)(2,1)S(1)} %broadcast_select_fusion.4), channel_id=1, source_target_pairs={{0,256},{8,264},{16,272},{24,280},{32,288},{40,296},{48,304},{56,3... | collective-permute-start | bytes 196616 | tf_op jit(solution)/shard_map/ppermute | solution.py:244
  74.0 41.6 %copy-start.6 = (bf16[64,256]{1,0:T(8,128)(2,1)}, bf16[64,256]{1,0:T(8,128)(2,1)S(1)}, u32[]{:S(2)}) copy-start(bf16[64,256]{1,0:T(8,128)(2,1)S(1)} %collective-permute-done.8.before_ref) | copy-start | bytes 98308
  74.0 41.5 %copy-start.8 = (bf16[64,256]{1,0:T(8,128)(2,1)}, bf16[64,256]{1,0:T(8,128)(2,1)S(1)}, u32[]{:S(2)}) copy-start(bf16[64,256]{1,0:T(8,128)(2,1)S(1)} %collective-permute-done.9.after_ref) | copy-start | bytes 98308
  74.0 41.5 %all-to-all-start.1 = ((bf16[64,4,16,128]{3,2,1,0:T(8,128)(2,1)}), bf16[64,4,16,128]{3,2,1,0:T(8,128)(2,1)S(1)}, u32[]{:S(2)}, u32[]{:S(2)}) async-start(bf16[64,4,16,128]{3,2,1,0:T(8,128)(2,1)} %get-tuple-element.20), calls=%async_computation.1 | async-start | bytes 2097152 | tf_op jit(solution)/shard_map/all_to_all | solution.py:250
  87.7 16.1 %collective-permute-start = (bf16[16,128]{1,0:T(8,128)(2,1)S(1)}, bf16[16,128]{1,0:T(8,128)(2,1)S(1)}, u32[]{:S(2)}, u32[]{:S(2)}) collective-permute-start(bf16[16,128]{1,0:T(8,128)(2,1)S(1)} %get-tuple-element.47), channel_id=1, source_target_pairs={{0,8},{8,16},{16,24},{24,32},{32,40},{40,48},{48,56},{56,64},{64,7... | collective-permute-start | bytes 12296 | tf_op jit(solution)/shard_map/ppermute | solution.py:251
  91.2 12.6 %collective-permute-start.1 = (bf16[16,128]{1,0:T(8,128)(2,1)S(1)}, bf16[16,128]{1,0:T(8,128)(2,1)S(1)}, u32[]{:S(2)}, u32[]{:S(2)}) collective-permute-start(bf16[16,128]{1,0:T(8,128)(2,1)S(1)} %get-tuple-element.46), channel_id=1, source_target_pairs={{8,0},{16,8},{24,16},{32,24},{40,32},{48,40},{56,48},{64,56},{72,6... | collective-permute-start | bytes 12296 | tf_op jit(solution)/shard_map/ppermute | solution.py:252
  116.4 14.3 %collective-permute-start.10 = (bf16[68,16,128]{2,1,0:T(8,128)(2,1)S(1)}, bf16[68,16,128]{2,1,0:T(8,128)(2,1)S(1)}, u32[]{:S(2)}, u32[]{:S(2)}) collective-permute-start(bf16[68,16,128]{2,1,0:T(8,128)(2,1)S(1)} %shard_map.115.refs_0_), channel_id=1, source_target_pairs={{0,1},{1,0},{2,3},{3,2},{4,5},{5,4},{6,7},{7,6},{8,9},{9,8},{10,11... | collective-permute-start | bytes 835592 | tf_op jit(solution)/shard_map/ppermute | solution.py:260
  130.7 111.6 %all-to-all-start.2 = ((bf16[64,2,64,256]{3,2,1,0:T(8,128)(2,1)}), bf16[64,2,64,256]{3,2,1,0:T(8,128)(2,1)}, u32[]{:S(2)}, u32[]{:S(2)}) async-start(bf16[64,2,64,256]{3,2,1,0:T(8,128)(2,1)} %bitcast.39), calls=%async_computation.2 | async-start | bytes 8388608 | tf_op jit(solution)/shard_map/all_to_all | solution.py:274
  142.0 46.5 %copy-start.11 = (f32[1,4,256]{2,1,0:T(4,128)S(1)}, f32[1,4,256]{2,1,0:T(4,128)}, u32[]{:S(2)}) copy-start(f32[1,4,256]{2,1,0:T(4,128)} %param.17) | copy-start | bytes 12292
  142.0 16.5 %collective-permute-start.11 = (bf16[68,16,128]{2,1,0:T(8,128)(2,1)S(1)}, bf16[68,16,128]{2,1,0:T(8,128)(2,1)S(1)}, u32[]{:S(2)}, u32[]{:S(2)}) collective-permute-start(bf16[68,16,128]{2,1,0:T(8,128)(2,1)S(1)} %shard_map.115.refs_0_), channel_id=1, source_target_pairs={{0,2},{1,3},{2,4},{3,5},{4,6},{5,7},{6,0},{7,1},{8,10},{9,11},{10,... | collective-permute-start | bytes 835592 | tf_op jit(solution)/shard_map/ppermute | solution.py:280
  146.1 45.3 %collective-permute-start.13 = (bf16[68,16,128]{2,1,0:T(8,128)(2,1)S(1)}, bf16[68,16,128]{2,1,0:T(8,128)(2,1)}, u32[]{:S(2)}, u32[]{:S(2)}) collective-permute-start(bf16[68,16,128]{2,1,0:T(8,128)(2,1)S(1)} %shard_map.115.refs_0_), channel_id=1, source_target_pairs={{0,4},{1,5},{2,6},{3,7},{4,0},{5,1},{6,2},{7,3},{8,12},{9,13},{10,... | collective-permute-start | bytes 835592 | tf_op jit(solution)/shard_map/ppermute | solution.py:280
  150.4 40.9 %collective-permute-start.15 = (bf16[68,16,128]{2,1,0:T(8,128)(2,1)S(1)}, bf16[68,16,128]{2,1,0:T(8,128)(2,1)}, u32[]{:S(2)}, u32[]{:S(2)}) collective-permute-start(bf16[68,16,128]{2,1,0:T(8,128)(2,1)S(1)} %shard_map.115.refs_0_), channel_id=1, source_target_pairs={{0,6},{1,7},{2,0},{3,1},{4,2},{5,3},{6,4},{7,5},{8,14},{9,15},{10,... | collective-permute-start | bytes 835592 | tf_op jit(solution)/shard_map/ppermute | solution.py:280
  153.5 37.9 %collective-permute-start.12 = (bf16[68,16,128]{2,1,0:T(8,128)(2,1)S(1)}, bf16[68,16,128]{2,1,0:T(8,128)(2,1)}, u32[]{:S(2)}, u32[]{:S(2)}) collective-permute-start(bf16[68,16,128]{2,1,0:T(8,128)(2,1)S(1)} %collective-permute-done.10.refs_1_), channel_id=1, source_target_pairs={{0,2},{1,3},{2,4},{3,5},{4,6},{5,7},{6,0},{7,1},{8,10},{9,11},{10,... | collective-permute-start | bytes 835592 | tf_op jit(solution)/shard_map/ppermute | solution.py:280
  155.7 35.7 %collective-permute-start.14 = (bf16[68,16,128]{2,1,0:T(8,128)(2,1)S(1)}, bf16[68,16,128]{2,1,0:T(8,128)(2,1)}, u32[]{:S(2)}, u32[]{:S(2)}) collective-permute-start(bf16[68,16,128]{2,1,0:T(8,128)(2,1)S(1)} %collective-permute-done.10.refs_1_), channel_id=1, source_target_pairs={{0,4},{1,5},{2,6},{3,7},{4,0},{5,1},{6,2},{7,3},{8,12},{9,13},{10,... | collective-permute-start | bytes 835592 | tf_op jit(solution)/shard_map/ppermute | solution.py:280
  158.5 32.9 %collective-permute-start.16 = (bf16[68,16,128]{2,1,0:T(8,128)(2,1)S(1)}, bf16[68,16,128]{2,1,0:T(8,128)(2,1)}, u32[]{:S(2)}, u32[]{:S(2)}) collective-permute-start(bf16[68,16,128]{2,1,0:T(8,128)(2,1)S(1)} %collective-permute-done.10.refs_1_), channel_id=1, source_target_pairs={{0,6},{1,7},{2,0},{3,1},{4,2},{5,3},{6,4},{7,5},{8,14},{9,15},{10,... | collective-permute-start | bytes 835592 | tf_op jit(solution)/shard_map/ppermute | solution.py:280
  188.5 1.6 copy-start
  242.2 1.2 copy-start.4
  243.5 1.2 copy-start.5
  244.7 0.8 copy-start.7
  245.4 0.8 copy-start.9

commit v4 on v3

--- a/solution.py
+++ b/solution.py
@@ -48,13 +48,15 @@
     return high, mid, (rest - mid.astype(F32)).astype(BF16)
 
 
-def pack_kv(src_ref, k_ref, v_ref, out_ref):
+def pack_kv(src_ref, owner_ref, k_ref, v_ref, tile_ref, out_ref):
     here = out_ref.shape[0]
     first = pl.program_id(0) * here
     for i in range(here):
-        rows = pl.ds(pl.multiple_of(src_ref[first + i] * BLK, BLK), BLK)
-        out_ref[i, :, :HEAD_SIZE] = k_ref[rows, :]
-        out_ref[i, :, HEAD_SIZE:] = v_ref[rows, :]
+        for c in range(CAP):
+            rows = pl.ds(pl.multiple_of(src_ref[(first + i) * CAP + c] * BLK, BLK), BLK)
+            out_ref[i, 2 * c * BLK : (2 * c + 1) * BLK] = k_ref[rows, :]
+            out_ref[i, (2 * c + 1) * BLK : (2 * c + 2) * BLK] = v_ref[rows, :]
+        out_ref[i, 2 * CAP * BLK :] = tile_ref[owner_ref[0], CAP + GLOB]
 
 
 def project(x_ref, t_ref, out_ref):
@@ -67,7 +69,7 @@
                 out_ref[half * PARTS + part, b] = y[row : row + ROWS, half * 128 : half * 128 + 128]
 
 
-def sum_pack(src_ref, gid_ref, x_ref, own_ref, out_ref, acc):
+def sum_pack(src_ref, gid_ref, x_ref, k_ref, v_ref, own_ref, out_ref, acc):
     own = x_ref[0].astype(F32)
     for i in range(1, x_ref.shape[0]):
         own = own + x_ref[i].astype(F32)
@@ -78,22 +80,28 @@
             out_ref[i, c] = acc[src_ref[i * CAP + c]]
         for g in range(GLOB):
             out_ref[i, CAP + g] = acc[gid_ref[g]]
+        if i < 2 * GLOB * PARTS:
+            row = gid_ref[i // (2 * PARTS)] * BLK + i % PARTS * ROWS
+            ref = (k_ref, v_ref)[i // PARTS % 2]
+            out_ref[i, CAP + GLOB] = ref[pl.ds(pl.multiple_of(row, ROWS), ROWS), :]
+        else:
+            out_ref[i, CAP + GLOB] = jnp.zeros((ROWS, 128), BF16)
 
 
 def collect(arrival_ref, owner_ref, own_ref, before_ref, after_ref, recv_ref, out_ref):
     blocks = own_ref.shape[0]
     tiles = [before_ref[...]] + [own_ref[b] for b in range(blocks)] + [after_ref[...]]
-    tiles += [recv_ref[owner_ref[g] * (CAP + GLOB) + CAP + g] for g in range(GLOB)]
-    tiles += [recv_ref[arrival_ref[n] // CAP * (CAP + GLOB) + arrival_ref[n] % CAP] for n in range(blocks * RAND)]
+    tiles += [recv_ref[owner_ref[g], CAP + g] for g in range(GLOB)]
+    tiles += [recv_ref[arrival_ref[n] // CAP, arrival_ref[n] % CAP] for n in range(blocks * RAND)]
     for n, tile in enumerate(tiles):
         out_ref[n] = tile
 
 
 def attend(
-    arrival_ref, edge_ref, from_ref, q_ref, g_ref, k_ref, v_ref, before_ref, after_ref, glob_ref, recv_ref, *refs
+    arrival_ref, edge_ref, from_ref, q_ref, g_ref, k_ref, v_ref, before_ref, after_ref, recv_ref, *refs
 ):
-    dq_ref, out_ref, kwin, vwin, wacc, gacc, kg_ref, total = refs[-8:]
-    tile_refs = refs[:-10]
+    dq_ref, out_ref, kwin, vwin, kglob, vglob, wacc, gacc, kg_ref, total = refs[-10:]
+    tile_refs = refs[:-12]
     step, steps = pl.program_id(0), pl.num_programs(0)
     tokens = k_ref.shape[0]
     blocks = tokens // BLK
@@ -107,6 +115,11 @@
             win[:BLK] = before_ref[:, low : low + h]
             win[BLK : BLK + tokens] = ref[...]
             win[BLK + tokens :] = after_ref[:, low : low + h]
+        for kind, ref in enumerate((kglob, vglob)):
+            for g in range(GLOB):
+                for part in range(PARTS):
+                    tile = recv_ref[(2 * g + kind) * PARTS + part, 2 * CAP * BLK :]
+                    ref[g * BLK + part * ROWS : g * BLK + (part + 1) * ROWS] = tile
         wacc[...] = jnp.zeros_like(wacc)
         gacc[...] = jnp.zeros_like(gacc)
 
@@ -114,8 +127,11 @@
         b = step * unroll + u
         rows = pl.ds(pl.multiple_of(b * BLK, BLK), 3 * BLK)
         picks = [arrival_ref[b * RAND + r] for r in range(RAND)]
-        k_all = jnp.concatenate([kwin[rows, :]] + [recv_ref[p, :, :h] for p in picks] + [glob_ref[:, :h]], axis=0)
-        v_all = jnp.concatenate([vwin[rows, :]] + [recv_ref[p, :, h:] for p in picks] + [glob_ref[:, h:]], axis=0)
+        at = [(p // CAP, pl.multiple_of(p % CAP * (2 * BLK), BLK)) for p in picks]
+        k_all = jnp.concatenate([kwin[rows, :]] + [recv_ref[o, pl.ds(i, BLK), :] for o, i in at] + [kglob[...]], axis=0)
+        v_all = jnp.concatenate(
+            [vwin[rows, :]] + [recv_ref[o, pl.ds(i + BLK, BLK), :] for o, i in at] + [vglob[...]], axis=0
+        )
         here = slice(u * BLK, (u + 1) * BLK)
         q = jnp.concatenate([q_ref[here, j * h : (j + 1) * h] for j in range(GROUP)], axis=0)
         g = jnp.concatenate([g_ref[here, j * h : (j + 1) * h] for j in range(GROUP)], axis=0)
@@ -221,66 +237,49 @@
     terms = lax.all_to_all(terms, "head", 0, 0, tiled=True)
     own, p_out = pl.pallas_call(
         sum_pack,
-        in_specs=[SMEM, SMEM, VMEM],
+        in_specs=[SMEM, SMEM] + [VMEM] * 3,
         out_specs=[VMEM] * 2,
         out_shape=[
             jax.ShapeDtypeStruct((blocks, ROWS, 128), BF16),
-            jax.ShapeDtypeStruct((ctx, CAP + GLOB, ROWS, 128), BF16),
+            jax.ShapeDtypeStruct((ctx, CAP + GLOB + 1, ROWS, 128), BF16),
         ],
         scratch_shapes=[pltpu.VMEM((blocks, ROWS, 128), BF16)],
         compiler_params=PARAMS,
-    )(sources, global_inner, terms)
+    )(sources, global_inner, terms, keys, values)
 
     kv_before = lax.ppermute(jnp.concatenate([keys[-BLK:], values[-BLK:]], axis=1), "ctx", up)
     kv_after = lax.ppermute(jnp.concatenate([keys[:BLK], values[:BLK]], axis=1), "ctx", down)
-    kv_glob = []
-    for g in range(GLOB):
-        row = global_inner[g] * BLK
-        kv_glob.append(jnp.concatenate([lax.dynamic_slice_in_dim(x, row, BLK, 0) for x in (keys, values)], axis=1))
-    kv_glob = jnp.stack(kv_glob)
-    apart = my_ctx ^ global_owner
-    bit = 1
-    while bit < ctx:
-        other = lax.ppermute(kv_glob, "ctx", [(i, i ^ bit) for i in range(ctx)])
-        kv_glob = jnp.where(((apart & bit) != 0)[:, None, None], other, kv_glob)
-        bit *= 2
-    kv_glob = kv_glob.reshape(GLOB * BLK, 2 * h)
-
-    p_out, kv_glob, kv_before, kv_after = lax.optimization_barrier((p_out, kv_glob, kv_before, kv_after))
     p_in = lax.all_to_all(p_out, "ctx", 0, 0, tiled=True)
     p_before = lax.ppermute(own[-1], "ctx", up)
     p_after = lax.ppermute(own[0], "ctx", down)
+
+    chunk = 8
+    tile_owner = global_owner[jnp.minimum(my_ctx // (2 * PARTS), GLOB - 1)]
+    span = 2 * CAP * BLK + ROWS
+    kv_out = pl.pallas_call(
+        pack_kv,
+        grid_spec=pltpu.PrefetchScalarGridSpec(
+            num_scalar_prefetch=2,
+            grid=(ctx // chunk,),
+            in_specs=[VMEM] * 3,
+            out_specs=pl.BlockSpec((chunk, span, h), lambda i, s, o: (i, 0, 0)),
+        ),
+        out_shape=pltpu.HBM((ctx, span, h), BF16),
+        compiler_params=PARAMS,
+    )(sources, tile_owner.reshape(1), keys, values, p_in)
+    kv_out, kv_before, kv_after, p_before, p_after = lax.optimization_barrier(
+        (kv_out, kv_before, kv_after, p_before, p_after)
+    )
+    kv_in = lax.all_to_all(kv_out, "ctx", 0, 0, tiled=True)
+
     tiles = pl.pallas_call(
         collect,
         in_specs=[SMEM, SMEM] + [VMEM] * 4,
         out_specs=VMEM,
         out_shape=jax.ShapeDtypeStruct((places, ROWS, 128), BF16),
         compiler_params=PARAMS,
-    )(arrival, global_owner, own, p_before, p_after, p_in.reshape(ctx * (CAP + GLOB), ROWS, 128))
+    )(arrival, global_owner, own, p_before, p_after, p_in)
     pair = [tiles, lax.ppermute(tiles, "head", [(i, i ^ 1) for i in range(heads)])]
-    chunk = 16
-    kv_out = pl.pallas_call(
-        pack_kv,
-        grid_spec=pltpu.PrefetchScalarGridSpec(
-            num_scalar_prefetch=1,
-            grid=(ctx * CAP // chunk,),
-            in_specs=[VMEM, VMEM],
-            out_specs=pl.BlockSpec((chunk, BLK, 2 * h), lambda i, s: (i, 0, 0)),
-        ),
-        out_shape=pltpu.HBM((ctx * CAP, BLK, 2 * h), BF16),
-        compiler_params=PARAMS,
-    )(sources, keys, values)
-    kv_out, pair[1], kv_before, kv_after, kv_glob = lax.optimization_barrier((kv_out, pair[1], kv_before, kv_after, kv_glob))
-    kv_in = lax.all_to_all(kv_out.reshape(ctx, CAP, BLK, 2 * h), "ctx", 0, 0, tiled=True)
-    kv_in = kv_in.reshape(ctx * CAP, BLK, 2 * h)
-
-    all_tiles, all_heads = list(pair), [my_head, my_head ^ 1]
-    for far in range(2, heads, 2):
-        there = [(i, (i + far) % heads) for i in range(heads)]
-        all_tiles += [lax.ppermute(t, "head", there) for t in pair]
-        source = (my_head - far) % heads
-        all_heads += [source, source ^ 1]
-
     every = jnp.arange(D, dtype=jnp.int32)
     table_new = proj_table(step_codes[1], rank_ids, every)
     table_old = proj_table(step_codes[0], rank_ids, every)
@@ -293,13 +292,21 @@
         compiler_params=PARAMS,
     )(jnp.pad(momentum[0], ((0, 8 - share), (0, 0))), table_old, table_new)
 
+    pair[1], carried = lax.optimization_barrier((pair[1], carried))
+    all_tiles, all_heads = list(pair), [my_head, my_head ^ 1]
+    for far in range(2, heads, 2):
+        there = [(i, (i + far) % heads) for i in range(heads)]
+        all_tiles += [lax.ppermute(t, "head", there) for t in pair]
+        source = (my_head - far) % heads
+        all_heads += [source, source ^ 1]
+
     edges = jnp.stack([my_ctx == 0, my_ctx == ctx - 1]).astype(jnp.int32)
     unroll = 2
     wide = pl.BlockSpec((unroll * BLK, GROUP * h), lambda i: (i, 0))
     dq, grad = pl.pallas_call(
         attend,
         grid=(blocks // unroll,),
-        in_specs=[SMEM] * 3 + [wide] * 2 + [VMEM] * (6 + heads) + [ANY] * 2,
+        in_specs=[SMEM] * 3 + [wide] * 2 + [VMEM] * (5 + heads) + [ANY] * 2,
         out_specs=[wide, VMEM],
         out_shape=[
             jax.ShapeDtypeStruct((tokens, GROUP * h), BF16),
@@ -308,6 +315,8 @@
         scratch_shapes=[
             pltpu.VMEM((tokens + 2 * BLK, h), BF16),
             pltpu.VMEM((tokens + 2 * BLK, h), BF16),
+            pltpu.VMEM((GLOB * BLK, h), BF16),
+            pltpu.VMEM((GLOB * BLK, h), BF16),
             pltpu.VMEM((tokens + 2 * BLK, 2 * h), F32),
             pltpu.VMEM((GLOB * BLK, 2 * h), F32),
             pltpu.VMEM((PARTS, places, ROWS, 2 * h), BF16),
@@ -315,7 +324,7 @@
         ],
         compiler_params=LARGE,
     )(
-        arrival, edges, jnp.stack(all_heads), queries, d_attn, keys, values, kv_before, kv_after, kv_glob, kv_in,
+        arrival, edges, jnp.stack(all_heads), queries, d_attn, keys, values, kv_before, kv_after, kv_in,
         *all_tiles, table_new, carried,
     )
     grad = lax.all_to_all(grad, "ctx", 0, 0, tiled=True)

time: 296 us -> 268 us (0.905)
  starting transfers between devices: 98.2 us -> 64 us
  waiting for transfers between devices: 93.6 us -> 104 us
    ppermute x1, waiting for transfers between devices: 2.9 us -> 58.6 us  [local(): lax.ppermute(tiles, 'head', [(i, i ^ 1) for i in range(heads)])]
    all_to_all x1, waiting for transfers between devices: 50.8 us -> 0.01 us  [local(): kv_in = lax.all_to_all(kv_out, 'ctx', 0, 0, tiled=True)]
    ppermute x6 -> x0, starting transfers between devices: 33.3 us -> none  [local(): other = lax.ppermute(kv_glob, 'ctx', [(i, i ^ bit) for i in range(ctx)])]
    ppermute x6 -> x0, waiting for transfers between devices: 17.5 us -> none  [local(): other = lax.ppermute(kv_glob, 'ctx', [(i, i ^ bit) for i in range(ctx)])]
    all_to_all x1, waiting for transfers between devices: 0.01 us -> 12.7 us  [local(): terms = lax.all_to_all(terms, 'head', 0, 0, tiled=True)]
    ppermute x1, waiting for transfers between devices: 10.6 us -> 0.01 us  [local(): p_before = lax.ppermute(own[-1], 'ctx', up)]
    all_to_all x1, waiting for transfers between devices: 11.7 us -> 22.2 us  [local(): p_in = lax.all_to_all(p_out, 'ctx', 0, 0, tiled=True)]
    ppermute x6, waiting for transfers between devices: 0.02 us -> 10.3 us  [local(): all_tiles += [lax.ppermute(t, 'head', there) for t in pair]]
  transfers between devices with their start and end apart: 20 -> 14, of which waited for: 8 -> 6; matrix products, arithmetic and copies ran while one was open for 11% -> 11% of each run, Pallas kernels for 3% -> 3%
where the time goes in v4:
time: 268 us; the launch traced here: 267 us
  waiting for transfers between devices  104 us (39%)
  starting transfers between devices  64 us (24%)
  blocking collectives  30.3 us (11%)
  other arithmetic  29.5 us (11%)
  Pallas kernels  28.9 us (11%)
  local copies, waits for them, and re-layouts  8.56 us (3%)
    ppermute x1, waiting for transfers between devices, local(): lax.ppermute(tiles, 'head', [(i, i ^ 1) for i in range(heads)])  58.6 us
    all_to_all x1, blocking collectives, local(): grad = lax.all_to_all(grad, 'ctx', 0, 0, tiled=True)  30.3 us
    convert_element_type x2, other arithmetic, proj_table(): return (unit_value * math.sqrt(12.0 / D)).astype(jnp.bfloat16)  27.4 us
    all_to_all x1, waiting for transfers between devices, local(): p_in = lax.all_to_all(p_out, 'ctx', 0, 0, tiled=True)  22.2 us
    pallas_call x1, Pallas kernels, local(): pl.pallas_call(attend, grid=(blocks // unroll,), in_specs=[SMEM] * 3 + [w...  17.8 us
    ppermute x6, starting transfers between devices, local(): all_tiles += [lax.ppermute(t, 'head', there) for t in pair]  17.3 us
    all_to_all x1, starting transfers between devices, local(): p_in = lax.all_to_all(p_out, 'ctx', 0, 0, tiled=True)  16.7 us
    all_to_all x1, waiting for transfers between devices, local(): terms = lax.all_to_all(terms, 'head', 0, 0, tiled=True)  12.7 us
  transfers between devices with their start and end apart: 14, of which 6 were waited for; matrix products, arithmetic and copies ran while one was open for 11% of the time, Pallas kernels for 3%

profile of v4, /device:TPU:1, one launch (start us, length us, event | category | flops | bytes accessed | tf_op | source)
XLA Modules:
  0.0 267.5 jit_solution(1013807387782617229)
XLA Ops:
  0.7 1.3 fusion.78
  2.6 1.8 fusion.59.t_ref
  4.5 1.2 copy-done.4
  5.7 1.3 shard_map.112
  7.0 10.1 %all-to-all-start = ((bf16[8,16,16,128]{3,2,1,0:T(8,128)(2,1)}), bf16[8,16,16,128]{3,2,1,0:T(8,128)(2,1)S(1)}, u32[]{:S(2)}, u32[]{:S(2)}) async-start(bf16[8,16,16,128]{3,2,1,0:T(8,128)(2,1)} %shard_map.112), calls=%async_computation | async-start | bytes 1048576 | tf_op jit(solution)/shard_map/all_to_all | solution.py:237
  19.3 12.7 %all-to-all-done.x_ref = bf16[8,16,16,128]{3,2,1,0:T(8,128)(2,1)S(1)} async-done(((bf16[8,16,16,128]{3,2,1,0:T(8,128)(2,1)}), bf16[8,16,16,128]{3,2,1,0:T(8,128)(2,1)S(1)}, u32[]{:S(2)}, u32[]{:S(2)}) %all-to-all-start) | async-done | bytes 524320 | tf_op jit(solution)/shard_map/all_to_all | solution.py:237
  34.0 1.8 shard_map.113
  35.8 16.7 %all-to-all-start.1 = ((bf16[64,5,16,128]{3,2,1,0:T(8,128)(2,1)}), bf16[64,5,16,128]{3,2,1,0:T(8,128)(2,1)S(1)}, u32[]{:S(2)}, u32[]{:S(2)}) async-start(bf16[64,5,16,128]{3,2,1,0:T(8,128)(2,1)} %get-tuple-element.16), calls=%async_computation.1 | async-start | bytes 2621440 | tf_op jit(solution)/shard_map/all_to_all | solution.py:252
  52.6 3.5 %collective-permute-start = (bf16[64,256]{1,0:T(8,128)(2,1)S(1)}, bf16[64,256]{1,0:T(8,128)(2,1)S(1)}, u32[]{:S(2)}, u32[]{:S(2)}) collective-permute-start(bf16[64,256]{1,0:T(8,128)(2,1)S(1)} %pad_maximum_fusion), channel_id=1, source_target_pairs={{0,8},{8,16},{16,24},{24,32},{32,40},{40,48},{48,56},{56,64},{64,7... | collective-permute-start | bytes 98312 | tf_op jit(solution)/shard_map/ppermute | solution.py:250
  56.1 1.9 collective-permute-start.1
  58.1 3.6 %collective-permute-start.2 = (bf16[16,128]{1,0:T(8,128)(2,1)S(1)}, bf16[16,128]{1,0:T(8,128)(2,1)S(1)}, u32[]{:S(2)}, u32[]{:S(2)}) collective-permute-start(bf16[16,128]{1,0:T(8,128)(2,1)S(1)} %get-tuple-element.36), channel_id=1, source_target_pairs={{0,8},{8,16},{16,24},{24,32},{32,40},{40,48},{48,56},{56,64},{64,7... | collective-permute-start | bytes 12296 | tf_op jit(solution)/shard_map/ppermute | solution.py:253
  61.7 1.9 collective-permute-start.3
  64.2 22.2 %all-to-all-done.1.tile_ref.recv_ref = bf16[64,5,16,128]{3,2,1,0:T(8,128)(2,1)S(1)} async-done(((bf16[64,5,16,128]{3,2,1,0:T(8,128)(2,1)}), bf16[64,5,16,128]{3,2,1,0:T(8,128)(2,1)S(1)}, u32[]{:S(2)}, u32[]{:S(2)}) %all-to-all-start.1) | async-done | bytes 1310752 | tf_op jit(solution)/shard_map/all_to_all | solution.py:252
  86.4 4.9 %shard_map.114 = bf16[64,272,128]{2,1,0:T(8,128)(2,1)} custom-call(s32[128]{0:T(128)S(1)} %reshape.129.src_ref, s32[1]{0:T(128)} %dynamic_slice.8.owner_ref, bf16[1024,128]{1,0:T(8,128)(2,1)S(1)} %copy-done.1, bf16[1024,128]{1,0:T(8,128)(2,1)S(1)} %copy-done.3, bf16[64,5,16,128]{3,2,1,0:T(8,128)(2,1)S(1)} %all-to-all-done.1.tile_ref.recv_ref), custom_call_target="tpu_custom_call" | custom-call | tf_op jit(solution)/shard_map/pallas_call | solution.py:259
  91.3 7.0 %all-to-all-start.2 = ((bf16[64,272,128]{2,1,0:T(8,128)(2,1)}), bf16[64,272,128]{2,1,0:T(8,128)(2,1)}, u32[]{:S(2)}, u32[]{:S(2)}) async-start(bf16[64,272,128]{2,1,0:T(8,128)(2,1)} %shard_map.114), calls=%async_computation.2 | async-start | bytes 8912896 | tf_op jit(solution)/shard_map/all_to_all | solution.py:273
  100.6 1.9 collective-permute-start.4
  102.6 2.1 collective-permute-start.5
  104.7 25.6 %fusion.41 = (bf16[256,4096]{1,0:T(8,128)(2,1)S(1)}, bf16[256,4096]{1,0:T(8,128)(2,1)S(1)}) fusion(s32[]{:T(128)} %bitcast.13, s32[256]{0:T(256)S(1)} %get-tuple-element.47, s32[4096]{0:T(1024)S(1)} %iota_multiply_fusion, s32[256]{0:T(256)S(1)} %get-tuple-element.48, s32[]{:T(128)} %bitcast.17), kind=kLoop, calls=%fused_computation.53 | loop fusion | flops 93323264 | bytes 4212744 | tf_op jit(solution)/shard_map/convert_element_type | solution.py:37
  131.4 3.7 %collective-permute-start.7 = (bf16[68,16,128]{2,1,0:T(8,128)(2,1)S(1)}, bf16[68,16,128]{2,1,0:T(8,128)(2,1)}, u32[]{:S(2)}, u32[]{:S(2)}) collective-permute-start(bf16[68,16,128]{2,1,0:T(8,128)(2,1)S(1)} %shard_map.115.refs_0_), channel_id=1, source_target_pairs={{0,4},{1,5},{2,6},{3,7},{4,0},{5,1},{6,2},{7,3},{8,12},{9,13},{10,... | collective-permute-start | bytes 835592 | tf_op jit(solution)/shard_map/ppermute | solution.py:299
  135.1 2.9 %collective-permute-start.9 = (bf16[68,16,128]{2,1,0:T(8,128)(2,1)S(1)}, bf16[68,16,128]{2,1,0:T(8,128)(2,1)}, u32[]{:S(2)}, u32[]{:S(2)}) collective-permute-start(bf16[68,16,128]{2,1,0:T(8,128)(2,1)S(1)} %shard_map.115.refs_0_), channel_id=1, source_target_pairs={{0,6},{1,7},{2,0},{3,1},{4,2},{5,3},{6,4},{7,5},{8,14},{9,15},{10,... | collective-permute-start | bytes 835592 | tf_op jit(solution)/shard_map/ppermute | solution.py:299
  138.0 58.6 %collective-permute-done.4.refs_1_ = bf16[68,16,128]{2,1,0:T(8,128)(2,1)S(1)} collective-permute-done((bf16[68,16,128]{2,1,0:T(8,128)(2,1)S(1)}, bf16[68,16,128]{2,1,0:T(8,128)(2,1)S(1)}, u32[]{:S(2)}, u32[]{:S(2)}) %collective-permute-start.4) | collective-permute-done | bytes 278560 | tf_op jit(solution)/shard_map/ppermute | solution.py:282
  196.6 1.9 collective-permute-start.6
  198.5 3.7 %collective-permute-start.8 = (bf16[68,16,128]{2,1,0:T(8,128)(2,1)S(1)}, bf16[68,16,128]{2,1,0:T(8,128)(2,1)}, u32[]{:S(2)}, u32[]{:S(2)}) collective-permute-start(bf16[68,16,128]{2,1,0:T(8,128)(2,1)S(1)} %collective-permute-done.4.refs_1_), channel_id=1, source_target_pairs={{0,4},{1,5},{2,6},{3,7},{4,0},{5,1},{6,2},{7,3},{8,12},{9,13},{10,... | collective-permute-start | bytes 835592 | tf_op jit(solution)/shard_map/ppermute | solution.py:299
  202.2 3.0 %collective-permute-start.10 = (bf16[68,16,128]{2,1,0:T(8,128)(2,1)S(1)}, bf16[68,16,128]{2,1,0:T(8,128)(2,1)}, u32[]{:S(2)}, u32[]{:S(2)}) collective-permute-start(bf16[68,16,128]{2,1,0:T(8,128)(2,1)S(1)} %collective-permute-done.4.refs_1_), channel_id=1, source_target_pairs={{0,6},{1,7},{2,0},{3,1},{4,2},{5,3},{6,4},{7,5},{8,14},{9,15},{10,... | collective-permute-start | bytes 835592 | tf_op jit(solution)/shard_map/ppermute | solution.py:299
  205.5 2.4 collective-permute-done.6.refs_3_
  207.9 4.2 %collective-permute-done.8.refs_5_ = bf16[68,16,128]{2,1,0:T(8,128)(2,1)} collective-permute-done((bf16[68,16,128]{2,1,0:T(8,128)(2,1)S(1)}, bf16[68,16,128]{2,1,0:T(8,128)(2,1)}, u32[]{:S(2)}, u32[]{:S(2)}) %collective-permute-start.8) | collective-permute-done | bytes 278560 | tf_op jit(solution)/shard_map/ppermute | solution.py:299
  212.1 3.6 %collective-permute-done.10.refs_7_ = bf16[68,16,128]{2,1,0:T(8,128)(2,1)} collective-permute-done((bf16[68,16,128]{2,1,0:T(8,128)(2,1)S(1)}, bf16[68,16,128]{2,1,0:T(8,128)(2,1)}, u32[]{:S(2)}, u32[]{:S(2)}) %collective-permute-start.10) | collective-permute-done | bytes 278560 | tf_op jit(solution)/shard_map/ppermute | solution.py:299
  215.7 1.2 copy-done.5
  217.0 1.2 copy-done.6
  218.2 17.8 %shard_map.117 = (bf16[1024,512]{1,0:T(8,128)(2,1)}, f32[64,8,128]{2,1,0:T(8,128)}) custom-call(s32[48]{0:T(128)S(1)} %convert_add_fusion.arrival_ref, s32[2]{0:T(128)S(1)} %add_convert_fusion.edge_ref, s32[8]{0:T(128)S(1)} %stack.52.from_ref, bf16[1024,512]{1,0:T(8,128)(2,1)S(1)} %copy-done.5, bf16[1024,512]{1,0:T(8,128)(2,1)S(1)} %copy-done.6, ...), custom_call_target="tpu_custom_call" | custom-call | tf_op jit(solution)/shard_map/pallas_call | solution.py:306
  236.0 30.3 %all_to_all.20.recv_ref = f32[64,8,128]{2,1,0:T(8,128)S(1)} all-to-all(f32[64,8,128]{2,1,0:T(8,128)} %get-tuple-element.26), channel_id=1, replica_groups=mesh['ctx'=64,'head'=8] {'ctx'}, dimensions={0} | all-to-all | bytes 524288 | tf_op jit(solution)/shard_map/all_to_all | solution.py:330
  266.3 1.2 shard_map.118
  (56 shorter events, 7.6 us)
Async XLA Ops:
  0.6 51.9 %copy-start.1 = (bf16[1024,128]{1,0:T(8,128)(2,1)S(1)}, bf16[1024,128]{1,0:T(8,128)(2,1)}, u32[]{:S(2)}) copy-start(bf16[1024,128]{1,0:T(8,128)(2,1)} %k_ref.5) | copy-start | bytes 786436
  0.6 51.9 %copy-start.3 = (bf16[1024,128]{1,0:T(8,128)(2,1)S(1)}, bf16[1024,128]{1,0:T(8,128)(2,1)}, u32[]{:S(2)}) copy-start(bf16[1024,128]{1,0:T(8,128)(2,1)} %v_ref.5) | copy-start | bytes 786436
  4.5 1.2 copy-start.4
  7.0 25.1 %all-to-all-start = ((bf16[8,16,16,128]{3,2,1,0:T(8,128)(2,1)}), bf16[8,16,16,128]{3,2,1,0:T(8,128)(2,1)S(1)}, u32[]{:S(2)}, u32[]{:S(2)}) async-start(bf16[8,16,16,128]{3,2,1,0:T(8,128)(2,1)} %shard_map.112), calls=%async_computation | async-start | bytes 1048576 | tf_op jit(solution)/shard_map/all_to_all | solution.py:237
  32.1 1.0 copy-start
  33.0 0.9 copy-start.2
  35.8 50.6 %all-to-all-start.1 = ((bf16[64,5,16,128]{3,2,1,0:T(8,128)(2,1)}), bf16[64,5,16,128]{3,2,1,0:T(8,128)(2,1)S(1)}, u32[]{:S(2)}, u32[]{:S(2)}) async-start(bf16[64,5,16,128]{3,2,1,0:T(8,128)(2,1)} %get-tuple-element.16), calls=%async_computation.1 | async-start | bytes 2621440 | tf_op jit(solution)/shard_map/all_to_all | solution.py:252
  52.6 38.7 %collective-permute-start = (bf16[64,256]{1,0:T(8,128)(2,1)S(1)}, bf16[64,256]{1,0:T(8,128)(2,1)S(1)}, u32[]{:S(2)}, u32[]{:S(2)}) collective-permute-start(bf16[64,256]{1,0:T(8,128)(2,1)S(1)} %pad_maximum_fusion), channel_id=1, source_target_pairs={{0,8},{8,16},{16,24},{24,32},{32,40},{40,48},{48,56},{56,64},{64,7... | collective-permute-start | bytes 98312 | tf_op jit(solution)/shard_map/ppermute | solution.py:250
  56.1 35.2 %collective-permute-start.1 = (bf16[64,256]{1,0:T(8,128)(2,1)S(1)}, bf16[64,256]{1,0:T(8,128)(2,1)S(1)}, u32[]{:S(2)}, u32[]{:S(2)}) collective-permute-start(bf16[64,256]{1,0:T(8,128)(2,1)S(1)} %pad_maximum_fusion.1), channel_id=1, source_target_pairs={{8,0},{16,8},{24,16},{32,24},{40,32},{48,40},{56,48},{64,56},{72,6... | collective-permute-start | bytes 98312 | tf_op jit(solution)/shard_map/ppermute | solution.py:251
  58.1 33.3 %collective-permute-start.2 = (bf16[16,128]{1,0:T(8,128)(2,1)S(1)}, bf16[16,128]{1,0:T(8,128)(2,1)S(1)}, u32[]{:S(2)}, u32[]{:S(2)}) collective-permute-start(bf16[16,128]{1,0:T(8,128)(2,1)S(1)} %get-tuple-element.36), channel_id=1, source_target_pairs={{0,8},{8,16},{16,24},{24,32},{32,40},{40,48},{48,56},{56,64},{64,7... | collective-permute-start | bytes 12296 | tf_op jit(solution)/shard_map/ppermute | solution.py:253
  61.7 29.6 %collective-permute-start.3 = (bf16[16,128]{1,0:T(8,128)(2,1)S(1)}, bf16[16,128]{1,0:T(8,128)(2,1)S(1)}, u32[]{:S(2)}, u32[]{:S(2)}) collective-permute-start(bf16[16,128]{1,0:T(8,128)(2,1)S(1)} %get-tuple-element.35), channel_id=1, source_target_pairs={{8,0},{16,8},{24,16},{32,24},{40,32},{48,40},{56,48},{64,56},{72,6... | collective-permute-start | bytes 12296 | tf_op jit(solution)/shard_map/ppermute | solution.py:254
  91.3 7.1 %copy-start.7 = (s32[1024,3]{0,1:T(4,128)S(1)}, s32[1024,3]{0,1:T(4,128)}, u32[]{:S(2)}) copy-start(s32[1024,3]{0,1:T(4,128)} %param.14) | copy-start | bytes 36868
  91.3 124.4 %all-to-all-start.2 = ((bf16[64,272,128]{2,1,0:T(8,128)(2,1)}), bf16[64,272,128]{2,1,0:T(8,128)(2,1)}, u32[]{:S(2)}, u32[]{:S(2)}) async-start(bf16[64,272,128]{2,1,0:T(8,128)(2,1)} %shard_map.114), calls=%async_computation.2 | async-start | bytes 8912896 | tf_op jit(solution)/shard_map/all_to_all | solution.py:273
  98.4 31.9 %copy-start.8 = (f32[1,4,256]{2,1,0:T(4,128)S(1)}, f32[1,4,256]{2,1,0:T(4,128)}, u32[]{:S(2)}) copy-start(f32[1,4,256]{2,1,0:T(4,128)} %param.17) | copy-start | bytes 12292
  100.6 96.0 %collective-permute-start.4 = (bf16[68,16,128]{2,1,0:T(8,128)(2,1)S(1)}, bf16[68,16,128]{2,1,0:T(8,128)(2,1)S(1)}, u32[]{:S(2)}, u32[]{:S(2)}) collective-permute-start(bf16[68,16,128]{2,1,0:T(8,128)(2,1)S(1)} %shard_map.115.refs_0_), channel_id=1, source_target_pairs={{0,1},{1,0},{2,3},{3,2},{4,5},{5,4},{6,7},{7,6},{8,9},{9,8},{10,11... | collective-permute-start | bytes 835592 | tf_op jit(solution)/shard_map/ppermute | solution.py:282
  102.6 99.7 %collective-permute-start.5 = (bf16[68,16,128]{2,1,0:T(8,128)(2,1)S(1)}, bf16[68,16,128]{2,1,0:T(8,128)(2,1)S(1)}, u32[]{:S(2)}, u32[]{:S(2)}) collective-permute-start(bf16[68,16,128]{2,1,0:T(8,128)(2,1)S(1)} %shard_map.115.refs_0_), channel_id=1, source_target_pairs={{0,2},{1,3},{2,4},{3,5},{4,6},{5,7},{6,0},{7,1},{8,10},{9,11},{10,... | collective-permute-start | bytes 835592 | tf_op jit(solution)/shard_map/ppermute | solution.py:299
  131.4 74.0 %collective-permute-start.7 = (bf16[68,16,128]{2,1,0:T(8,128)(2,1)S(1)}, bf16[68,16,128]{2,1,0:T(8,128)(2,1)}, u32[]{:S(2)}, u32[]{:S(2)}) collective-permute-start(bf16[68,16,128]{2,1,0:T(8,128)(2,1)S(1)} %shard_map.115.refs_0_), channel_id=1, source_target_pairs={{0,4},{1,5},{2,6},{3,7},{4,0},{5,1},{6,2},{7,3},{8,12},{9,13},{10,... | collective-permute-start | bytes 835592 | tf_op jit(solution)/shard_map/ppermute | solution.py:299
  135.1 70.3 %collective-permute-start.9 = (bf16[68,16,128]{2,1,0:T(8,128)(2,1)S(1)}, bf16[68,16,128]{2,1,0:T(8,128)(2,1)}, u32[]{:S(2)}, u32[]{:S(2)}) collective-permute-start(bf16[68,16,128]{2,1,0:T(8,128)(2,1)S(1)} %shard_map.115.refs_0_), channel_id=1, source_target_pairs={{0,6},{1,7},{2,0},{3,1},{4,2},{5,3},{6,4},{7,5},{8,14},{9,15},{10,... | collective-permute-start | bytes 835592 | tf_op jit(solution)/shard_map/ppermute | solution.py:299
  196.6 11.3 %collective-permute-start.6 = (bf16[68,16,128]{2,1,0:T(8,128)(2,1)S(1)}, bf16[68,16,128]{2,1,0:T(8,128)(2,1)}, u32[]{:S(2)}, u32[]{:S(2)}) collective-permute-start(bf16[68,16,128]{2,1,0:T(8,128)(2,1)S(1)} %collective-permute-done.4.refs_1_), channel_id=1, source_target_pairs={{0,2},{1,3},{2,4},{3,5},{4,6},{5,7},{6,0},{7,1},{8,10},{9,11},{10,... | collective-permute-start | bytes 835592 | tf_op jit(solution)/shard_map/ppermute | solution.py:299
  198.5 13.6 %collective-permute-start.8 = (bf16[68,16,128]{2,1,0:T(8,128)(2,1)S(1)}, bf16[68,16,128]{2,1,0:T(8,128)(2,1)}, u32[]{:S(2)}, u32[]{:S(2)}) collective-permute-start(bf16[68,16,128]{2,1,0:T(8,128)(2,1)S(1)} %collective-permute-done.4.refs_1_), channel_id=1, source_target_pairs={{0,4},{1,5},{2,6},{3,7},{4,0},{5,1},{6,2},{7,3},{8,12},{9,13},{10,... | collective-permute-start | bytes 835592 | tf_op jit(solution)/shard_map/ppermute | solution.py:299
  202.2 13.5 %collective-permute-start.10 = (bf16[68,16,128]{2,1,0:T(8,128)(2,1)S(1)}, bf16[68,16,128]{2,1,0:T(8,128)(2,1)}, u32[]{:S(2)}, u32[]{:S(2)}) collective-permute-start(bf16[68,16,128]{2,1,0:T(8,128)(2,1)S(1)} %collective-permute-done.4.refs_1_), channel_id=1, source_target_pairs={{0,6},{1,7},{2,0},{3,1},{4,2},{5,3},{6,4},{7,5},{8,14},{9,15},{10,... | collective-permute-start | bytes 835592 | tf_op jit(solution)/shard_map/ppermute | solution.py:299
  215.7 1.2 copy-start.5
  217.0 1.2 copy-start.6

commit v5 on v4

--- a/solution.py
+++ b/solution.py
@@ -48,7 +48,7 @@
     return high, mid, (rest - mid.astype(F32)).astype(BF16)
 
 
-def pack_kv(src_ref, owner_ref, k_ref, v_ref, tile_ref, out_ref):
+def pack_kv(src_ref, k_ref, v_ref, out_ref):
     here = out_ref.shape[0]
     first = pl.program_id(0) * here
     for i in range(here):
@@ -56,7 +56,15 @@
             rows = pl.ds(pl.multiple_of(src_ref[(first + i) * CAP + c] * BLK, BLK), BLK)
             out_ref[i, 2 * c * BLK : (2 * c + 1) * BLK] = k_ref[rows, :]
             out_ref[i, (2 * c + 1) * BLK : (2 * c + 2) * BLK] = v_ref[rows, :]
-        out_ref[i, 2 * CAP * BLK :] = tile_ref[owner_ref[0], CAP + GLOB]
+
+
+def add_tile(owner_ref, packed_ref, tile_ref, out_ref, wide, sem):
+    tile = tile_ref[owner_ref[0], CAP + 1]
+    for i in range(wide.shape[0]):
+        wide[i] = tile
+    copy = pltpu.make_async_copy(wide, out_ref.at[:, pl.ds(2 * CAP * BLK, ROWS), :], sem)
+    copy.start()
+    copy.wait()
 
 
 def project(x_ref, t_ref, out_ref):
@@ -78,20 +86,19 @@
     for i in range(out_ref.shape[0]):
         for c in range(CAP):
             out_ref[i, c] = acc[src_ref[i * CAP + c]]
-        for g in range(GLOB):
-            out_ref[i, CAP + g] = acc[gid_ref[g]]
+        out_ref[i, CAP] = acc[gid_ref[i % GLOB]]
         if i < 2 * GLOB * PARTS:
             row = gid_ref[i // (2 * PARTS)] * BLK + i % PARTS * ROWS
             ref = (k_ref, v_ref)[i // PARTS % 2]
-            out_ref[i, CAP + GLOB] = ref[pl.ds(pl.multiple_of(row, ROWS), ROWS), :]
+            out_ref[i, CAP + 1] = ref[pl.ds(pl.multiple_of(row, ROWS), ROWS), :]
         else:
-            out_ref[i, CAP + GLOB] = jnp.zeros((ROWS, 128), BF16)
-
-
-def collect(arrival_ref, owner_ref, own_ref, before_ref, after_ref, recv_ref, out_ref):
+            out_ref[i, CAP + 1] = jnp.zeros((ROWS, 128), BF16)
+
+
+def collect(arrival_ref, core_ref, own_ref, before_ref, after_ref, here_ref, there_ref, recv_ref, out_ref):
     blocks = own_ref.shape[0]
     tiles = [before_ref[...]] + [own_ref[b] for b in range(blocks)] + [after_ref[...]]
-    tiles += [recv_ref[owner_ref[g], CAP + g] for g in range(GLOB)]
+    tiles += [jnp.where(core_ref[0] == g, here_ref[...], there_ref[...]) for g in range(GLOB)]
     tiles += [recv_ref[arrival_ref[n] // CAP, arrival_ref[n] % CAP] for n in range(blocks * RAND)]
     for n, tile in enumerate(tiles):
         out_ref[n] = tile
@@ -235,13 +242,28 @@
         compiler_params=PARAMS,
     )(inputs, table_part)
     terms = lax.all_to_all(terms, "head", 0, 0, tiled=True)
+
+    chunk = 8
+    span = 2 * CAP * BLK + ROWS
+    kv_out = pl.pallas_call(
+        pack_kv,
+        grid_spec=pltpu.PrefetchScalarGridSpec(
+            num_scalar_prefetch=1,
+            grid=(ctx // chunk,),
+            in_specs=[VMEM] * 2,
+            out_specs=pl.BlockSpec((chunk, 2 * CAP * BLK, h), lambda i, s: (i, 0, 0)),
+        ),
+        out_shape=pltpu.HBM((ctx, span, h), BF16),
+        compiler_params=PARAMS,
+    )(sources, keys, values)
+    terms, kv_out = lax.optimization_barrier((terms, kv_out))
     own, p_out = pl.pallas_call(
         sum_pack,
         in_specs=[SMEM, SMEM] + [VMEM] * 3,
         out_specs=[VMEM] * 2,
         out_shape=[
             jax.ShapeDtypeStruct((blocks, ROWS, 128), BF16),
-            jax.ShapeDtypeStruct((ctx, CAP + GLOB + 1, ROWS, 128), BF16),
+            jax.ShapeDtypeStruct((ctx, CAP + 2, ROWS, 128), BF16),
         ],
         scratch_shapes=[pltpu.VMEM((blocks, ROWS, 128), BF16)],
         compiler_params=PARAMS,
@@ -253,20 +275,20 @@
     p_before = lax.ppermute(own[-1], "ctx", up)
     p_after = lax.ppermute(own[0], "ctx", down)
 
-    chunk = 8
+    core = my_ctx % GLOB
+    p_here = lax.dynamic_index_in_dim(p_in[:, CAP], global_owner[core], 0, keepdims=False)
+    p_there = lax.ppermute(p_here, "ctx", [(i, i ^ 1) for i in range(ctx)])
+
     tile_owner = global_owner[jnp.minimum(my_ctx // (2 * PARTS), GLOB - 1)]
-    span = 2 * CAP * BLK + ROWS
     kv_out = pl.pallas_call(
-        pack_kv,
-        grid_spec=pltpu.PrefetchScalarGridSpec(
-            num_scalar_prefetch=2,
-            grid=(ctx // chunk,),
-            in_specs=[VMEM] * 3,
-            out_specs=pl.BlockSpec((chunk, span, h), lambda i, s, o: (i, 0, 0)),
-        ),
-        out_shape=pltpu.HBM((ctx, span, h), BF16),
-        compiler_params=PARAMS,
-    )(sources, tile_owner.reshape(1), keys, values, p_in)
+        add_tile,
+        in_specs=[SMEM, ANY, VMEM],
+        out_specs=ANY,
+        out_shape=pltpu.HBM(kv_out.shape, BF16),
+        input_output_aliases={1: 0},
+        scratch_shapes=[pltpu.VMEM((ctx, ROWS, h), BF16), pltpu.SemaphoreType.DMA],
+        compiler_params=PARAMS,
+    )(tile_owner.reshape(1), kv_out, p_in)
     kv_out, kv_before, kv_after, p_before, p_after = lax.optimization_barrier(
         (kv_out, kv_before, kv_after, p_before, p_after)
     )
@@ -274,11 +296,11 @@
 
     tiles = pl.pallas_call(
         collect,
-        in_specs=[SMEM, SMEM] + [VMEM] * 4,
+        in_specs=[SMEM, SMEM] + [VMEM] * 6,
         out_specs=VMEM,
         out_shape=jax.ShapeDtypeStruct((places, ROWS, 128), BF16),
         compiler_params=PARAMS,
-    )(arrival, global_owner, own, p_before, p_after, p_in)
+    )(arrival, core.reshape(1), own, p_before, p_after, p_here, p_there, p_in)
     pair = [tiles, lax.ppermute(tiles, "head", [(i, i ^ 1) for i in range(heads)])]
     every = jnp.arange(D, dtype=jnp.int32)
     table_new = proj_table(step_codes[1], rank_ids, every)
@@ -301,8 +323,9 @@
         all_heads += [source, source ^ 1]
 
     edges = jnp.stack([my_ctx == 0, my_ctx == ctx - 1]).astype(jnp.int32)
-    unroll = 2
+    unroll = 8
     wide = pl.BlockSpec((unroll * BLK, GROUP * h), lambda i: (i, 0))
+    queries, d_attn = (pltpu.with_memory_space_constraint(x, pltpu.HBM) for x in (queries, d_attn))
     dq, grad = pl.pallas_call(
         attend,
         grid=(blocks // unroll,),

time: 268 us -> 253 us (0.944)
  waiting for transfers between devices: 104 us -> 88.8 us
    all_to_all x1, waiting for transfers between devices: 12.7 us -> 7.33 us  [local(): terms = lax.all_to_all(terms, 'head', 0, 0, tiled=True)]
    all_to_all x1, waiting for transfers between devices: 22.2 us -> 17.1 us  [local(): p_in = lax.all_to_all(p_out, 'ctx', 0, 0, tiled=True)]
    ppermute x1, waiting for transfers between devices: 58.6 us -> 53.9 us  [local(): lax.ppermute(tiles, 'head', [(i, i ^ 1) for i in range(heads)])]
    unnamed x19 -> x17, local copies, waits for them, and re-layouts: 5.81 us -> 3.36 us
  transfers between devices with their start and end apart: 14 -> 15, of which waited for: 6 -> 7; matrix products, arithmetic and copies ran while one was open for 11% -> 11% of each run, Pallas kernels for 3% -> 3%
where the time goes in v5:
time: 253 us; the launch traced here: 252 us
  waiting for transfers between devices  88.8 us (35%)
  starting transfers between devices  65.9 us (26%)
  blocking collectives  30.3 us (12%)
  other arithmetic  28.8 us (11%)
  Pallas kernels  27.8 us (11%)
  local copies, waits for them, and re-layouts  6.24 us (2%)
  between operations  4.36 us (2%)
    ppermute x1, waiting for transfers between devices, local(): lax.ppermute(tiles, 'head', [(i, i ^ 1) for i in range(heads)])  53.9 us
    all_to_all x1, blocking collectives, local(): grad = lax.all_to_all(grad, 'ctx', 0, 0, tiled=True)  30.3 us
    convert_element_type x2, other arithmetic, proj_table(): return (unit_value * math.sqrt(12.0 / D)).astype(jnp.bfloat16)  27.4 us
    ppermute x6, starting transfers between devices, local(): all_tiles += [lax.ppermute(t, 'head', there) for t in pair]  17.3 us
    all_to_all x1, waiting for transfers between devices, local(): p_in = lax.all_to_all(p_out, 'ctx', 0, 0, tiled=True)  17.1 us
    all_to_all x1, starting transfers between devices, local(): p_in = lax.all_to_all(p_out, 'ctx', 0, 0, tiled=True)  16.7 us
    pallas_call x1, Pallas kernels, local(): pl.pallas_call(attend, grid=(blocks // unroll,), in_specs=[SMEM] * 3 + [w...  16 us
    ppermute x6, waiting for transfers between devices, local(): all_tiles += [lax.ppermute(t, 'head', there) for t in pair]  10.3 us
  transfers between devices with their start and end apart: 15, of which 7 were waited for; matrix products, arithmetic and copies ran while one was open for 11% of the time, Pallas kernels for 3%

profile of v5, /device:TPU:1, one launch (start us, length us, event | category | flops | bytes accessed | tf_op | source)
XLA Modules:
  0.0 252.2 jit_solution(5391089214318014406)
XLA Ops:
  0.7 1.3 fusion.78
  2.6 1.8 fusion.59.t_ref
  4.5 1.2 copy-done.4
  5.7 1.3 shard_map.112
  7.0 10.1 %all-to-all-start = ((bf16[8,16,16,128]{3,2,1,0:T(8,128)(2,1)}), bf16[8,16,16,128]{3,2,1,0:T(8,128)(2,1)S(1)}, u32[]{:S(2)}, u32[]{:S(2)}) async-start(bf16[8,16,16,128]{3,2,1,0:T(8,128)(2,1)} %shard_map.112), calls=%async_computation | async-start | bytes 1048576 | tf_op jit(solution)/shard_map/all_to_all | solution.py:244
  20.5 4.2 %shard_map.113.packed_ref = bf16[64,272,128]{2,1,0:T(8,128)(2,1)} custom-call(s32[128]{0:T(128)S(1)} %reshape.134.src_ref, bf16[1024,128]{1,0:T(8,128)(2,1)S(1)} %copy-done, bf16[1024,128]{1,0:T(8,128)(2,1)S(1)} %copy-done.2), custom_call_target="tpu_custom_call" | custom-call | tf_op jit(solution)/shard_map/pallas_call | solution.py:248
  24.7 7.3 %all-to-all-done.x_ref = bf16[8,16,16,128]{3,2,1,0:T(8,128)(2,1)S(1)} async-done(((bf16[8,16,16,128]{3,2,1,0:T(8,128)(2,1)}), bf16[8,16,16,128]{3,2,1,0:T(8,128)(2,1)S(1)}, u32[]{:S(2)}, u32[]{:S(2)}) %all-to-all-start) | async-done | bytes 524320 | tf_op jit(solution)/shard_map/all_to_all | solution.py:244
  32.1 1.7 shard_map.114
  33.8 16.7 %all-to-all-start.1 = ((bf16[64,4,16,128]{3,2,1,0:T(8,128)(2,1)}), bf16[64,4,16,128]{3,2,1,0:T(8,128)(2,1)S(1)}, u32[]{:S(2)}, u32[]{:S(2)}) async-start(bf16[64,4,16,128]{3,2,1,0:T(8,128)(2,1)} %get-tuple-element.20), calls=%async_computation.1 | async-start | bytes 2097152 | tf_op jit(solution)/shard_map/all_to_all | solution.py:274
  50.5 3.5 %collective-permute-start = (bf16[64,256]{1,0:T(8,128)(2,1)S(1)}, bf16[64,256]{1,0:T(8,128)(2,1)S(1)}, u32[]{:S(2)}, u32[]{:S(2)}) collective-permute-start(bf16[64,256]{1,0:T(8,128)(2,1)S(1)} %pad_maximum_fusion), channel_id=1, source_target_pairs={{0,8},{8,16},{16,24},{24,32},{32,40},{40,48},{48,56},{56,64},{64,7... | collective-permute-start | bytes 98312 | tf_op jit(solution)/shard_map/ppermute | solution.py:272
  54.1 1.9 collective-permute-start.1
  56.0 3.6 %collective-permute-start.2 = (bf16[16,128]{1,0:T(8,128)(2,1)S(1)}, bf16[16,128]{1,0:T(8,128)(2,1)S(1)}, u32[]{:S(2)}, u32[]{:S(2)}) collective-permute-start(bf16[16,128]{1,0:T(8,128)(2,1)S(1)} %get-tuple-element.40), channel_id=1, source_target_pairs={{0,8},{8,16},{16,24},{24,32},{32,40},{40,48},{48,56},{56,64},{64,7... | collective-permute-start | bytes 12296 | tf_op jit(solution)/shard_map/ppermute | solution.py:275
  59.7 1.9 collective-permute-start.3
  62.3 17.1 %all-to-all-done.1.tile_ref.recv_ref = bf16[64,4,16,128]{3,2,1,0:T(8,128)(2,1)S(1)} async-done(((bf16[64,4,16,128]{3,2,1,0:T(8,128)(2,1)}), bf16[64,4,16,128]{3,2,1,0:T(8,128)(2,1)S(1)}, u32[]{:S(2)}, u32[]{:S(2)}) %all-to-all-start.1) | async-done | bytes 1048608 | tf_op jit(solution)/shard_map/all_to_all | solution.py:274
  79.4 1.5 shard_map.115
  80.9 6.4 %all-to-all-start.2 = ((bf16[64,272,128]{2,1,0:T(8,128)(2,1)}), bf16[64,272,128]{2,1,0:T(8,128)(2,1)}, u32[]{:S(2)}, u32[]{:S(2)}) async-start(bf16[64,272,128]{2,1,0:T(8,128)(2,1)} %shard_map.115), calls=%async_computation.2 | async-start | bytes 8912896 | tf_op jit(solution)/shard_map/all_to_all | solution.py:295
  90.1 2.5 %collective-permute-start.4 = (bf16[16,128]{1,0:T(8,128)(2,1)S(1)}, bf16[16,128]{1,0:T(8,128)(2,1)S(1)}, u32[]{:S(2)}, u32[]{:S(2)}) collective-permute-start(bf16[16,128]{1,0:T(8,128)(2,1)S(1)} %dynamic-slice_bitcast_fusion.here_ref), channel_id=1, source_target_pairs={{0,8},{8,0},{16,24},{24,16},{32,40},{40,32},{48,56},{56,48},{64,72... | collective-permute-start | bytes 12296 | tf_op jit(solution)/shard_map/ppermute | solution.py:280
  94.3 1.9 collective-permute-start.5
  96.2 2.1 collective-permute-start.6
  98.3 25.6 %fusion.41 = (bf16[256,4096]{1,0:T(8,128)(2,1)S(1)}, bf16[256,4096]{1,0:T(8,128)(2,1)S(1)}) fusion(s32[]{:T(128)} %bitcast.11, s32[256]{0:T(256)S(1)} %get-tuple-element.53, s32[4096]{0:T(1024)S(1)} %iota_multiply_fusion, s32[256]{0:T(256)S(1)} %get-tuple-element.54, s32[]{:T(128)} %bitcast.20), kind=kLoop, calls=%fused_computation.53 | loop fusion | flops 93323264 | bytes 4212744 | tf_op jit(solution)/shard_map/convert_element_type | solution.py:37
  125.1 3.7 %collective-permute-start.8 = (bf16[68,16,128]{2,1,0:T(8,128)(2,1)S(1)}, bf16[68,16,128]{2,1,0:T(8,128)(2,1)}, u32[]{:S(2)}, u32[]{:S(2)}) collective-permute-start(bf16[68,16,128]{2,1,0:T(8,128)(2,1)S(1)} %shard_map.116.refs_0_), channel_id=1, source_target_pairs={{0,4},{1,5},{2,6},{3,7},{4,0},{5,1},{6,2},{7,3},{8,12},{9,13},{10,... | collective-permute-start | bytes 835592 | tf_op jit(solution)/shard_map/ppermute | solution.py:321
  128.8 2.9 %collective-permute-start.10 = (bf16[68,16,128]{2,1,0:T(8,128)(2,1)S(1)}, bf16[68,16,128]{2,1,0:T(8,128)(2,1)}, u32[]{:S(2)}, u32[]{:S(2)}) collective-permute-start(bf16[68,16,128]{2,1,0:T(8,128)(2,1)S(1)} %shard_map.116.refs_0_), channel_id=1, source_target_pairs={{0,6},{1,7},{2,0},{3,1},{4,2},{5,3},{6,4},{7,5},{8,14},{9,15},{10,... | collective-permute-start | bytes 835592 | tf_op jit(solution)/shard_map/ppermute | solution.py:321
  131.7 53.9 %collective-permute-done.5.refs_1_ = bf16[68,16,128]{2,1,0:T(8,128)(2,1)S(1)} collective-permute-done((bf16[68,16,128]{2,1,0:T(8,128)(2,1)S(1)}, bf16[68,16,128]{2,1,0:T(8,128)(2,1)S(1)}, u32[]{:S(2)}, u32[]{:S(2)}) %collective-permute-start.5) | collective-permute-done | bytes 278560 | tf_op jit(solution)/shard_map/ppermute | solution.py:304
  185.6 1.9 collective-permute-start.7
  187.5 3.7 %collective-permute-start.9 = (bf16[68,16,128]{2,1,0:T(8,128)(2,1)S(1)}, bf16[68,16,128]{2,1,0:T(8,128)(2,1)}, u32[]{:S(2)}, u32[]{:S(2)}) collective-permute-start(bf16[68,16,128]{2,1,0:T(8,128)(2,1)S(1)} %collective-permute-done.5.refs_1_), channel_id=1, source_target_pairs={{0,4},{1,5},{2,6},{3,7},{4,0},{5,1},{6,2},{7,3},{8,12},{9,13},{10,... | collective-permute-start | bytes 835592 | tf_op jit(solution)/shard_map/ppermute | solution.py:321
  191.2 3.0 %collective-permute-start.11 = (bf16[68,16,128]{2,1,0:T(8,128)(2,1)S(1)}, bf16[68,16,128]{2,1,0:T(8,128)(2,1)}, u32[]{:S(2)}, u32[]{:S(2)}) collective-permute-start(bf16[68,16,128]{2,1,0:T(8,128)(2,1)S(1)} %collective-permute-done.5.refs_1_), channel_id=1, source_target_pairs={{0,6},{1,7},{2,0},{3,1},{4,2},{5,3},{6,4},{7,5},{8,14},{9,15},{10,... | collective-permute-start | bytes 835592 | tf_op jit(solution)/shard_map/ppermute | solution.py:321
  194.4 2.4 collective-permute-done.7.refs_3_
  196.9 4.2 %collective-permute-done.9.refs_5_ = bf16[68,16,128]{2,1,0:T(8,128)(2,1)} collective-permute-done((bf16[68,16,128]{2,1,0:T(8,128)(2,1)S(1)}, bf16[68,16,128]{2,1,0:T(8,128)(2,1)}, u32[]{:S(2)}, u32[]{:S(2)}) %collective-permute-start.9) | collective-permute-done | bytes 278560 | tf_op jit(solution)/shard_map/ppermute | solution.py:321
  201.1 3.6 %collective-permute-done.11.refs_7_ = bf16[68,16,128]{2,1,0:T(8,128)(2,1)} collective-permute-done((bf16[68,16,128]{2,1,0:T(8,128)(2,1)S(1)}, bf16[68,16,128]{2,1,0:T(8,128)(2,1)}, u32[]{:S(2)}, u32[]{:S(2)}) %collective-permute-start.11) | collective-permute-done | bytes 278560 | tf_op jit(solution)/shard_map/ppermute | solution.py:321
  204.7 16.0 %shard_map.118 = (bf16[1024,512]{1,0:T(8,128)(2,1)}, f32[64,8,128]{2,1,0:T(8,128)}) custom-call(s32[48]{0:T(128)S(1)} %convert_add_fusion.arrival_ref, s32[2]{0:T(128)S(1)} %add_convert_fusion.edge_ref, s32[8]{0:T(128)S(1)} %stack.52.from_ref, bf16[1024,512]{1,0:T(8,128)(2,1)} %q_ref.1, bf16[1024,512]{1,0:T(8,128)(2,1)} %g_ref.1, ...), custom_call_target="tpu_custom_call" | custom-call | tf_op jit(solution)/shard_map/pallas_call | solution.py:329
  220.8 30.3 %all_to_all.20.recv_ref = f32[64,8,128]{2,1,0:T(8,128)S(1)} all-to-all(f32[64,8,128]{2,1,0:T(8,128)} %get-tuple-element.30), channel_id=1, replica_groups=mesh['ctx'=64,'head'=8] {'ctx'}, dimensions={0} | all-to-all | bytes 524288 | tf_op jit(solution)/shard_map/all_to_all | solution.py:353
  251.0 1.2 shard_map.119
  (59 shorter events, 7.2 us)
Async XLA Ops:
  4.5 1.2 copy-start.4
  5.7 19.0 %copy-start.7 = (s32[2]{0:T(128)S(1)}, s32[2]{0:T(128)}, u32[]{:S(2)}) copy-start(s32[2]{0:T(128)} %param.15) | copy-start | bytes 28
  5.7 26.4 %copy-start.1 = (bf16[1024,128]{1,0:T(8,128)(2,1)S(1)}, bf16[1024,128]{1,0:T(8,128)(2,1)}, u32[]{:S(2)}) copy-start(bf16[1024,128]{1,0:T(8,128)(2,1)} %k_ref.5) | copy-start | bytes 786436
  5.7 26.4 %copy-start.3 = (bf16[1024,128]{1,0:T(8,128)(2,1)S(1)}, bf16[1024,128]{1,0:T(8,128)(2,1)}, u32[]{:S(2)}) copy-start(bf16[1024,128]{1,0:T(8,128)(2,1)} %v_ref.5) | copy-start | bytes 786436
  7.0 25.1 %all-to-all-start = ((bf16[8,16,16,128]{3,2,1,0:T(8,128)(2,1)}), bf16[8,16,16,128]{3,2,1,0:T(8,128)(2,1)S(1)}, u32[]{:S(2)}, u32[]{:S(2)}) async-start(bf16[8,16,16,128]{3,2,1,0:T(8,128)(2,1)} %shard_map.112), calls=%async_computation | async-start | bytes 1048576 | tf_op jit(solution)/shard_map/all_to_all | solution.py:244
  18.6 1.0 copy-start
  19.6 0.9 copy-start.2
  33.8 45.6 %all-to-all-start.1 = ((bf16[64,4,16,128]{3,2,1,0:T(8,128)(2,1)}), bf16[64,4,16,128]{3,2,1,0:T(8,128)(2,1)S(1)}, u32[]{:S(2)}, u32[]{:S(2)}) async-start(bf16[64,4,16,128]{3,2,1,0:T(8,128)(2,1)} %get-tuple-element.20), calls=%async_computation.1 | async-start | bytes 2097152 | tf_op jit(solution)/shard_map/all_to_all | solution.py:274
  50.5 30.4 %collective-permute-start = (bf16[64,256]{1,0:T(8,128)(2,1)S(1)}, bf16[64,256]{1,0:T(8,128)(2,1)S(1)}, u32[]{:S(2)}, u32[]{:S(2)}) collective-permute-start(bf16[64,256]{1,0:T(8,128)(2,1)S(1)} %pad_maximum_fusion), channel_id=1, source_target_pairs={{0,8},{8,16},{16,24},{24,32},{32,40},{40,48},{48,56},{56,64},{64,7... | collective-permute-start | bytes 98312 | tf_op jit(solution)/shard_map/ppermute | solution.py:272
  54.1 26.8 %collective-permute-start.1 = (bf16[64,256]{1,0:T(8,128)(2,1)S(1)}, bf16[64,256]{1,0:T(8,128)(2,1)S(1)}, u32[]{:S(2)}, u32[]{:S(2)}) collective-permute-start(bf16[64,256]{1,0:T(8,128)(2,1)S(1)} %pad_maximum_fusion.1), channel_id=1, source_target_pairs={{8,0},{16,8},{24,16},{32,24},{40,32},{48,40},{56,48},{64,56},{72,6... | collective-permute-start | bytes 98312 | tf_op jit(solution)/shard_map/ppermute | solution.py:273
  56.0 24.9 %collective-permute-start.2 = (bf16[16,128]{1,0:T(8,128)(2,1)S(1)}, bf16[16,128]{1,0:T(8,128)(2,1)S(1)}, u32[]{:S(2)}, u32[]{:S(2)}) collective-permute-start(bf16[16,128]{1,0:T(8,128)(2,1)S(1)} %get-tuple-element.40), channel_id=1, source_target_pairs={{0,8},{8,16},{16,24},{24,32},{32,40},{40,48},{48,56},{56,64},{64,7... | collective-permute-start | bytes 12296 | tf_op jit(solution)/shard_map/ppermute | solution.py:275
  59.7 21.2 %collective-permute-start.3 = (bf16[16,128]{1,0:T(8,128)(2,1)S(1)}, bf16[16,128]{1,0:T(8,128)(2,1)S(1)}, u32[]{:S(2)}, u32[]{:S(2)}) collective-permute-start(bf16[16,128]{1,0:T(8,128)(2,1)S(1)} %get-tuple-element.39), channel_id=1, source_target_pairs={{8,0},{16,8},{24,16},{32,24},{40,32},{48,40},{56,48},{64,56},{72,6... | collective-permute-start | bytes 12296 | tf_op jit(solution)/shard_map/ppermute | solution.py:276
  80.8 6.5 %copy-start.5 = (s32[1024,3]{0,1:T(4,128)S(1)}, s32[1024,3]{0,1:T(4,128)}, u32[]{:S(2)}) copy-start(s32[1024,3]{0,1:T(4,128)} %param.14) | copy-start | bytes 36868
  80.9 123.8 %all-to-all-start.2 = ((bf16[64,272,128]{2,1,0:T(8,128)(2,1)}), bf16[64,272,128]{2,1,0:T(8,128)(2,1)}, u32[]{:S(2)}, u32[]{:S(2)}) async-start(bf16[64,272,128]{2,1,0:T(8,128)(2,1)} %shard_map.115), calls=%async_computation.2 | async-start | bytes 8912896 | tf_op jit(solution)/shard_map/all_to_all | solution.py:295
  87.3 36.6 %copy-start.6 = (f32[1,4,256]{2,1,0:T(4,128)S(1)}, f32[1,4,256]{2,1,0:T(4,128)}, u32[]{:S(2)}) copy-start(f32[1,4,256]{2,1,0:T(4,128)} %param.17) | copy-start | bytes 12292
  90.1 3.4 %collective-permute-start.4 = (bf16[16,128]{1,0:T(8,128)(2,1)S(1)}, bf16[16,128]{1,0:T(8,128)(2,1)S(1)}, u32[]{:S(2)}, u32[]{:S(2)}) collective-permute-start(bf16[16,128]{1,0:T(8,128)(2,1)S(1)} %dynamic-slice_bitcast_fusion.here_ref), channel_id=1, source_target_pairs={{0,8},{8,0},{16,24},{24,16},{32,40},{40,32},{48,56},{56,48},{64,72... | collective-permute-start | bytes 12296 | tf_op jit(solution)/shard_map/ppermute | solution.py:280
  94.3 91.3 %collective-permute-start.5 = (bf16[68,16,128]{2,1,0:T(8,128)(2,1)S(1)}, bf16[68,16,128]{2,1,0:T(8,128)(2,1)S(1)}, u32[]{:S(2)}, u32[]{:S(2)}) collective-permute-start(bf16[68,16,128]{2,1,0:T(8,128)(2,1)S(1)} %shard_map.116.refs_0_), channel_id=1, source_target_pairs={{0,1},{1,0},{2,3},{3,2},{4,5},{5,4},{6,7},{7,6},{8,9},{9,8},{10,11... | collective-permute-start | bytes 835592 | tf_op jit(solution)/shard_map/ppermute | solution.py:304
  96.2 95.0 %collective-permute-start.6 = (bf16[68,16,128]{2,1,0:T(8,128)(2,1)S(1)}, bf16[68,16,128]{2,1,0:T(8,128)(2,1)S(1)}, u32[]{:S(2)}, u32[]{:S(2)}) collective-permute-start(bf16[68,16,128]{2,1,0:T(8,128)(2,1)S(1)} %shard_map.116.refs_0_), channel_id=1, source_target_pairs={{0,2},{1,3},{2,4},{3,5},{4,6},{5,7},{6,0},{7,1},{8,10},{9,11},{10,... | collective-permute-start | bytes 835592 | tf_op jit(solution)/shard_map/ppermute | solution.py:321
  125.1 69.3 %collective-permute-start.8 = (bf16[68,16,128]{2,1,0:T(8,128)(2,1)S(1)}, bf16[68,16,128]{2,1,0:T(8,128)(2,1)}, u32[]{:S(2)}, u32[]{:S(2)}) collective-permute-start(bf16[68,16,128]{2,1,0:T(8,128)(2,1)S(1)} %shard_map.116.refs_0_), channel_id=1, source_target_pairs={{0,4},{1,5},{2,6},{3,7},{4,0},{5,1},{6,2},{7,3},{8,12},{9,13},{10,... | collective-permute-start | bytes 835592 | tf_op jit(solution)/shard_map/ppermute | solution.py:321
  128.8 65.6 %collective-permute-start.10 = (bf16[68,16,128]{2,1,0:T(8,128)(2,1)S(1)}, bf16[68,16,128]{2,1,0:T(8,128)(2,1)}, u32[]{:S(2)}, u32[]{:S(2)}) collective-permute-start(bf16[68,16,128]{2,1,0:T(8,128)(2,1)S(1)} %shard_map.116.refs_0_), channel_id=1, source_target_pairs={{0,6},{1,7},{2,0},{3,1},{4,2},{5,3},{6,4},{7,5},{8,14},{9,15},{10,... | collective-permute-start | bytes 835592 | tf_op jit(solution)/shard_map/ppermute | solution.py:321
  185.6 11.3 %collective-permute-start.7 = (bf16[68,16,128]{2,1,0:T(8,128)(2,1)S(1)}, bf16[68,16,128]{2,1,0:T(8,128)(2,1)}, u32[]{:S(2)}, u32[]{:S(2)}) collective-permute-start(bf16[68,16,128]{2,1,0:T(8,128)(2,1)S(1)} %collective-permute-done.5.refs_1_), channel_id=1, source_target_pairs={{0,2},{1,3},{2,4},{3,5},{4,6},{5,7},{6,0},{7,1},{8,10},{9,11},{10,... | collective-permute-start | bytes 835592 | tf_op jit(solution)/shard_map/ppermute | solution.py:321
  187.5 13.6 %collective-permute-start.9 = (bf16[68,16,128]{2,1,0:T(8,128)(2,1)S(1)}, bf16[68,16,128]{2,1,0:T(8,128)(2,1)}, u32[]{:S(2)}, u32[]{:S(2)}) collective-permute-start(bf16[68,16,128]{2,1,0:T(8,128)(2,1)S(1)} %collective-permute-done.5.refs_1_), channel_id=1, source_target_pairs={{0,4},{1,5},{2,6},{3,7},{4,0},{5,1},{6,2},{7,3},{8,12},{9,13},{10,... | collective-permute-start | bytes 835592 | tf_op jit(solution)/shard_map/ppermute | solution.py:321
  191.2 13.5 %collective-permute-start.11 = (bf16[68,16,128]{2,1,0:T(8,128)(2,1)S(1)}, bf16[68,16,128]{2,1,0:T(8,128)(2,1)}, u32[]{:S(2)}, u32[]{:S(2)}) collective-permute-start(bf16[68,16,128]{2,1,0:T(8,128)(2,1)S(1)} %collective-permute-done.5.refs_1_), channel_id=1, source_target_pairs={{0,6},{1,7},{2,0},{3,1},{4,2},{5,3},{6,4},{7,5},{8,14},{9,15},{10,... | collective-permute-start | bytes 835592 | tf_op jit(solution)/shard_map/ppermute | solution.py:321

commit v6 on v5

--- a/solution.py
+++ b/solution.py
@@ -95,11 +95,10 @@
             out_ref[i, CAP + 1] = jnp.zeros((ROWS, 128), BF16)
 
 
-def collect(arrival_ref, core_ref, own_ref, before_ref, after_ref, here_ref, there_ref, recv_ref, out_ref):
-    blocks = own_ref.shape[0]
-    tiles = [before_ref[...]] + [own_ref[b] for b in range(blocks)] + [after_ref[...]]
+def collect(arrival_ref, core_ref, before_ref, after_ref, here_ref, there_ref, recv_ref, out_ref):
+    tiles = [before_ref[...], after_ref[...]]
     tiles += [jnp.where(core_ref[0] == g, here_ref[...], there_ref[...]) for g in range(GLOB)]
-    tiles += [recv_ref[arrival_ref[n] // CAP, arrival_ref[n] % CAP] for n in range(blocks * RAND)]
+    tiles += [recv_ref[arrival_ref[n] // CAP, arrival_ref[n] % CAP] for n in range(arrival_ref.shape[0])]
     for n, tile in enumerate(tiles):
         out_ref[n] = tile
 
@@ -172,17 +171,19 @@
 
     @pl.when(step == steps - 1)
     def _():
-        for acc, first, count in ((wacc, 0, blocks + 2), (gacc, blocks + 2, GLOB)):
-            for n in range(count):
-                for part in range(PARTS):
-                    low = n * BLK + part * ROWS
-                    kg_ref[part, first + n] = acc[low : low + ROWS, :].astype(BF16)
+        window = [(wacc, n + 1, n) for n in range(blocks)] + [(wacc, 0, blocks), (wacc, blocks + 1, blocks + 1)]
+        for acc, n, place in window + [(gacc, n, blocks + 2 + n) for n in range(GLOB)]:
+            for part in range(PARTS):
+                low = n * BLK + part * ROWS
+                kg_ref[part, place] = acc[low : low + ROWS, :].astype(BF16)
         total[...] = jnp.zeros_like(total)
         many = kg_ref.shape[1] * ROWS
-        for i, ref in enumerate(tile_refs):
+        for i in range(from_ref.shape[0]):
             head = from_ref[i]
+            own, other = tile_refs[i // 2], tile_refs[from_ref.shape[0] // 2 + i]
             kg = kg_ref[head % PARTS].reshape(many, 2 * h)
-            total[head // PARTS] += dot(kg, ref[...].reshape(many, 128), 0, 0)
+            tile = jnp.concatenate([own[i % 2].reshape(blocks * ROWS, 128), other[...].reshape(-1, 128)], axis=0)
+            total[head // PARTS] += dot(kg, tile, 0, 0)
         rows = total.shape[1] // out_ref.shape[0]
         for d in range(out_ref.shape[0]):
             for half in range(2):
@@ -271,6 +272,8 @@
 
     kv_before = lax.ppermute(jnp.concatenate([keys[-BLK:], values[-BLK:]], axis=1), "ctx", up)
     kv_after = lax.ppermute(jnp.concatenate([keys[:BLK], values[:BLK]], axis=1), "ctx", down)
+    across = [(i, i ^ 1) for i in range(heads)]
+    own_pair = jnp.stack([own, lax.ppermute(own, "head", across)])
     p_in = lax.all_to_all(p_out, "ctx", 0, 0, tiled=True)
     p_before = lax.ppermute(own[-1], "ctx", up)
     p_after = lax.ppermute(own[0], "ctx", down)
@@ -289,22 +292,23 @@
         scratch_shapes=[pltpu.VMEM((ctx, ROWS, h), BF16), pltpu.SemaphoreType.DMA],
         compiler_params=PARAMS,
     )(tile_owner.reshape(1), kv_out, p_in)
-    kv_out, kv_before, kv_after, p_before, p_after = lax.optimization_barrier(
-        (kv_out, kv_before, kv_after, p_before, p_after)
+    kv_out, kv_before, kv_after, p_before, p_after, own_pair = lax.optimization_barrier(
+        (kv_out, kv_before, kv_after, p_before, p_after, own_pair)
     )
     kv_in = lax.all_to_all(kv_out, "ctx", 0, 0, tiled=True)
 
     tiles = pl.pallas_call(
         collect,
-        in_specs=[SMEM, SMEM] + [VMEM] * 6,
+        in_specs=[SMEM, SMEM] + [VMEM] * 5,
         out_specs=VMEM,
-        out_shape=jax.ShapeDtypeStruct((places, ROWS, 128), BF16),
-        compiler_params=PARAMS,
-    )(arrival, core.reshape(1), own, p_before, p_after, p_here, p_there, p_in)
-    pair = [tiles, lax.ppermute(tiles, "head", [(i, i ^ 1) for i in range(heads)])]
+        out_shape=jax.ShapeDtypeStruct((places - blocks, ROWS, 128), BF16),
+        compiler_params=PARAMS,
+    )(arrival, core.reshape(1), p_before, p_after, p_here, p_there, p_in)
+    pair = [tiles, lax.ppermute(tiles, "head", across)]
     every = jnp.arange(D, dtype=jnp.int32)
     table_new = proj_table(step_codes[1], rank_ids, every)
     table_old = proj_table(step_codes[0], rank_ids, every)
+    own_pair, table_new = lax.optimization_barrier((own_pair, table_new))
     share = momentum.shape[1]
     carried = pl.pallas_call(
         carry,
@@ -315,9 +319,10 @@
     )(jnp.pad(momentum[0], ((0, 8 - share), (0, 0))), table_old, table_new)
 
     pair[1], carried = lax.optimization_barrier((pair[1], carried))
-    all_tiles, all_heads = list(pair), [my_head, my_head ^ 1]
+    own_tiles, all_tiles, all_heads = [own_pair], list(pair), [my_head, my_head ^ 1]
     for far in range(2, heads, 2):
         there = [(i, (i + far) % heads) for i in range(heads)]
+        own_tiles.append(lax.ppermute(own_pair, "head", there))
         all_tiles += [lax.ppermute(t, "head", there) for t in pair]
         source = (my_head - far) % heads
         all_heads += [source, source ^ 1]
@@ -329,7 +334,7 @@
     dq, grad = pl.pallas_call(
         attend,
         grid=(blocks // unroll,),
-        in_specs=[SMEM] * 3 + [wide] * 2 + [VMEM] * (5 + heads) + [ANY] * 2,
+        in_specs=[SMEM] * 3 + [wide] * 2 + [VMEM] * (5 + heads // 2 + heads) + [ANY] * 2,
         out_specs=[wide, VMEM],
         out_shape=[
             jax.ShapeDtypeStruct((tokens, GROUP * h), BF16),
@@ -348,7 +353,7 @@
         compiler_params=LARGE,
     )(
         arrival, edges, jnp.stack(all_heads), queries, d_attn, keys, values, kv_before, kv_after, kv_in,
-        *all_tiles, table_new, carried,
+        *own_tiles, *all_tiles, table_new, carried,
     )
     grad = lax.all_to_all(grad, "ctx", 0, 0, tiled=True)
     new_momentum, weight_step = pl.pallas_call(

time: 253 us -> 257 us (1.016)
  starting transfers between devices: 65.9 us -> 77.2 us
  waiting for transfers between devices: 88.8 us -> 80.8 us
  local copies, waits for them, and re-layouts: 6.24 us -> 11.4 us
  blocking collectives: 30.3 us -> 25.5 us
    ppermute x1 -> x5, starting transfers between devices: 1.92 us -> 13.4 us  [the longest x3 9.58 us: local(): own_tiles.append(lax.ppermute(own_pair, 'head', there))]
    all_to_all x1, waiting for transfers between devices: 17.1 us -> 10.8 us  [local(): p_in = lax.all_to_all(p_out, 'ctx', 0, 0, tiled=True)]
    unnamed x17 -> x33, local copies, waits for them, and re-layouts: 3.36 us -> 8.56 us
    all_to_all x1, blocking collectives: 30.3 us -> 25.5 us  [local(): grad = lax.all_to_all(grad, 'ctx', 0, 0, tiled=True)]
    ppermute x6, waiting for transfers between devices: 10.3 us -> 6.32 us  [local(): all_tiles += [lax.ppermute(t, 'head', there) for t in pair]]
    ppermute x1 -> x5, waiting for transfers between devices: 53.9 us -> 56.2 us  [the longest x1 49.2 us: local(): pair = [tiles, lax.ppermute(tiles, 'head', across)]]
  transfers between devices with their start and end apart: 15 -> 19, of which waited for: 7 -> 7; matrix products, arithmetic and copies ran while one was open for 11% -> 11% of each run, Pallas kernels for 3% -> 3%
where the time goes in v6:
time: 257 us; the launch traced here: 256 us
  waiting for transfers between devices  80.8 us (31%)
  starting transfers between devices  77.2 us (30%)
  other arithmetic  28.8 us (11%)
  Pallas kernels  27.7 us (11%)
  blocking collectives  25.5 us (10%)
  local copies, waits for them, and re-layouts  11.4 us (4%)
  between operations  4.6 us (2%)
    ppermute x1, waiting for transfers between devices, local(): pair = [tiles, lax.ppermute(tiles, 'head', across)]  49.2 us
    convert_element_type x2, other arithmetic, proj_table(): return (unit_value * math.sqrt(12.0 / D)).astype(jnp.bfloat16)  27.4 us
    all_to_all x1, blocking collectives, local(): grad = lax.all_to_all(grad, 'ctx', 0, 0, tiled=True)  25.5 us
    ppermute x6, starting transfers between devices, local(): all_tiles += [lax.ppermute(t, 'head', there) for t in pair]  16.8 us
    all_to_all x1, starting transfers between devices, local(): p_in = lax.all_to_all(p_out, 'ctx', 0, 0, tiled=True)  16.7 us
    pallas_call x1, Pallas kernels, local(): pl.pallas_call(attend, grid=(blocks // unroll,), in_specs=[SMEM] * 3 + [w...  15.9 us
    all_to_all x1, waiting for transfers between devices, local(): p_in = lax.all_to_all(p_out, 'ctx', 0, 0, tiled=True)  10.8 us
    all_to_all x1, starting transfers between devices, local(): terms = lax.all_to_all(terms, 'head', 0, 0, tiled=True)  10.1 us
  transfers between devices with their start and end apart: 19, of which 7 were waited for; matrix products, arithmetic and copies ran while one was open for 11% of the time, Pallas kernels for 3%

profile of v6, /device:TPU:1, one launch (start us, length us, event | category | flops | bytes accessed | tf_op | source)
XLA Modules:
  0.0 256.0 jit_solution(7069182412926251065)
XLA Ops:
  2.6 1.8 fusion.59.t_ref
  7.0 10.1 %all-to-all-start = ((bf16[8,16,16,128]{3,2,1,0:T(8,128)(2,1)}), bf16[8,16,16,128]{3,2,1,0:T(8,128)(2,1)S(1)}, u32[]{:S(2)}, u32[]{:S(2)}) async-start(bf16[8,16,16,128]{3,2,1,0:T(8,128)(2,1)} %shard_map.112), calls=%async_computation | async-start | bytes 1048576 | tf_op jit(solution)/shard_map/all_to_all | solution.py:245
  20.5 4.2 %shard_map.113.packed_ref = bf16[64,272,128]{2,1,0:T(8,128)(2,1)} custom-call(s32[128]{0:T(128)S(1)} %reshape.134.src_ref, bf16[1024,128]{1,0:T(8,128)(2,1)S(1)} %copy-done, bf16[1024,128]{1,0:T(8,128)(2,1)S(1)} %copy-done.2), custom_call_target="tpu_custom_call" | custom-call | tf_op jit(solution)/shard_map/pallas_call | solution.py:249
  24.8 7.3 %all-to-all-done.x_ref = bf16[8,16,16,128]{3,2,1,0:T(8,128)(2,1)S(1)} async-done(((bf16[8,16,16,128]{3,2,1,0:T(8,128)(2,1)}), bf16[8,16,16,128]{3,2,1,0:T(8,128)(2,1)S(1)}, u32[]{:S(2)}, u32[]{:S(2)}) %all-to-all-start) | async-done | bytes 524320 | tf_op jit(solution)/shard_map/all_to_all | solution.py:245
  32.1 1.7 shard_map.114
  33.8 16.7 %all-to-all-start.1 = ((bf16[64,4,16,128]{3,2,1,0:T(8,128)(2,1)}), bf16[64,4,16,128]{3,2,1,0:T(8,128)(2,1)S(1)}, u32[]{:S(2)}, u32[]{:S(2)}) async-start(bf16[64,4,16,128]{3,2,1,0:T(8,128)(2,1)} %get-tuple-element.23), calls=%async_computation.1 | async-start | bytes 2097152 | tf_op jit(solution)/shard_map/all_to_all | solution.py:277
  50.5 3.5 %collective-permute-start = (bf16[64,256]{1,0:T(8,128)(2,1)S(1)}, bf16[64,256]{1,0:T(8,128)(2,1)S(1)}, u32[]{:S(2)}, u32[]{:S(2)}) collective-permute-start(bf16[64,256]{1,0:T(8,128)(2,1)S(1)} %pad_maximum_fusion.1), channel_id=1, source_target_pairs={{0,8},{8,16},{16,24},{24,32},{32,40},{40,48},{48,56},{56,64},{64,7... | collective-permute-start | bytes 98312 | tf_op jit(solution)/shard_map/ppermute | solution.py:273
  54.1 1.9 collective-permute-start.1
  56.7 1.9 collective-permute-start.4
  58.6 3.8 %collective-permute-start.2 = (bf16[16,128]{1,0:T(8,128)(2,1)S(1)}, bf16[16,128]{1,0:T(8,128)(2,1)S(1)}, u32[]{:S(2)}, u32[]{:S(2)}) collective-permute-start(bf16[16,128]{1,0:T(8,128)(2,1)S(1)} %get-tuple-element.46), channel_id=1, source_target_pairs={{0,8},{8,16},{16,24},{24,32},{32,40},{40,48},{48,56},{56,64},{64,7... | collective-permute-start | bytes 12296 | tf_op jit(solution)/shard_map/ppermute | solution.py:278
  62.5 1.9 collective-permute-start.3
  64.4 7.0 %collective-permute-done.4 = bf16[16,16,128]{2,1,0:T(8,128)(2,1)S(1)} collective-permute-done((bf16[16,16,128]{2,1,0:T(8,128)(2,1)S(1)}, bf16[16,16,128]{2,1,0:T(8,128)(2,1)S(1)}, u32[]{:S(2)}, u32[]{:S(2)}) %collective-permute-start.4) | collective-permute-done | bytes 65568 | tf_op jit(solution)/shard_map/ppermute | solution.py:276
  71.4 10.8 %all-to-all-done.1.tile_ref.recv_ref = bf16[64,4,16,128]{3,2,1,0:T(8,128)(2,1)S(1)} async-done(((bf16[64,4,16,128]{3,2,1,0:T(8,128)(2,1)}), bf16[64,4,16,128]{3,2,1,0:T(8,128)(2,1)S(1)}, u32[]{:S(2)}, u32[]{:S(2)}) %all-to-all-start.1) | async-done | bytes 1048608 | tf_op jit(solution)/shard_map/all_to_all | solution.py:277
  82.2 1.4 shard_map.115
  84.3 6.4 %all-to-all-start.2 = ((bf16[64,272,128]{2,1,0:T(8,128)(2,1)}), bf16[64,272,128]{2,1,0:T(8,128)(2,1)}, u32[]{:S(2)}, u32[]{:S(2)}) async-start(bf16[64,272,128]{2,1,0:T(8,128)(2,1)} %shard_map.115), calls=%async_computation.2 | async-start | bytes 8912896 | tf_op jit(solution)/shard_map/all_to_all | solution.py:298
  93.6 2.5 collective-permute-start.8
  97.8 1.9 collective-permute-start.9
  99.7 2.1 collective-permute-start.10
  101.8 25.6 %fusion.41 = (bf16[256,4096]{1,0:T(8,128)(2,1)S(1)}, bf16[256,4096]{1,0:T(8,128)(2,1)S(1)}) fusion(s32[]{:T(128)} %bitcast.22, s32[256]{0:T(256)S(1)} %get-tuple-element.59, s32[4096]{0:T(1024)S(1)} %iota_multiply_fusion, s32[256]{0:T(256)S(1)} %get-tuple-element.60, s32[]{:T(128)} %bitcast.11), kind=kLoop, calls=%fused_computation.53 | loop fusion | flops 93323264 | bytes 4212744 | tf_op jit(solution)/shard_map/convert_element_type | solution.py:37
  127.4 2.3 collective-permute-start.5
  129.7 5.2 %collective-permute-start.6 = (bf16[2,16,16,128]{3,2,1,0:T(8,128)(2,1)S(1)}, bf16[2,16,16,128]{3,2,1,0:T(8,128)(2,1)S(1)}, u32[]{:S(2)}, u32[]{:S(2)}) collective-permute-start(bf16[2,16,16,128]{3,2,1,0:T(8,128)(2,1)S(1)} %pad_maximum_fusion.refs_0_), channel_id=1, source_target_pairs={{0,4},{1,5},{2,6},{3,7},{4,0},{5,1},{6,2},{7,3},{8,12},{9,13},{10,... | collective-permute-start | bytes 393224 | tf_op jit(solution)/shard_map/ppermute | solution.py:325
  134.9 2.1 collective-permute-start.7
  138.2 49.2 %collective-permute-done.9.refs_5_ = bf16[52,16,128]{2,1,0:T(8,128)(2,1)S(1)} collective-permute-done((bf16[52,16,128]{2,1,0:T(8,128)(2,1)S(1)}, bf16[52,16,128]{2,1,0:T(8,128)(2,1)S(1)}, u32[]{:S(2)}, u32[]{:S(2)}) %collective-permute-start.9) | collective-permute-done | bytes 213024 | tf_op jit(solution)/shard_map/ppermute | solution.py:307
  187.4 2.1 collective-permute-start.12
  189.5 3.1 %collective-permute-start.14 = (bf16[52,16,128]{2,1,0:T(8,128)(2,1)S(1)}, bf16[52,16,128]{2,1,0:T(8,128)(2,1)}, u32[]{:S(2)}, u32[]{:S(2)}) collective-permute-start(bf16[52,16,128]{2,1,0:T(8,128)(2,1)S(1)} %shard_map.116.refs_4_), channel_id=1, source_target_pairs={{0,6},{1,7},{2,0},{3,1},{4,2},{5,3},{6,4},{7,5},{8,14},{9,15},{10,... | collective-permute-start | bytes 638984 | tf_op jit(solution)/shard_map/ppermute | solution.py:326
  193.2 2.2 collective-permute-start.11
  196.1 4.7 %collective-permute-start.13 = (bf16[52,16,128]{2,1,0:T(8,128)(2,1)S(1)}, bf16[52,16,128]{2,1,0:T(8,128)(2,1)}, u32[]{:S(2)}, u32[]{:S(2)}) collective-permute-start(bf16[52,16,128]{2,1,0:T(8,128)(2,1)S(1)} %collective-permute-done.9.refs_5_), channel_id=1, source_target_pairs={{0,4},{1,5},{2,6},{3,7},{4,0},{5,1},{6,2},{7,3},{8,12},{9,13},{10,... | collective-permute-start | bytes 638984 | tf_op jit(solution)/shard_map/ppermute | solution.py:326
  200.8 2.7 %collective-permute-start.15 = (bf16[52,16,128]{2,1,0:T(8,128)(2,1)S(1)}, bf16[52,16,128]{2,1,0:T(8,128)(2,1)}, u32[]{:S(2)}, u32[]{:S(2)}) collective-permute-start(bf16[52,16,128]{2,1,0:T(8,128)(2,1)S(1)} %collective-permute-done.9.refs_5_), channel_id=1, source_target_pairs={{0,6},{1,7},{2,0},{3,1},{4,2},{5,3},{6,4},{7,5},{8,14},{9,15},{10,... | collective-permute-start | bytes 638984 | tf_op jit(solution)/shard_map/ppermute | solution.py:326
  203.7 3.1 %collective-permute-done.13.refs_9_ = bf16[52,16,128]{2,1,0:T(8,128)(2,1)} collective-permute-done((bf16[52,16,128]{2,1,0:T(8,128)(2,1)S(1)}, bf16[52,16,128]{2,1,0:T(8,128)(2,1)}, u32[]{:S(2)}, u32[]{:S(2)}) %collective-permute-start.13) | collective-permute-done | bytes 213024 | tf_op jit(solution)/shard_map/ppermute | solution.py:326
  206.8 3.2 %collective-permute-done.15.refs_11_ = bf16[52,16,128]{2,1,0:T(8,128)(2,1)} collective-permute-done((bf16[52,16,128]{2,1,0:T(8,128)(2,1)S(1)}, bf16[52,16,128]{2,1,0:T(8,128)(2,1)}, u32[]{:S(2)}, u32[]{:S(2)}) %collective-permute-start.15) | collective-permute-done | bytes 213024 | tf_op jit(solution)/shard_map/ppermute | solution.py:326
  213.4 15.9 %shard_map.118 = (bf16[1024,512]{1,0:T(8,128)(2,1)}, f32[64,8,128]{2,1,0:T(8,128)}) custom-call(s32[48]{0:T(128)S(1)} %convert_add_fusion.arrival_ref, s32[2]{0:T(128)S(1)} %add_convert_fusion.edge_ref, s32[8]{0:T(128)S(1)} %stack.61.from_ref, bf16[1024,512]{1,0:T(8,128)(2,1)} %q_ref.1, bf16[1024,512]{1,0:T(8,128)(2,1)} %g_ref.1, ...), custom_call_target="tpu_custom_call" | custom-call | tf_op jit(solution)/shard_map/pallas_call | solution.py:334
  229.3 25.5 %all_to_all.20.recv_ref = f32[64,8,128]{2,1,0:T(8,128)S(1)} all-to-all(f32[64,8,128]{2,1,0:T(8,128)} %get-tuple-element.36), channel_id=1, replica_groups=mesh['ctx'=64,'head'=8] {'ctx'}, dimensions={0} | all-to-all | bytes 524288 | tf_op jit(solution)/shard_map/all_to_all | solution.py:358
  (84 shorter events, 17.4 us)
Async XLA Ops:
  4.5 1.2 copy-start.4
  5.7 19.1 %copy-start.15 = (s32[2]{0:T(128)S(1)}, s32[2]{0:T(128)}, u32[]{:S(2)}) copy-start(s32[2]{0:T(128)} %param.15) | copy-start | bytes 28
  5.7 26.4 %copy-start.1 = (bf16[1024,128]{1,0:T(8,128)(2,1)S(1)}, bf16[1024,128]{1,0:T(8,128)(2,1)}, u32[]{:S(2)}) copy-start(bf16[1024,128]{1,0:T(8,128)(2,1)} %k_ref.5) | copy-start | bytes 786436
  5.7 26.4 %copy-start.3 = (bf16[1024,128]{1,0:T(8,128)(2,1)S(1)}, bf16[1024,128]{1,0:T(8,128)(2,1)}, u32[]{:S(2)}) copy-start(bf16[1024,128]{1,0:T(8,128)(2,1)} %v_ref.5) | copy-start | bytes 786436
  7.0 25.1 %all-to-all-start = ((bf16[8,16,16,128]{3,2,1,0:T(8,128)(2,1)}), bf16[8,16,16,128]{3,2,1,0:T(8,128)(2,1)S(1)}, u32[]{:S(2)}, u32[]{:S(2)}) async-start(bf16[8,16,16,128]{3,2,1,0:T(8,128)(2,1)} %shard_map.112), calls=%async_computation | async-start | bytes 1048576 | tf_op jit(solution)/shard_map/all_to_all | solution.py:245
  18.6 1.0 copy-start
  19.6 0.9 copy-start.2
  33.8 48.4 %all-to-all-start.1 = ((bf16[64,4,16,128]{3,2,1,0:T(8,128)(2,1)}), bf16[64,4,16,128]{3,2,1,0:T(8,128)(2,1)S(1)}, u32[]{:S(2)}, u32[]{:S(2)}) async-start(bf16[64,4,16,128]{3,2,1,0:T(8,128)(2,1)} %get-tuple-element.23), calls=%async_computation.1 | async-start | bytes 2097152 | tf_op jit(solution)/shard_map/all_to_all | solution.py:277
  50.5 33.1 %collective-permute-start = (bf16[64,256]{1,0:T(8,128)(2,1)S(1)}, bf16[64,256]{1,0:T(8,128)(2,1)S(1)}, u32[]{:S(2)}, u32[]{:S(2)}) collective-permute-start(bf16[64,256]{1,0:T(8,128)(2,1)S(1)} %pad_maximum_fusion.1), channel_id=1, source_target_pairs={{0,8},{8,16},{16,24},{24,32},{32,40},{40,48},{48,56},{56,64},{64,7... | collective-permute-start | bytes 98312 | tf_op jit(solution)/shard_map/ppermute | solution.py:273
  54.1 29.6 %collective-permute-start.1 = (bf16[64,256]{1,0:T(8,128)(2,1)S(1)}, bf16[64,256]{1,0:T(8,128)(2,1)S(1)}, u32[]{:S(2)}, u32[]{:S(2)}) collective-permute-start(bf16[64,256]{1,0:T(8,128)(2,1)S(1)} %pad_maximum_fusion.2), channel_id=1, source_target_pairs={{8,0},{16,8},{24,16},{32,24},{40,32},{48,40},{56,48},{64,56},{72,6... | collective-permute-start | bytes 98312 | tf_op jit(solution)/shard_map/ppermute | solution.py:274
  56.7 14.7 %collective-permute-start.4 = (bf16[16,16,128]{2,1,0:T(8,128)(2,1)S(1)}, bf16[16,16,128]{2,1,0:T(8,128)(2,1)S(1)}, u32[]{:S(2)}, u32[]{:S(2)}) collective-permute-start(bf16[16,16,128]{2,1,0:T(8,128)(2,1)S(1)} %get-tuple-element.24), channel_id=1, source_target_pairs={{0,1},{1,0},{2,3},{3,2},{4,5},{5,4},{6,7},{7,6},{8,9},{9,8},{10,11... | collective-permute-start | bytes 196616 | tf_op jit(solution)/shard_map/ppermute | solution.py:276
  58.6 25.0 %collective-permute-start.2 = (bf16[16,128]{1,0:T(8,128)(2,1)S(1)}, bf16[16,128]{1,0:T(8,128)(2,1)S(1)}, u32[]{:S(2)}, u32[]{:S(2)}) collective-permute-start(bf16[16,128]{1,0:T(8,128)(2,1)S(1)} %get-tuple-element.46), channel_id=1, source_target_pairs={{0,8},{8,16},{16,24},{24,32},{32,40},{40,48},{48,56},{56,64},{64,7... | collective-permute-start | bytes 12296 | tf_op jit(solution)/shard_map/ppermute | solution.py:278
  62.5 21.2 %collective-permute-start.3 = (bf16[16,128]{1,0:T(8,128)(2,1)S(1)}, bf16[16,128]{1,0:T(8,128)(2,1)S(1)}, u32[]{:S(2)}, u32[]{:S(2)}) collective-permute-start(bf16[16,128]{1,0:T(8,128)(2,1)S(1)} %get-tuple-element.45), channel_id=1, source_target_pairs={{8,0},{16,8},{24,16},{32,24},{40,32},{48,40},{56,48},{64,56},{72,6... | collective-permute-start | bytes 12296 | tf_op jit(solution)/shard_map/ppermute | solution.py:279
  83.6 7.1 %copy-start.13 = (s32[1024,3]{0,1:T(4,128)S(1)}, s32[1024,3]{0,1:T(4,128)}, u32[]{:S(2)}) copy-start(s32[1024,3]{0,1:T(4,128)} %param.14) | copy-start | bytes 36868
  84.3 125.8 %all-to-all-start.2 = ((bf16[64,272,128]{2,1,0:T(8,128)(2,1)}), bf16[64,272,128]{2,1,0:T(8,128)(2,1)}, u32[]{:S(2)}, u32[]{:S(2)}) async-start(bf16[64,272,128]{2,1,0:T(8,128)(2,1)} %shard_map.115), calls=%async_computation.2 | async-start | bytes 8912896 | tf_op jit(solution)/shard_map/all_to_all | solution.py:298
  90.7 46.4 %copy-start.14 = (f32[1,4,256]{2,1,0:T(4,128)S(1)}, f32[1,4,256]{2,1,0:T(4,128)}, u32[]{:S(2)}) copy-start(f32[1,4,256]{2,1,0:T(4,128)} %param.17) | copy-start | bytes 12292
  93.6 3.4 %collective-permute-start.8 = (bf16[16,128]{1,0:T(8,128)(2,1)S(1)}, bf16[16,128]{1,0:T(8,128)(2,1)S(1)}, u32[]{:S(2)}, u32[]{:S(2)}) collective-permute-start(bf16[16,128]{1,0:T(8,128)(2,1)S(1)} %dynamic-slice_bitcast_fusion.here_ref), channel_id=1, source_target_pairs={{0,8},{8,0},{16,24},{24,16},{32,40},{40,32},{48,56},{56,48},{64,72... | collective-permute-start | bytes 12296 | tf_op jit(solution)/shard_map/ppermute | solution.py:283
  97.8 89.6 %collective-permute-start.9 = (bf16[52,16,128]{2,1,0:T(8,128)(2,1)S(1)}, bf16[52,16,128]{2,1,0:T(8,128)(2,1)S(1)}, u32[]{:S(2)}, u32[]{:S(2)}) collective-permute-start(bf16[52,16,128]{2,1,0:T(8,128)(2,1)S(1)} %shard_map.116.refs_4_), channel_id=1, source_target_pairs={{0,1},{1,0},{2,3},{3,2},{4,5},{5,4},{6,7},{7,6},{8,9},{9,8},{10,11... | collective-permute-start | bytes 638984 | tf_op jit(solution)/shard_map/ppermute | solution.py:307
  99.7 101.1 %collective-permute-start.10 = (bf16[52,16,128]{2,1,0:T(8,128)(2,1)S(1)}, bf16[52,16,128]{2,1,0:T(8,128)(2,1)S(1)}, u32[]{:S(2)}, u32[]{:S(2)}) collective-permute-start(bf16[52,16,128]{2,1,0:T(8,128)(2,1)S(1)} %shard_map.116.refs_4_), channel_id=1, source_target_pairs={{0,2},{1,3},{2,4},{3,5},{4,6},{5,7},{6,0},{7,1},{8,10},{9,11},{10,... | collective-permute-start | bytes 638984 | tf_op jit(solution)/shard_map/ppermute | solution.py:326
  127.4 62.0 %collective-permute-start.5 = (bf16[2,16,16,128]{3,2,1,0:T(8,128)(2,1)S(1)}, bf16[2,16,16,128]{3,2,1,0:T(8,128)(2,1)S(1)}, u32[]{:S(2)}, u32[]{:S(2)}) collective-permute-start(bf16[2,16,16,128]{3,2,1,0:T(8,128)(2,1)S(1)} %pad_maximum_fusion.refs_0_), channel_id=1, source_target_pairs={{0,2},{1,3},{2,4},{3,5},{4,6},{5,7},{6,0},{7,1},{8,10},{9,11},{10,... | collective-permute-start | bytes 393224 | tf_op jit(solution)/shard_map/ppermute | solution.py:325
  129.7 62.8 %collective-permute-start.6 = (bf16[2,16,16,128]{3,2,1,0:T(8,128)(2,1)S(1)}, bf16[2,16,16,128]{3,2,1,0:T(8,128)(2,1)S(1)}, u32[]{:S(2)}, u32[]{:S(2)}) collective-permute-start(bf16[2,16,16,128]{3,2,1,0:T(8,128)(2,1)S(1)} %pad_maximum_fusion.refs_0_), channel_id=1, source_target_pairs={{0,4},{1,5},{2,6},{3,7},{4,0},{5,1},{6,2},{7,3},{8,12},{9,13},{10,... | collective-permute-start | bytes 393224 | tf_op jit(solution)/shard_map/ppermute | solution.py:325
  134.9 60.5 %collective-permute-start.7 = (bf16[2,16,16,128]{3,2,1,0:T(8,128)(2,1)S(1)}, bf16[2,16,16,128]{3,2,1,0:T(8,128)(2,1)S(1)}, u32[]{:S(2)}, u32[]{:S(2)}) collective-permute-start(bf16[2,16,16,128]{3,2,1,0:T(8,128)(2,1)S(1)} %pad_maximum_fusion.refs_0_), channel_id=1, source_target_pairs={{0,6},{1,7},{2,0},{3,1},{4,2},{5,3},{6,4},{7,5},{8,14},{9,15},{10,... | collective-permute-start | bytes 393224 | tf_op jit(solution)/shard_map/ppermute | solution.py:325
  187.4 16.4 %collective-permute-start.12 = (bf16[52,16,128]{2,1,0:T(8,128)(2,1)S(1)}, bf16[52,16,128]{2,1,0:T(8,128)(2,1)}, u32[]{:S(2)}, u32[]{:S(2)}) collective-permute-start(bf16[52,16,128]{2,1,0:T(8,128)(2,1)S(1)} %shard_map.116.refs_4_), channel_id=1, source_target_pairs={{0,4},{1,5},{2,6},{3,7},{4,0},{5,1},{6,2},{7,3},{8,12},{9,13},{10,... | collective-permute-start | bytes 638984 | tf_op jit(solution)/shard_map/ppermute | solution.py:326
  189.5 14.3 %collective-permute-start.14 = (bf16[52,16,128]{2,1,0:T(8,128)(2,1)S(1)}, bf16[52,16,128]{2,1,0:T(8,128)(2,1)}, u32[]{:S(2)}, u32[]{:S(2)}) collective-permute-start(bf16[52,16,128]{2,1,0:T(8,128)(2,1)S(1)} %shard_map.116.refs_4_), channel_id=1, source_target_pairs={{0,6},{1,7},{2,0},{3,1},{4,2},{5,3},{6,4},{7,5},{8,14},{9,15},{10,... | collective-permute-start | bytes 638984 | tf_op jit(solution)/shard_map/ppermute | solution.py:326
  192.5 0.7 copy-start.5
  193.2 10.5 %collective-permute-start.11 = (bf16[52,16,128]{2,1,0:T(8,128)(2,1)S(1)}, bf16[52,16,128]{2,1,0:T(8,128)(2,1)}, u32[]{:S(2)}, u32[]{:S(2)}) collective-permute-start(bf16[52,16,128]{2,1,0:T(8,128)(2,1)S(1)} %collective-permute-done.9.refs_5_), channel_id=1, source_target_pairs={{0,2},{1,3},{2,4},{3,5},{4,6},{5,7},{6,0},{7,1},{8,10},{9,11},{10,... | collective-permute-start | bytes 638984 | tf_op jit(solution)/shard_map/ppermute | solution.py:326
  196.1 10.7 %collective-permute-start.13 = (bf16[52,16,128]{2,1,0:T(8,128)(2,1)S(1)}, bf16[52,16,128]{2,1,0:T(8,128)(2,1)}, u32[]{:S(2)}, u32[]{:S(2)}) collective-permute-start(bf16[52,16,128]{2,1,0:T(8,128)(2,1)S(1)} %collective-permute-done.9.refs_5_), channel_id=1, source_target_pairs={{0,4},{1,5},{2,6},{3,7},{4,0},{5,1},{6,2},{7,3},{8,12},{9,13},{10,... | collective-permute-start | bytes 638984 | tf_op jit(solution)/shard_map/ppermute | solution.py:326
  200.8 9.3 %collective-permute-start.15 = (bf16[52,16,128]{2,1,0:T(8,128)(2,1)S(1)}, bf16[52,16,128]{2,1,0:T(8,128)(2,1)}, u32[]{:S(2)}, u32[]{:S(2)}) collective-permute-start(bf16[52,16,128]{2,1,0:T(8,128)(2,1)S(1)} %collective-permute-done.9.refs_5_), channel_id=1, source_target_pairs={{0,6},{1,7},{2,0},{3,1},{4,2},{5,3},{6,4},{7,5},{8,14},{9,15},{10,... | collective-permute-start | bytes 638984 | tf_op jit(solution)/shard_map/ppermute | solution.py:326
  210.1 0.9 copy-start.6
  211.0 0.9 copy-start.8
  211.9 0.8 copy-start.10
  212.6 0.8 copy-start.12
  (3 other events, 1.9 us)

commit v7 on v5

--- a/solution.py
+++ b/solution.py
@@ -256,7 +256,9 @@
         out_shape=pltpu.HBM((ctx, span, h), BF16),
         compiler_params=PARAMS,
     )(sources, keys, values)
-    terms, kv_out = lax.optimization_barrier((terms, kv_out))
+    kv_before = lax.ppermute(jnp.concatenate([keys[-BLK:], values[-BLK:]], axis=1), "ctx", up)
+    kv_after = lax.ppermute(jnp.concatenate([keys[:BLK], values[:BLK]], axis=1), "ctx", down)
+    terms, kv_out, kv_before, kv_after = lax.optimization_barrier((terms, kv_out, kv_before, kv_after))
     own, p_out = pl.pallas_call(
         sum_pack,
         in_specs=[SMEM, SMEM] + [VMEM] * 3,
@@ -269,8 +271,6 @@
         compiler_params=PARAMS,
     )(sources, global_inner, terms, keys, values)
 
-    kv_before = lax.ppermute(jnp.concatenate([keys[-BLK:], values[-BLK:]], axis=1), "ctx", up)
-    kv_after = lax.ppermute(jnp.concatenate([keys[:BLK], values[:BLK]], axis=1), "ctx", down)
     p_in = lax.all_to_all(p_out, "ctx", 0, 0, tiled=True)
     p_before = lax.ppermute(own[-1], "ctx", up)
     p_after = lax.ppermute(own[0], "ctx", down)
@@ -289,9 +289,7 @@
         scratch_shapes=[pltpu.VMEM((ctx, ROWS, h), BF16), pltpu.SemaphoreType.DMA],
         compiler_params=PARAMS,
     )(tile_owner.reshape(1), kv_out, p_in)
-    kv_out, kv_before, kv_after, p_before, p_after = lax.optimization_barrier(
-        (kv_out, kv_before, kv_after, p_before, p_after)
-    )
+    kv_out, p_before, p_after = lax.optimization_barrier((kv_out, p_before, p_after))
     kv_in = lax.all_to_all(kv_out, "ctx", 0, 0, tiled=True)
 
     tiles = pl.pallas_call(

time: 253 us -> 253 us (level)
  waiting for transfers between devices: 88.8 us -> 80.3 us
  starting transfers between devices: 65.9 us -> 74 us
    all_to_all x1, waiting for transfers between devices: 7.33 us -> 0.86 us  [local(): terms = lax.all_to_all(terms, 'head', 0, 0, tiled=True)]
    all_to_all x1, waiting for transfers between devices: 17.1 us -> 22.4 us  [local(): p_in = lax.all_to_all(p_out, 'ctx', 0, 0, tiled=True)]
    ppermute x1, waiting for transfers between devices: 53.9 us -> 49.4 us  [local(): lax.ppermute(tiles, 'head', [(i, i ^ 1) for i in range(heads)])]
    ppermute x6, starting transfers between devices: 17.3 us -> 21.5 us  [local(): all_tiles += [lax.ppermute(t, 'head', there) for t in pair]]
    ppermute x1, starting transfers between devices: 1.92 us -> 6.01 us  [local(): lax.ppermute(tiles, 'head', [(i, i ^ 1) for i in range(heads)])]
    ppermute x6, waiting for transfers between devices: 10.3 us -> 7.48 us  [local(): all_tiles += [lax.ppermute(t, 'head', there) for t in pair]]
  transfers between devices with their start and end apart: 15 -> 15, of which waited for: 7 -> 6; matrix products, arithmetic and copies ran while one was open for 11% -> 12% of each run, Pallas kernels for 3% -> 3%
where the time goes in v7:
time: 253 us; the launch traced here: 252 us
  waiting for transfers between devices  80.3 us (32%)
  starting transfers between devices  74 us (29%)
  other arithmetic  29.5 us (12%)
  blocking collectives  28.8 us (11%)
  Pallas kernels  27.7 us (11%)
  local copies, waits for them, and re-layouts  6.92 us (3%)
  between operations  4.4 us (2%)
    ppermute x1, waiting for transfers between devices, local(): lax.ppermute(tiles, 'head', [(i, i ^ 1) for i in range(heads)])  49.4 us
    all_to_all x1, blocking collectives, local(): grad = lax.all_to_all(grad, 'ctx', 0, 0, tiled=True)  28.8 us
    convert_element_type x2, other arithmetic, proj_table(): return (unit_value * math.sqrt(12.0 / D)).astype(jnp.bfloat16)  27.4 us
    all_to_all x1, waiting for transfers between devices, local(): p_in = lax.all_to_all(p_out, 'ctx', 0, 0, tiled=True)  22.4 us
    ppermute x6, starting transfers between devices, local(): all_tiles += [lax.ppermute(t, 'head', there) for t in pair]  21.5 us
    all_to_all x1, starting transfers between devices, local(): p_in = lax.all_to_all(p_out, 'ctx', 0, 0, tiled=True)  16.9 us
    pallas_call x1, Pallas kernels, local(): pl.pallas_call(attend, grid=(blocks // unroll,), in_specs=[SMEM] * 3 + [w...  16.1 us
    all_to_all x1, starting transfers between devices, local(): terms = lax.all_to_all(terms, 'head', 0, 0, tiled=True)  10.1 us
  transfers between devices with their start and end apart: 15, of which 6 were waited for; matrix products, arithmetic and copies ran while one was open for 12% of the time, Pallas kernels for 3%

profile of v7, /device:TPU:1, one launch (start us, length us, event | category | flops | bytes accessed | tf_op | source)
XLA Modules:
  0.0 251.7 jit_solution(5330878982054286909)
XLA Ops:
  0.7 1.3 fusion.78
  2.6 1.8 fusion.59.t_ref
  4.5 1.2 copy-done.4
  5.7 1.3 shard_map.112
  7.0 10.1 %all-to-all-start = ((bf16[8,16,16,128]{3,2,1,0:T(8,128)(2,1)}), bf16[8,16,16,128]{3,2,1,0:T(8,128)(2,1)S(1)}, u32[]{:S(2)}, u32[]{:S(2)}) async-start(bf16[8,16,16,128]{3,2,1,0:T(8,128)(2,1)} %shard_map.112), calls=%async_computation | async-start | bytes 1048576 | tf_op jit(solution)/shard_map/all_to_all | solution.py:244
  17.9 3.1 %collective-permute-start = (bf16[64,256]{1,0:T(8,128)(2,1)S(1)}, bf16[64,256]{1,0:T(8,128)(2,1)S(1)}, u32[]{:S(2)}, u32[]{:S(2)}) collective-permute-start(bf16[64,256]{1,0:T(8,128)(2,1)S(1)} %pad_maximum_fusion), channel_id=1, source_target_pairs={{0,8},{8,16},{16,24},{24,32},{32,40},{40,48},{48,56},{56,64},{64,7... | collective-permute-start | bytes 98312 | tf_op jit(solution)/shard_map/ppermute | solution.py:259
  21.0 1.9 collective-permute-start.1
  26.1 0.9 copy-done.2
  27.1 4.2 %shard_map.113.packed_ref = bf16[64,272,128]{2,1,0:T(8,128)(2,1)} custom-call(s32[128]{0:T(128)S(1)} %reshape.134.src_ref, bf16[1024,128]{1,0:T(8,128)(2,1)S(1)} %copy-done, bf16[1024,128]{1,0:T(8,128)(2,1)S(1)} %copy-done.2), custom_call_target="tpu_custom_call" | custom-call | tf_op jit(solution)/shard_map/pallas_call | solution.py:248
  32.2 1.7 shard_map.114
  33.9 16.9 %all-to-all-start.1 = ((bf16[64,4,16,128]{3,2,1,0:T(8,128)(2,1)}), bf16[64,4,16,128]{3,2,1,0:T(8,128)(2,1)S(1)}, u32[]{:S(2)}, u32[]{:S(2)}) async-start(bf16[64,4,16,128]{3,2,1,0:T(8,128)(2,1)} %get-tuple-element.22), calls=%async_computation.1 | async-start | bytes 2097152 | tf_op jit(solution)/shard_map/all_to_all | solution.py:274
  50.8 3.5 %collective-permute-start.2 = (bf16[16,128]{1,0:T(8,128)(2,1)S(1)}, bf16[16,128]{1,0:T(8,128)(2,1)S(1)}, u32[]{:S(2)}, u32[]{:S(2)}) collective-permute-start(bf16[16,128]{1,0:T(8,128)(2,1)S(1)} %get-tuple-element.40), channel_id=1, source_target_pairs={{0,8},{8,16},{16,24},{24,32},{32,40},{40,48},{48,56},{56,64},{64,7... | collective-permute-start | bytes 12296 | tf_op jit(solution)/shard_map/ppermute | solution.py:275
  54.4 1.9 collective-permute-start.3
  56.9 22.4 %all-to-all-done.1.tile_ref.recv_ref = bf16[64,4,16,128]{3,2,1,0:T(8,128)(2,1)S(1)} async-done(((bf16[64,4,16,128]{3,2,1,0:T(8,128)(2,1)}), bf16[64,4,16,128]{3,2,1,0:T(8,128)(2,1)S(1)}, u32[]{:S(2)}, u32[]{:S(2)}) %all-to-all-start.1) | async-done | bytes 1048608 | tf_op jit(solution)/shard_map/all_to_all | solution.py:274
  79.4 1.4 shard_map.115
  80.8 6.4 %all-to-all-start.2 = ((bf16[64,272,128]{2,1,0:T(8,128)(2,1)}), bf16[64,272,128]{2,1,0:T(8,128)(2,1)}, u32[]{:S(2)}, u32[]{:S(2)}) async-start(bf16[64,272,128]{2,1,0:T(8,128)(2,1)} %shard_map.115), calls=%async_computation.2 | async-start | bytes 8912896 | tf_op jit(solution)/shard_map/all_to_all | solution.py:293
  89.9 2.5 %collective-permute-start.4 = (bf16[16,128]{1,0:T(8,128)(2,1)S(1)}, bf16[16,128]{1,0:T(8,128)(2,1)S(1)}, u32[]{:S(2)}, u32[]{:S(2)}) collective-permute-start(bf16[16,128]{1,0:T(8,128)(2,1)S(1)} %dynamic-slice_bitcast_fusion.here_ref), channel_id=1, source_target_pairs={{0,8},{8,0},{16,24},{24,16},{32,40},{40,32},{48,56},{56,48},{64,72... | collective-permute-start | bytes 12296 | tf_op jit(solution)/shard_map/ppermute | solution.py:280
  94.2 6.0 %collective-permute-start.5 = (bf16[68,16,128]{2,1,0:T(8,128)(2,1)S(1)}, bf16[68,16,128]{2,1,0:T(8,128)(2,1)S(1)}, u32[]{:S(2)}, u32[]{:S(2)}) collective-permute-start(bf16[68,16,128]{2,1,0:T(8,128)(2,1)S(1)} %shard_map.116.refs_0_), channel_id=1, source_target_pairs={{0,1},{1,0},{2,3},{3,2},{4,5},{5,4},{6,7},{7,6},{8,9},{9,8},{10,11... | collective-permute-start | bytes 835592 | tf_op jit(solution)/shard_map/ppermute | solution.py:302
  100.2 3.1 %collective-permute-start.6 = (bf16[68,16,128]{2,1,0:T(8,128)(2,1)S(1)}, bf16[68,16,128]{2,1,0:T(8,128)(2,1)S(1)}, u32[]{:S(2)}, u32[]{:S(2)}) collective-permute-start(bf16[68,16,128]{2,1,0:T(8,128)(2,1)S(1)} %shard_map.116.refs_0_), channel_id=1, source_target_pairs={{0,2},{1,3},{2,4},{3,5},{4,6},{5,7},{6,0},{7,1},{8,10},{9,11},{10,... | collective-permute-start | bytes 835592 | tf_op jit(solution)/shard_map/ppermute | solution.py:319
  103.3 25.6 %fusion.41 = (bf16[256,4096]{1,0:T(8,128)(2,1)S(1)}, bf16[256,4096]{1,0:T(8,128)(2,1)S(1)}) fusion(s32[]{:T(128)} %bitcast.11, s32[256]{0:T(256)S(1)} %get-tuple-element.53, s32[4096]{0:T(1024)S(1)} %iota_multiply_fusion, s32[256]{0:T(256)S(1)} %get-tuple-element.54, s32[]{:T(128)} %bitcast.20), kind=kLoop, calls=%fused_computation.53 | loop fusion | flops 93323264 | bytes 4212744 | tf_op jit(solution)/shard_map/convert_element_type | solution.py:37
  128.9 1.1 shard_map.117.refs_9_.carried_ref
  130.0 4.3 %collective-permute-start.8 = (bf16[68,16,128]{2,1,0:T(8,128)(2,1)S(1)}, bf16[68,16,128]{2,1,0:T(8,128)(2,1)}, u32[]{:S(2)}, u32[]{:S(2)}) collective-permute-start(bf16[68,16,128]{2,1,0:T(8,128)(2,1)S(1)} %shard_map.116.refs_0_), channel_id=1, source_target_pairs={{0,4},{1,5},{2,6},{3,7},{4,0},{5,1},{6,2},{7,3},{8,12},{9,13},{10,... | collective-permute-start | bytes 835592 | tf_op jit(solution)/shard_map/ppermute | solution.py:319
  134.3 3.1 %collective-permute-start.10 = (bf16[68,16,128]{2,1,0:T(8,128)(2,1)S(1)}, bf16[68,16,128]{2,1,0:T(8,128)(2,1)}, u32[]{:S(2)}, u32[]{:S(2)}) collective-permute-start(bf16[68,16,128]{2,1,0:T(8,128)(2,1)S(1)} %shard_map.116.refs_0_), channel_id=1, source_target_pairs={{0,6},{1,7},{2,0},{3,1},{4,2},{5,3},{6,4},{7,5},{8,14},{9,15},{10,... | collective-permute-start | bytes 835592 | tf_op jit(solution)/shard_map/ppermute | solution.py:319
  137.4 49.4 %collective-permute-done.5.refs_1_ = bf16[68,16,128]{2,1,0:T(8,128)(2,1)S(1)} collective-permute-done((bf16[68,16,128]{2,1,0:T(8,128)(2,1)S(1)}, bf16[68,16,128]{2,1,0:T(8,128)(2,1)S(1)}, u32[]{:S(2)}, u32[]{:S(2)}) %collective-permute-start.5) | collective-permute-done | bytes 278560 | tf_op jit(solution)/shard_map/ppermute | solution.py:302
  186.9 3.4 %collective-permute-start.7 = (bf16[68,16,128]{2,1,0:T(8,128)(2,1)S(1)}, bf16[68,16,128]{2,1,0:T(8,128)(2,1)}, u32[]{:S(2)}, u32[]{:S(2)}) collective-permute-start(bf16[68,16,128]{2,1,0:T(8,128)(2,1)S(1)} %collective-permute-done.5.refs_1_), channel_id=1, source_target_pairs={{0,2},{1,3},{2,4},{3,5},{4,6},{5,7},{6,0},{7,1},{8,10},{9,11},{10,... | collective-permute-start | bytes 835592 | tf_op jit(solution)/shard_map/ppermute | solution.py:319
  190.3 4.3 %collective-permute-start.9 = (bf16[68,16,128]{2,1,0:T(8,128)(2,1)S(1)}, bf16[68,16,128]{2,1,0:T(8,128)(2,1)}, u32[]{:S(2)}, u32[]{:S(2)}) collective-permute-start(bf16[68,16,128]{2,1,0:T(8,128)(2,1)S(1)} %collective-permute-done.5.refs_1_), channel_id=1, source_target_pairs={{0,4},{1,5},{2,6},{3,7},{4,0},{5,1},{6,2},{7,3},{8,12},{9,13},{10,... | collective-permute-start | bytes 835592 | tf_op jit(solution)/shard_map/ppermute | solution.py:319
  194.7 3.3 %collective-permute-start.11 = (bf16[68,16,128]{2,1,0:T(8,128)(2,1)S(1)}, bf16[68,16,128]{2,1,0:T(8,128)(2,1)}, u32[]{:S(2)}, u32[]{:S(2)}) collective-permute-start(bf16[68,16,128]{2,1,0:T(8,128)(2,1)S(1)} %collective-permute-done.5.refs_1_), channel_id=1, source_target_pairs={{0,6},{1,7},{2,0},{3,1},{4,2},{5,3},{6,4},{7,5},{8,14},{9,15},{10,... | collective-permute-start | bytes 835592 | tf_op jit(solution)/shard_map/ppermute | solution.py:319
  198.2 6.3 %collective-permute-done.9.refs_5_ = bf16[68,16,128]{2,1,0:T(8,128)(2,1)} collective-permute-done((bf16[68,16,128]{2,1,0:T(8,128)(2,1)S(1)}, bf16[68,16,128]{2,1,0:T(8,128)(2,1)}, u32[]{:S(2)}, u32[]{:S(2)}) %collective-permute-start.9) | collective-permute-done | bytes 278560 | tf_op jit(solution)/shard_map/ppermute | solution.py:319
  204.5 1.1 collective-permute-done.11.refs_7_
  205.6 16.1 %shard_map.118 = (bf16[1024,512]{1,0:T(8,128)(2,1)}, f32[64,8,128]{2,1,0:T(8,128)}) custom-call(s32[48]{0:T(128)S(1)} %convert_add_fusion.arrival_ref, s32[2]{0:T(128)S(1)} %add_convert_fusion.edge_ref, s32[8]{0:T(128)S(1)} %stack.52.from_ref, bf16[1024,512]{1,0:T(8,128)(2,1)} %q_ref.1, bf16[1024,512]{1,0:T(8,128)(2,1)} %g_ref.1, ...), custom_call_target="tpu_custom_call" | custom-call | tf_op jit(solution)/shard_map/pallas_call | solution.py:327
  221.7 28.8 %all_to_all.20.recv_ref = f32[64,8,128]{2,1,0:T(8,128)S(1)} all-to-all(f32[64,8,128]{2,1,0:T(8,128)} %get-tuple-element.30), channel_id=1, replica_groups=mesh['ctx'=64,'head'=8] {'ctx'}, dimensions={0} | all-to-all | bytes 524288 | tf_op jit(solution)/shard_map/all_to_all | solution.py:351
  250.5 1.2 shard_map.119
  (57 shorter events, 7.3 us)
Async XLA Ops:
  4.5 1.2 copy-start.4
  5.7 26.5 %copy-start.1 = (bf16[1024,128]{1,0:T(8,128)(2,1)S(1)}, bf16[1024,128]{1,0:T(8,128)(2,1)}, u32[]{:S(2)}) copy-start(bf16[1024,128]{1,0:T(8,128)(2,1)} %k_ref.5) | copy-start | bytes 786436
  5.7 26.5 %copy-start.3 = (bf16[1024,128]{1,0:T(8,128)(2,1)S(1)}, bf16[1024,128]{1,0:T(8,128)(2,1)}, u32[]{:S(2)}) copy-start(bf16[1024,128]{1,0:T(8,128)(2,1)} %v_ref.5) | copy-start | bytes 786436
  7.0 25.2 %all-to-all-start = ((bf16[8,16,16,128]{3,2,1,0:T(8,128)(2,1)}), bf16[8,16,16,128]{3,2,1,0:T(8,128)(2,1)S(1)}, u32[]{:S(2)}, u32[]{:S(2)}) async-start(bf16[8,16,16,128]{3,2,1,0:T(8,128)(2,1)} %shard_map.112), calls=%async_computation | async-start | bytes 1048576 | tf_op jit(solution)/shard_map/all_to_all | solution.py:244
  17.9 13.4 %collective-permute-start = (bf16[64,256]{1,0:T(8,128)(2,1)S(1)}, bf16[64,256]{1,0:T(8,128)(2,1)S(1)}, u32[]{:S(2)}, u32[]{:S(2)}) collective-permute-start(bf16[64,256]{1,0:T(8,128)(2,1)S(1)} %pad_maximum_fusion), channel_id=1, source_target_pairs={{0,8},{8,16},{16,24},{24,32},{32,40},{40,48},{48,56},{56,64},{64,7... | collective-permute-start | bytes 98312 | tf_op jit(solution)/shard_map/ppermute | solution.py:259
  21.0 10.3 %collective-permute-start.1 = (bf16[64,256]{1,0:T(8,128)(2,1)S(1)}, bf16[64,256]{1,0:T(8,128)(2,1)S(1)}, u32[]{:S(2)}, u32[]{:S(2)}) collective-permute-start(bf16[64,256]{1,0:T(8,128)(2,1)S(1)} %pad_maximum_fusion.1), channel_id=1, source_target_pairs={{8,0},{16,8},{24,16},{32,24},{40,32},{48,40},{56,48},{64,56},{72,6... | collective-permute-start | bytes 98312 | tf_op jit(solution)/shard_map/ppermute | solution.py:260
  25.2 1.0 copy-start
  26.1 0.9 copy-start.2
  33.9 45.5 %all-to-all-start.1 = ((bf16[64,4,16,128]{3,2,1,0:T(8,128)(2,1)}), bf16[64,4,16,128]{3,2,1,0:T(8,128)(2,1)S(1)}, u32[]{:S(2)}, u32[]{:S(2)}) async-start(bf16[64,4,16,128]{3,2,1,0:T(8,128)(2,1)} %get-tuple-element.22), calls=%async_computation.1 | async-start | bytes 2097152 | tf_op jit(solution)/shard_map/all_to_all | solution.py:274
  50.8 29.9 %collective-permute-start.2 = (bf16[16,128]{1,0:T(8,128)(2,1)S(1)}, bf16[16,128]{1,0:T(8,128)(2,1)S(1)}, u32[]{:S(2)}, u32[]{:S(2)}) collective-permute-start(bf16[16,128]{1,0:T(8,128)(2,1)S(1)} %get-tuple-element.40), channel_id=1, source_target_pairs={{0,8},{8,16},{16,24},{24,32},{32,40},{40,48},{48,56},{56,64},{64,7... | collective-permute-start | bytes 12296 | tf_op jit(solution)/shard_map/ppermute | solution.py:275
  54.4 26.4 %collective-permute-start.3 = (bf16[16,128]{1,0:T(8,128)(2,1)S(1)}, bf16[16,128]{1,0:T(8,128)(2,1)S(1)}, u32[]{:S(2)}, u32[]{:S(2)}) collective-permute-start(bf16[16,128]{1,0:T(8,128)(2,1)S(1)} %get-tuple-element.39), channel_id=1, source_target_pairs={{8,0},{16,8},{24,16},{32,24},{40,32},{48,40},{56,48},{64,56},{72,6... | collective-permute-start | bytes 12296 | tf_op jit(solution)/shard_map/ppermute | solution.py:276
  80.7 6.4 %copy-start.5 = (s32[1024,3]{0,1:T(4,128)S(1)}, s32[1024,3]{0,1:T(4,128)}, u32[]{:S(2)}) copy-start(s32[1024,3]{0,1:T(4,128)} %param.14) | copy-start | bytes 36868
  80.8 124.9 %all-to-all-start.2 = ((bf16[64,272,128]{2,1,0:T(8,128)(2,1)}), bf16[64,272,128]{2,1,0:T(8,128)(2,1)}, u32[]{:S(2)}, u32[]{:S(2)}) async-start(bf16[64,272,128]{2,1,0:T(8,128)(2,1)} %shard_map.115), calls=%async_computation.2 | async-start | bytes 8912896 | tf_op jit(solution)/shard_map/all_to_all | solution.py:293
  87.2 41.7 %copy-start.6 = (f32[1,4,256]{2,1,0:T(4,128)S(1)}, f32[1,4,256]{2,1,0:T(4,128)}, u32[]{:S(2)}) copy-start(f32[1,4,256]{2,1,0:T(4,128)} %param.17) | copy-start | bytes 12292
  89.9 3.4 %collective-permute-start.4 = (bf16[16,128]{1,0:T(8,128)(2,1)S(1)}, bf16[16,128]{1,0:T(8,128)(2,1)S(1)}, u32[]{:S(2)}, u32[]{:S(2)}) collective-permute-start(bf16[16,128]{1,0:T(8,128)(2,1)S(1)} %dynamic-slice_bitcast_fusion.here_ref), channel_id=1, source_target_pairs={{0,8},{8,0},{16,24},{24,16},{32,40},{40,32},{48,56},{56,48},{64,72... | collective-permute-start | bytes 12296 | tf_op jit(solution)/shard_map/ppermute | solution.py:280
  94.2 92.7 %collective-permute-start.5 = (bf16[68,16,128]{2,1,0:T(8,128)(2,1)S(1)}, bf16[68,16,128]{2,1,0:T(8,128)(2,1)S(1)}, u32[]{:S(2)}, u32[]{:S(2)}) collective-permute-start(bf16[68,16,128]{2,1,0:T(8,128)(2,1)S(1)} %shard_map.116.refs_0_), channel_id=1, source_target_pairs={{0,1},{1,0},{2,3},{3,2},{4,5},{5,4},{6,7},{7,6},{8,9},{9,8},{10,11... | collective-permute-start | bytes 835592 | tf_op jit(solution)/shard_map/ppermute | solution.py:302
  100.2 94.5 %collective-permute-start.6 = (bf16[68,16,128]{2,1,0:T(8,128)(2,1)S(1)}, bf16[68,16,128]{2,1,0:T(8,128)(2,1)S(1)}, u32[]{:S(2)}, u32[]{:S(2)}) collective-permute-start(bf16[68,16,128]{2,1,0:T(8,128)(2,1)S(1)} %shard_map.116.refs_0_), channel_id=1, source_target_pairs={{0,2},{1,3},{2,4},{3,5},{4,6},{5,7},{6,0},{7,1},{8,10},{9,11},{10,... | collective-permute-start | bytes 835592 | tf_op jit(solution)/shard_map/ppermute | solution.py:319
  130.0 68.1 %collective-permute-start.8 = (bf16[68,16,128]{2,1,0:T(8,128)(2,1)S(1)}, bf16[68,16,128]{2,1,0:T(8,128)(2,1)}, u32[]{:S(2)}, u32[]{:S(2)}) collective-permute-start(bf16[68,16,128]{2,1,0:T(8,128)(2,1)S(1)} %shard_map.116.refs_0_), channel_id=1, source_target_pairs={{0,4},{1,5},{2,6},{3,7},{4,0},{5,1},{6,2},{7,3},{8,12},{9,13},{10,... | collective-permute-start | bytes 835592 | tf_op jit(solution)/shard_map/ppermute | solution.py:319
  134.3 63.8 %collective-permute-start.10 = (bf16[68,16,128]{2,1,0:T(8,128)(2,1)S(1)}, bf16[68,16,128]{2,1,0:T(8,128)(2,1)}, u32[]{:S(2)}, u32[]{:S(2)}) collective-permute-start(bf16[68,16,128]{2,1,0:T(8,128)(2,1)S(1)} %shard_map.116.refs_0_), channel_id=1, source_target_pairs={{0,6},{1,7},{2,0},{3,1},{4,2},{5,3},{6,4},{7,5},{8,14},{9,15},{10,... | collective-permute-start | bytes 835592 | tf_op jit(solution)/shard_map/ppermute | solution.py:319
  186.9 11.3 %collective-permute-start.7 = (bf16[68,16,128]{2,1,0:T(8,128)(2,1)S(1)}, bf16[68,16,128]{2,1,0:T(8,128)(2,1)}, u32[]{:S(2)}, u32[]{:S(2)}) collective-permute-start(bf16[68,16,128]{2,1,0:T(8,128)(2,1)S(1)} %collective-permute-done.5.refs_1_), channel_id=1, source_target_pairs={{0,2},{1,3},{2,4},{3,5},{4,6},{5,7},{6,0},{7,1},{8,10},{9,11},{10,... | collective-permute-start | bytes 835592 | tf_op jit(solution)/shard_map/ppermute | solution.py:319
  190.3 14.2 %collective-permute-start.9 = (bf16[68,16,128]{2,1,0:T(8,128)(2,1)S(1)}, bf16[68,16,128]{2,1,0:T(8,128)(2,1)}, u32[]{:S(2)}, u32[]{:S(2)}) collective-permute-start(bf16[68,16,128]{2,1,0:T(8,128)(2,1)S(1)} %collective-permute-done.5.refs_1_), channel_id=1, source_target_pairs={{0,4},{1,5},{2,6},{3,7},{4,0},{5,1},{6,2},{7,3},{8,12},{9,13},{10,... | collective-permute-start | bytes 835592 | tf_op jit(solution)/shard_map/ppermute | solution.py:319
  194.7 11.0 %collective-permute-start.11 = (bf16[68,16,128]{2,1,0:T(8,128)(2,1)S(1)}, bf16[68,16,128]{2,1,0:T(8,128)(2,1)}, u32[]{:S(2)}, u32[]{:S(2)}) collective-permute-start(bf16[68,16,128]{2,1,0:T(8,128)(2,1)S(1)} %collective-permute-done.5.refs_1_), channel_id=1, source_target_pairs={{0,6},{1,7},{2,0},{3,1},{4,2},{5,3},{6,4},{7,5},{8,14},{9,15},{10,... | collective-permute-start | bytes 835592 | tf_op jit(solution)/shard_map/ppermute | solution.py:319
